TPU v7x, 32 devices: a whole 2x2x4 slice. The times are simulated.
32 devices in a mesh: grp: 2 (over y), seq: 4 (over x, core), tp: 4 (over z).
Axes of the slice: x: 2, y: 2, z: 4, core: 2. Of those that a mesh axis runs over, the one named last changes fastest.
Arguments:
- fc_big: bfloat16 [1024, 6912], P(('grp', 'seq'), 'tp'), may hold values from -6 to 6
- fc_guide: bfloat16 [1024, 4480], P(('grp', 'seq'), 'tp'), may hold values from -6 to 6
- res_big: bfloat16 [1024, 5120], P(('grp', 'tp'), 'seq'), may hold values from -6 to 6
- res_guide: bfloat16 [1024, 1536], P(('grp', 'tp'), 'seq'), may hold values from -6 to 6
- cotangent: float32 [1024, 64], P(('grp', 'tp')), may hold values from -6 to 6
- proj_big: bfloat16 [6912, 5120], P('tp', 'seq'), may hold values from -0.078125 to 0.078125
- proj_guide: bfloat16 [4480, 1536], P('tp', 'seq'), may hold values from -0.09375 to 0.09375
- head_big: bfloat16 [5120, 64], P('seq'), may hold values from -0.078125 to 0.078125
- head_guide: bfloat16 [1536, 64], P('seq'), may hold values from -0.15625 to 0.15625
- modulation_big: float32 [50, 3, 5120], P(None, None, 'seq'), may hold values from -3 to 3
- modulation_guide: float32 [50, 3, 1536], P(None, None, 'seq'), may hold values from -3 to 3
- weight_table: float32 [8], replicated, may hold values from 1.5 to 4
- time_index: int32 [2], P('grp'), may hold values from 0 to 49
- weight_index: int32 [2], P('grp'), may hold values from 0 to 7
Outputs:
- guided: float32 [1024, 64], P(('grp', 'tp'))
- grad_proj: bfloat16 [6912, 5120], P('tp', 'seq')
- grad_head: float32 [5120, 64], P('seq')
- grad_res_big: bfloat16 [1024, 5120], P(('grp', 'tp'), 'seq')
- grad_res_guide: bfloat16 [1024, 1536], P(('grp', 'tp'), 'seq')
All inputs are finite; a program needn't handle non-finite values.
Results may differ from a plain program's by a relative error of at most 0.019.
Values may be sent and summed in bfloat16 or wider, within the bound.
No kernel may reach another device: no remote copies, remote signals or barrier semaphores. Data moves between devices by JAX's collectives and lax.ppermute only.
A program may use at most 64 MiB of HBM per device.

v0:
```python
import jax
import jax.numpy as jnp
from jax import lax
from jax.sharding import PartitionSpec as P

DB = 5120
DG = 1536
STEPS = 50
LEVELS = 8


EPSILON = 1e-06


def lookup(hot_row, table):
    flat = jnp.dot(hot_row, table.reshape(table.shape[0], -1), precision=lax.Precision.HIGHEST)
    return flat.reshape(3, -1)


def shards(
    fc_big,
    fc_guide,
    res_big,
    res_guide,
    cotangent,
    proj_big,
    proj_guide,
    head_big,
    head_guide,
    modulation_big,
    modulation_guide,
    weight_table,
    time_index,
    weight_index,
):
    width_big = res_big.shape[1]
    full_big, full_guide = (
        lax.all_gather(fc_big, "seq", axis=0, tiled=True),
        lax.all_gather(fc_guide, "seq", axis=0, tiled=True),
    )
    term_big = jnp.dot(full_big, proj_big, preferred_element_type=jnp.float32)
    term_guide = jnp.dot(full_guide, proj_guide, preferred_element_type=jnp.float32)
    summed = lax.psum_scatter(
        jnp.concatenate([term_big, term_guide], axis=1).astype(jnp.bfloat16),
        "tp",
        scatter_dimension=0,
        tiled=True,
    ).astype(jnp.float32)
    time_hot = (jnp.arange(STEPS) == time_index[0]).astype(jnp.float32)
    level_hot = (jnp.arange(LEVELS) == weight_index[0]).astype(jnp.float32)
    strength = jnp.dot(level_hot, weight_table, precision=lax.Precision.HIGHEST)
    table_big = lookup(time_hot, modulation_big)
    table_guide = lookup(time_hot, modulation_guide)
    stream_big = res_big.astype(jnp.float32) + table_big[0] * summed[:, :width_big]
    stream_guide = res_guide.astype(jnp.float32) + table_guide[0] * summed[:, width_big:]
    totals = lax.psum((jnp.sum(stream_big, axis=1), jnp.sum(stream_guide, axis=1)), "seq")
    centred_big = stream_big - (totals[0] / DB)[:, None]
    centred_guide = stream_guide - (totals[1] / DG)[:, None]
    squares = lax.psum(
        (
            jnp.sum(centred_big * centred_big, axis=1),
            jnp.sum(centred_guide * centred_guide, axis=1),
        ),
        "seq",
    )
    variance_big = squares[0] / DB
    variance_guide = squares[1] / DG
    inverse_big = lax.rsqrt(variance_big + EPSILON)[:, None]
    inverse_guide = lax.rsqrt(variance_guide + EPSILON)[:, None]
    normed_big = centred_big * inverse_big
    normed_guide = centred_guide * inverse_guide
    shaped_big = (normed_big * (1.0 + table_big[2]) + table_big[1]).astype(jnp.bfloat16)
    shaped_guide = (normed_guide * (1.0 + table_guide[2]) + table_guide[1]).astype(jnp.bfloat16)
    product_big = jnp.dot(shaped_big, head_big, preferred_element_type=jnp.float32)
    product_guide = jnp.dot(shaped_guide, head_guide, preferred_element_type=jnp.float32)
    cot_big = (strength * cotangent).astype(jnp.bfloat16)
    cot_guide = ((1.0 - strength) * cotangent).astype(jnp.bfloat16)
    scaled_big = jnp.dot(cot_big, head_big.T, preferred_element_type=jnp.float32) * (
        1.0 + table_big[2]
    )
    scaled_guide = jnp.dot(cot_guide, head_guide.T, preferred_element_type=jnp.float32) * (
        1.0 + table_guide[2]
    )
    local_sums = (
        jnp.sum(scaled_big, axis=1),
        jnp.sum(scaled_big * normed_big, axis=1),
        jnp.sum(scaled_guide, axis=1),
        jnp.sum(scaled_guide * normed_guide, axis=1),
    )
    head_sum_big, head_sum_guide, first_big, second_big, first_guide, second_guide = (
        lax.psum(product_big.astype(jnp.bfloat16), "seq").astype(jnp.float32),
        lax.psum(product_guide.astype(jnp.bfloat16), "seq").astype(jnp.float32),
        lax.psum(local_sums[0].astype(jnp.bfloat16), "seq").astype(jnp.float32),
        lax.psum(local_sums[1].astype(jnp.bfloat16), "seq").astype(jnp.float32),
        lax.psum(local_sums[2].astype(jnp.bfloat16), "seq").astype(jnp.float32),
        lax.psum(local_sums[3].astype(jnp.bfloat16), "seq").astype(jnp.float32),
    )
    guided = head_sum_guide + strength * (head_sum_big - head_sum_guide)
    grad_big = inverse_big * (
        scaled_big - (first_big / DB)[:, None] - normed_big * (second_big / DB)[:, None]
    )
    grad_guide = inverse_guide * (
        scaled_guide - (first_guide / DG)[:, None] - normed_guide * (second_guide / DG)[:, None]
    )
    signal = (grad_big * table_big[0]).astype(jnp.bfloat16)
    group_grad = lax.dot_general(
        full_big,
        lax.all_gather(signal, "tp", axis=0, tiled=True),
        (((0,), (0,)), ((), ())),
        preferred_element_type=jnp.float32,
    )
    grad_proj = lax.psum(group_grad.astype(jnp.bfloat16), "grp")
    head_local = lax.dot_general(
        shaped_big, cot_big, (((0,), (0,)), ((), ())), preferred_element_type=jnp.float32
    )
    grad_head = lax.psum(head_local, ("grp", "tp"))
    return (
        guided,
        grad_proj,
        grad_head,
        grad_big.astype(jnp.bfloat16),
        grad_guide.astype(jnp.bfloat16),
    )


def solution(mesh):
    placed = (
        P(("grp", "seq"), "tp"),
        P(("grp", "seq"), "tp"),
        P(("grp", "tp"), "seq"),
        P(("grp", "tp"), "seq"),
        P(("grp", "tp"), None),
        P("tp", "seq"),
        P("tp", "seq"),
        P("seq", None),
        P("seq", None),
        P(None, None, "seq"),
        P(None, None, "seq"),
        P(),
        P("grp"),
        P("grp"),
    )
    return jax.shard_map(
        shards,
        mesh=mesh,
        in_specs=placed,
        out_specs=(
            P(("grp", "tp"), None),
            P("tp", "seq"),
            P("seq", None),
            P(("grp", "tp"), "seq"),
            P(("grp", "tp"), "seq"),
        ),
        check_vma=False,
    )
```

profile of v0, /device:TPU:0, one launch (start us, length us, event | category | flops | bytes accessed | tf_op | source)
XLA Modules:
  0.0 357.4 jit_solution(5863668627623955737)
XLA Ops:
  7.2 0.0 copy-start
  7.2 0.0 all-gather.6.cloned.1.call-start
  7.2 0.7 all-gather.6.cloned.1.call-update
  7.9 0.0 all-gather.4.cloned.1.call-start
  8.0 0.7 all-gather.4.cloned.1.call-update
  8.7 0.0 reduce-scatter.2.cloned.1.call-start
  8.7 21.0 %all-gather.6.cloned.1.call-done = bf16[512,1120]{0,1:T(8,128)(2,1)} async-done(((bf16[128,1120]{0,1:T(8,128)(2,1)}), bf16[512,1120]{0,1:T(8,128)(2,1)}) %all-gather.6.cloned.1.call-update) | async-done | bytes 1146896 | tf_op jit(solution)/shard_map/all_gather | solution.py:39
  29.7 0.0 copy-done
  29.7 2.1 convolution_convert_fusion.2
  31.8 20.4 %all-gather.4.cloned.1.call-done = bf16[512,1728]{0,1:T(8,128)(2,1)} async-done(((bf16[128,1728]{0,1:T(8,128)(2,1)}), bf16[512,1728]{0,1:T(8,128)(2,1)}) %all-gather.4.cloned.1.call-update) | async-done | bytes 1769488 | tf_op jit(solution)/shard_map/all_gather | solution.py:38
  52.3 5.4 %convolution_convert_fusion.1 = bf16[512,1280]{1,0:T(8,128)(2,1)S(1)} fusion(bf16[512,1728]{0,1:T(8,128)(2,1)} %all-gather.4.cloned.1.call-done, bf16[1728,1280]{1,0:T(8,128)(2,1)} %param.19), kind=kOutput, calls=%fused_computation.2 | convolution fusion | flops 2265579520 | bytes 7503872 | tf_op jit(solution)/shard_map/dot_general | solution.py:41
  57.6 0.0 copy-start.6
  57.7 1.3 pad_maximum_fusion
  59.0 0.0 reduce-scatter.2.cloned.1.call-update
  59.0 0.0 all-gather.8.cloned.1.call-start
  60.4 0.0 copy-done.6
  60.4 0.1 copy.20
  60.5 0.1 pad.2
  60.6 0.0 copy-done.1
  60.6 0.4 copy.22
  61.0 0.0 copy-start.9
  61.0 0.2 pad.3
  61.2 0.0 copy-start.7
  61.2 0.2 copy.27
  61.4 0.0 copy-start.4
  61.4 0.3 copy-done.9
  61.7 0.6 fusion.16
  63.0 0.2 convolution_reduce_fusion.1
  63.2 0.4 convolution_reduce_fusion
  63.6 32.9 %reduce-scatter.2.cloned.1.call-done = bf16[128,1664]{1,0:T(8,128)(2,1)} async-done(((bf16[512,1664]{1,0:T(8,128)(2,1)}), bf16[128,1664]{1,0:T(8,128)(2,1)}) %reduce-scatter.2.cloned.1.call-update) | async-done | bytes 426000 | tf_op jit(solution)/shard_map/reduce_scatter | solution.py:43
  96.5 1.1 convert_element_type.76
  97.5 0.0 copy-start.8
  97.5 0.0 copy-start.5
  97.6 0.0 copy-done.7
  97.6 0.1 fusion.24
  97.7 0.0 copy-start.2
  97.7 0.0 copy-done.4
  97.7 0.2 fusion.22
  97.9 6.4 %all-reduce.1 = (f32[128]{0:T(128)S(1)}, f32[128]{0:T(128)S(1)}) all-reduce(f32[128]{0:T(128)S(1)} %get-tuple-element.23, f32[128]{0:T(128)S(1)} %get-tuple-element.21), channel_id=1, replica_groups=mesh['grp'=2,'seq'=4,'tp'=4] {'seq'}, use_global_device_ids=true, to_apply=%region_2.0 | all-reduce | flops 256 | bytes 2048 | tf_op jit(solution)/shard_map/psum | solution.py:56
  104.3 0.2 multiply_reduce_fusion.1
  104.5 0.2 multiply_reduce_fusion.3
  104.7 5.9 %all-reduce = (f32[128]{0:T(128)S(1)}, f32[128]{0:T(128)S(1)}) all-reduce(f32[128]{0:T(128)S(1)} %multiply_reduce_fusion.3, f32[128]{0:T(128)S(1)} %multiply_reduce_fusion.1), channel_id=1, replica_groups=mesh['grp'=2,'seq'=4,'tp'=4] {'seq'}, use_global_device_ids=true, to_apply=%region_4.0 | all-reduce | flops 256 | bytes 2048 | tf_op jit(solution)/shard_map/psum | solution.py:59
  110.6 0.0 copy-done.8
  110.6 0.2 convolution_convert_fusion.3
  110.8 0.3 fusion.20
  111.2 1.0 fusion.19
  112.2 0.2 convolution_convert_fusion.4
  112.4 11.0 %all-reduce.2 = (bf16[128,64]{0,1:T(8,128)(2,1)S(1)}, bf16[128,64]{0,1:T(8,128)(2,1)S(1)}, bf16[128]{0:T(256)(128)(2,1)S(1)}, bf16[128]{0:T(256)(128)(2,1)S(1)},...) all-reduce(bf16[128,64]{0,1:T(8,128)(2,1)S(1)} %convolution_convert, ...), channel_id=1, replica_groups=mesh['grp'=2,'seq'=4,'tp'=4] {'seq'}, use_global_device_ids=true, to_apply=%region_5.0 | all-reduce | flops 16896 | bytes 67584 | tf_op jit(solution)/shard_map/psum | solution.py:92
  123.5 1.0 fusion.21
  124.4 0.8 multiply_convert_fusion
  125.2 0.0 all-gather.8.cloned.1.call-update
  125.2 0.0 all-reduce.8.cloned.1.call-start
  125.3 1.6 fusion.9
  126.8 0.0 all-reduce.8.cloned.1.call-update
  126.8 0.0 all-reduce.6.cloned.1.call-start
  126.9 30.0 %all-gather.8.cloned.1.call-done = bf16[512,1280]{1,0:T(8,128)(2,1)} async-done(((bf16[128,1280]{1,0:T(8,128)(2,1)}), bf16[512,1280]{1,0:T(8,128)(2,1)}) %all-gather.8.cloned.1.call-update) | async-done | bytes 1310736 | tf_op jit(solution)/shard_map/all_gather | solution.py:108
  156.9 6.4 %fusion = bf16[1728,1280]{1,0:T(8,128)(2,1)} fusion(bf16[512,1728]{0,1:T(8,128)(2,1)} %all-gather.4.cloned.1.call-done, bf16[512,1280]{1,0:T(8,128)(2,1)} %all-gather.8.cloned.1.call-done), kind=kOutput, calls=%fused_computation.1 | convolution fusion | flops 2267136000 | bytes 7503872 | tf_op jit(solution)/shard_map/dot_general | solution.py:106
  163.3 0.0 all-reduce.6.cloned.1.call-update
  163.3 1.2 convert_add_fusion
  164.6 0.8 multiply_convert_fusion.1
  165.4 64.7 %all-reduce.8.cloned.1.call-done = f32[1280,64]{0,1:T(8,128)} async-done(((f32[1280,64]{0,1:T(8,128)}), f32[1280,64]{0,1:T(8,128)}) %all-reduce.8.cloned.1.call-update) | async-done | bytes 327696 | tf_op jit(solution)/shard_map/psum | solution.py:116
  230.1 115.1 %all-reduce.6.cloned.1.call-done = bf16[1728,1280]{1,0:T(8,128)(2,1)} async-done(((bf16[1728,1280]{1,0:T(8,128)(2,1)}), bf16[1728,1280]{1,0:T(8,128)(2,1)}) %all-reduce.6.cloned.1.call-update) | async-done | bytes 4423696 | tf_op jit(solution)/shard_map/psum | solution.py:112
  345.2 4.7 %copy.32 = bf16[1728,1280]{1,0:T(8,128)(2,1)} copy(bf16[1728,1280]{1,0:T(8,128)(2,1)} %all-reduce.6.cloned.1.call-done) | data formatting | bytes 8847360
  349.8 0.7 copy.33
  (15 shorter events, 0.1 us)
Async XLA Ops:
  7.2 22.5 %copy-start = (bf16[1120,384]{1,0:T(8,128)(2,1)S(1)}, bf16[1120,384]{1,0:T(8,128)(2,1)}, u32[]{:S(2)}) copy-start(bf16[1120,384]{1,0:T(8,128)(2,1)} %param.20) | copy-start | bytes 2580484
  7.2 22.5 %all-gather.6.cloned.1.call-start = ((), (), s32[]{:S(2)}) async-start(), calls=%async_computation.2 | async-start | bytes 1433600 | tf_op jit(solution)/shard_map/all_gather | solution.py:39
  7.9 44.3 %all-gather.4.cloned.1.call-start = ((), (), s32[]{:S(2)}) async-start(), calls=%async_computation.1 | async-start | bytes 2211840 | tf_op jit(solution)/shard_map/all_gather | solution.py:38
  8.7 87.8 %reduce-scatter.2.cloned.1.call-start = ((), (), s32[]{:S(2)}) async-start(), calls=%async_computation.3 | async-start | bytes 2129920 | tf_op jit(solution)/shard_map/reduce_scatter | solution.py:43
  57.6 2.8 copy-start.6
  59.0 1.6 copy-start.1
  59.0 97.9 %all-gather.8.cloned.1.call-start = ((), (), s32[]{:S(2)}) async-start(), calls=%async_computation.4 | async-start | bytes 1638400 | tf_op jit(solution)/shard_map/all_gather | solution.py:108
  61.0 0.7 copy-start.9
  61.2 36.3 %copy-start.7 = (bf16[128,384]{1,0:T(8,128)(2,1)S(1)}, bf16[128,384]{1,0:T(8,128)(2,1)}, u32[]{:S(2)}) copy-start(bf16[128,384]{1,0:T(8,128)(2,1)} %param.17) | copy-start | bytes 294916
  61.4 36.3 %copy-start.4 = (bf16[128,1280]{1,0:T(8,128)(2,1)S(1)}, bf16[128,1280]{1,0:T(8,128)(2,1)}, u32[]{:S(2)}) copy-start(bf16[128,1280]{1,0:T(8,128)(2,1)} %param.16) | copy-start | bytes 983044
  97.5 13.0 %copy-start.8 = (bf16[384,64]{0,1:T(8,128)(2,1)S(1)}, bf16[384,64]{0,1:T(8,128)(2,1)}, u32[]{:S(2)}) copy-start(bf16[384,64]{0,1:T(8,128)(2,1)} %param.22) | copy-start | bytes 147460
  97.5 13.3 %copy-start.5 = (f32[128,64]{0,1:T(8,128)S(1)}, f32[128,64]{0,1:T(8,128)}, u32[]{:S(2)}) copy-start(f32[128,64]{0,1:T(8,128)} %param.18) | copy-start | bytes 98308
  97.7 13.5 %copy-start.2 = (bf16[1280,64]{0,1:T(8,128)(2,1)S(1)}, bf16[1280,64]{0,1:T(8,128)(2,1)}, u32[]{:S(2)}) copy-start(bf16[1280,64]{0,1:T(8,128)(2,1)} %param.21) | copy-start | bytes 491524
  125.2 104.9 %all-reduce.8.cloned.1.call-start = ((), (), s32[]{:S(2)}) async-start(), calls=%async_computation.6 | async-start | bytes 655360 | tf_op jit(solution)/shard_map/psum | solution.py:116
  126.8 218.3 %all-reduce.6.cloned.1.call-start = ((), (), s32[]{:S(2)}) async-start(), calls=%async_computation.5 | async-start | bytes 8847360 | tf_op jit(solution)/shard_map/psum | solution.py:112
  345.2 4.7 %copy-start.3 = (f32[1280,64]{0,1:T(8,128)S(1)}, f32[1280,64]{0,1:T(8,128)}, u32[]{:S(2)}) copy-start(f32[1280,64]{0,1:T(8,128)} %all-reduce.8.cloned.1.call-done) | copy-start | bytes 983044
Sparse Core Ops, SparseCore 0:
  9.6 20.0 all-gather.5
  31.3 20.9 all-gather.3
  59.1 37.3 reduce-scatter.1
  125.3 31.4 all-gather.7
  160.1 69.9 all-reduce.7
  233.1 112.0 all-reduce.5
where the time goes:
time: 358 us; the launch traced here: 357 us
  waiting for transfers between devices  286 us (80%)
  blocking collectives  23.3 us (7%)
  matrix products  17.9 us (5%)
  between operations  16.4 us (5%)
  other arithmetic  7.52 us (2%)
  local copies, waits for them, and re-layouts  6.62 us (2%)
    psum x1, waiting for transfers between devices, shards(): grad_proj = lax.psum(group_grad.astype(jnp.bfloat16), 'grp')  115 us
    psum x1, waiting for transfers between devices, shards(): grad_head = lax.psum(head_local, ('grp', 'tp'))  64.7 us
    reduce_scatter x1, waiting for transfers between devices, shards(): lax.psum_scatter(jnp.concatenate([term_big, term_guide], axis=1).astype(j...  32.9 us
    all_gather x1, waiting for transfers between devices, shards(): lax.all_gather(signal, 'tp', axis=0, tiled=True)  30 us
    all_gather x1, waiting for transfers between devices, shards(): lax.all_gather(fc_guide, 'seq', axis=0, tiled=True)  21 us
    all_gather x1, waiting for transfers between devices, shards(): lax.all_gather(fc_big, 'seq', axis=0, tiled=True)  20.4 us
    psum x1, blocking collectives, shards(): lax.psum(product_guide.astype(jnp.bfloat16), 'seq').astype(jnp.float32)  11 us
  transfers between devices with their start and end apart: 6, of which 6 were waited for; matrix products, arithmetic and copies ran while one was open for 4% of the time, Pallas kernels for 0%

commit v1 on v0

v1 whole, which is shorter than its diff:
```python
import functools

import jax
import jax.numpy as jnp
from jax import lax
from jax.experimental import pallas as pl
from jax.experimental.pallas import tpu as pltpu
from jax.sharding import PartitionSpec as P

EPSILON = 1e-06
F32 = jnp.float32
BF16 = jnp.bfloat16
VMEM = 40 * 1024 * 1024
VMEM_NORM = 24 * 1024 * 1024
VMEM_SMALL = 8 * 1024 * 1024
SHORT = pl.CostEstimate(flops=0, bytes_accessed=0, transcendentals=0)


def swap(x, axis, size, bits):
    return lax.ppermute(x, axis, [(i, i ^ bits) for i in range(size)])


def near_far(block, n, later=()):
    far = [swap(after(block, later), "seq", n, k) for k in range(2, n, 2)]
    return [block, swap(block, "seq", n, 1)], far


def forward(far, n, later=()):
    return [x for block in far for x in (block, swap(after(block, later), "seq", n, 1))]


def gather_direct(block, axis, n):
    return [block] + [swap(block, axis, n, j) for j in range(1, n)]


def after(x, *others):
    return lax.optimization_barrier((x, others))[0]


def gather_pairs(block):
    pairs = [(4 * g + t, 4 * (1 - g) + (t ^ 1)) for g in range(2) for t in range(4)]
    two = swap(block, "tp", 4, 2)
    across = swap(block, "grp", 2, 1)
    across_one = lax.ppermute(block, ("grp", "tp"), pairs)
    two = lax.optimization_barrier((across_one, across, two))[2]
    three = swap(two, "tp", 4, 1)
    across_two = swap(two, "grp", 2, 1)
    three = after(three, across_two)
    across_three = swap(three, "grp", 2, 1)
    one = swap(after(block, two), "tp", 4, 1)
    return [block, one, two, three], [across, across_one, across_two, across_three]


def add_kernel(left, right, out):
    out[...] = (left[...].astype(F32) + right[...].astype(F32)).astype(BF16)


def add(left, right):
    return pl.pallas_call(
        add_kernel,
        out_shape=jax.ShapeDtypeStruct(left.shape, BF16),
        compiler_params=pltpu.CompilerParams(vmem_limit_bytes=VMEM_SMALL),
        cost_estimate=SHORT,
        name="add",
    )(left, right)


def scatter(terms, n):
    if n != 4:
        return [terms[0]] + [swap(terms[k], "tp", n, k) for k in range(1, n)], terms[0]
    joined = add(terms[2], swap(terms[3], "tp", n, 1))
    return [terms[0], swap(terms[1], "tp", n, 1), swap(joined, "tp", n, 2)], joined


def lookup_kernel(count, *refs):
    steps, tables, outs = refs[:count], refs[count : 2 * count], refs[2 * count :]
    for step, table, out in zip(steps, tables, outs):
        for row in range(3):
            out[row : row + 1, :] = table[row, pl.ds(step[0], 1), :]


def lookup(tables, steps):
    turned = [jnp.transpose(table, (1, 0, 2)) for table in tables]
    count = len(tables)
    return pl.pallas_call(
        functools.partial(lookup_kernel, count),
        in_specs=[pl.BlockSpec(memory_space=pltpu.SMEM)] * count
        + [pl.BlockSpec(memory_space=pltpu.VMEM)] * count,
        out_shape=[jax.ShapeDtypeStruct((3, t.shape[2]), F32) for t in turned],
        compiler_params=pltpu.CompilerParams(vmem_limit_bytes=VMEM_SMALL),
        cost_estimate=SHORT,
        name="lookup",
    )(*steps, *turned)


def total(parts):
    return sum(p.astype(F32) for p in parts)


def meeting():
    return jnp.bitwise_xor(lax.axis_index("seq"), lax.axis_index("tp"))


def turned_dot(left, right):
    return lax.dot_general(left, right, (((0,), (0,)), ((), ())), preferred_element_type=F32)


def whole_block(x):
    return pl.BlockSpec(x.shape, lambda i: (0,) * x.ndim)


def project_kernel(last, filled, n, *refs):
    blocks, weight = refs[:n], refs[n]
    rows = blocks[0].shape[1]
    left = refs[-2] if last else refs[-1]

    @pl.when(pl.program_id(0) == 0)
    def _():
        for j in range(n):
            left[j * rows : (j + 1) * rows, :] = blocks[j][...].T

    product = jnp.dot(left[...], weight[...], preferred_element_type=F32).astype(BF16)
    if not last:
        refs[n + 1][...] = product
        return
    every = refs[-1]
    earlier = refs[n + 1].shape[0]
    total_blocks = n + earlier // rows
    every[:earlier, :] = refs[n + 1][...]
    every[earlier:, :] = product
    outs = refs[n + 2 + filled * total_blocks : -2]
    turn = meeting()
    for k in range(total_blocks):
        start = pl.multiple_of(jnp.bitwise_xor(turn, k) * rows, rows)
        outs[k][...] = every[pl.ds(start, rows), :]


def project_early(blocks, weight, tile):
    n = len(blocks)
    depth, columns = weight.shape
    rows = blocks[0].shape[0]
    turned = [block.T for block in blocks]
    return pl.pallas_call(
        functools.partial(project_kernel, False, False, n),
        grid=(pl.cdiv(columns, tile),),
        in_specs=[whole_block(t) for t in turned] + [pl.BlockSpec((depth, tile), lambda i: (0, i))],
        out_specs=pl.BlockSpec((n * rows, tile), lambda i: (0, i)),
        out_shape=jax.ShapeDtypeStruct((n * rows, columns), BF16),
        scratch_shapes=[pltpu.VMEM((n * rows, depth), BF16)],
        compiler_params=pltpu.CompilerParams(vmem_limit_bytes=VMEM),
        cost_estimate=SHORT,
        name="project_early",
    )(*turned, weight)


def project(blocks, weight, tile, width, early, before=()):
    n = len(blocks)
    depth, columns = weight.shape
    rows = blocks[0].shape[0]
    owners = n + early.shape[0] // rows
    turned = [block.T for block in blocks]
    first = (width - columns) // tile if before else 0
    anywhere = pl.BlockSpec(memory_space=pl.ANY)
    return pl.pallas_call(
        functools.partial(project_kernel, True, bool(before), n),
        grid=(pl.cdiv(columns, tile),),
        in_specs=[whole_block(t) for t in turned]
        + [pl.BlockSpec((depth, tile), lambda i: (0, i))]
        + [pl.BlockSpec((early.shape[0], tile), lambda i: (0, i))]
        + [anywhere] * len(before),
        out_specs=[pl.BlockSpec((rows, tile), lambda i: (0, first + i)) for _ in range(owners)],
        out_shape=[jax.ShapeDtypeStruct((rows, width), BF16) for _ in range(owners)],
        input_output_aliases={n + 2 + k: k for k in range(len(before))},
        scratch_shapes=[
            pltpu.VMEM((n * rows, depth), BF16),
            pltpu.VMEM((owners * rows, tile), BF16),
        ],
        compiler_params=pltpu.CompilerParams(vmem_limit_bytes=VMEM),
        cost_estimate=SHORT,
        name="project",
    )(*turned, weight, early, *before)


def contract_kernel(n, counts, more, *refs):
    refs = list(refs)
    take = lambda count: [refs.pop(0) for _ in range(count)]
    samples = [(take(n), take(len(slots)), *take(1)) for slots in counts]
    (head,) = take(1)
    before = take(2) if more else None
    out, head_out, signal, shelf, done = refs
    patch, rows, tile = head.shape[0], shelf.shape[2], out.shape[0]
    turn = meeting()
    wanted = [(hidden, k) for slots, (hidden, *_) in zip(counts, samples) for k in slots]

    @pl.when(pl.program_id(0) == 0)
    def _():
        for place, (hidden, k) in enumerate(wanted):
            for j in range(n):

                @pl.when(jnp.bitwise_xor(turn, k) == j)
                def _():
                    pltpu.make_async_copy(hidden[j], shelf.at[place], done.at[place]).start()

        gradient = before[1][...] if more else jnp.zeros(head_out.shape, F32)
        place = 0
        for _, sent, table in samples:
            gate, shift, scale = table[0:1, :], table[1:2, :], 1.0 + table[2:3, :]
            for ref in sent:
                block = ref[...].astype(F32)
                normed = block[:rows]
                pieces = [
                    block[r : r + 8, c : c + rows]
                    for r in range(rows, block.shape[0], 8)
                    for c in range(0, block.shape[1] - rows + 1, rows)
                ]
                sums = pieces[0] + jnp.concatenate([pieces[0][3:], pieces[0][:3]], axis=0)
                sums = sums.T
                cot = jnp.concatenate(pieces[1 : 1 + patch // 8], axis=0).astype(BF16)
                inverse, first, second = sums[:, 0:1], sums[:, 1:2], sums[:, 2:3]
                scaled = turned_dot(cot, head[...]) * scale
                grad = inverse * (scaled - first - normed * second)
                signal[place : place + rows, :] = (grad * gate).astype(BF16)
                shaped = (normed * scale + shift).astype(BF16)
                gradient = gradient + jnp.dot(cot, shaped, preferred_element_type=F32)
                place += rows
        head_out[...] = gradient
        for place, (hidden, _) in enumerate(wanted):
            pltpu.make_async_copy(hidden[0], shelf.at[place], done.at[place]).wait()

    here = pl.ds(pl.multiple_of(pl.program_id(0) * tile, tile), tile)
    left = jnp.concatenate([shelf[place, here, :] for place in range(len(wanted))], axis=1)
    product = jnp.dot(left, signal[...], preferred_element_type=F32)
    if more:
        product = product + before[0][here, :].astype(F32)
    out[...] = product.astype(BF16)


def contract(samples, head, before=None):
    n = len(samples[0][0])
    counts = [tuple(slots) for _, slots, *_ in samples]
    tokens, depth = samples[0][0][0].shape
    width = head.shape[1]
    tile = max(t for t in range(16, min(depth, 576) + 1, 16) if depth % t == 0)
    operands, in_specs = [], []
    for hidden, slots, sent, table in samples:
        operands += [block.T for block in hidden]
        in_specs += [pl.BlockSpec(memory_space=pl.ANY) for _ in range(n)]
        rest = [*(sent[k] for k in slots), table]
        operands += rest
        in_specs += [whole_block(x) for x in rest]
    operands.append(head)
    in_specs.append(whole_block(head))
    if before is not None:
        operands += before
        in_specs += [pl.BlockSpec(memory_space=pltpu.VMEM), whole_block(before[1])]
    return pl.pallas_call(
        functools.partial(contract_kernel, n, counts, before is not None),
        grid=(depth // tile,),
        in_specs=in_specs,
        out_specs=[pl.BlockSpec((tile, width), lambda i: (i, 0)), whole_block(head)],
        out_shape=[
            jax.ShapeDtypeStruct((depth, width), BF16),
            jax.ShapeDtypeStruct(head.shape, F32),
        ],
        scratch_shapes=[
            pltpu.VMEM((sum(map(len, counts)) * tokens, width), BF16),
            pltpu.VMEM((sum(map(len, counts)), depth, tokens), BF16),
            pltpu.SemaphoreType.DMA((sum(map(len, counts)),)),
        ],
        compiler_params=pltpu.CompilerParams(vmem_limit_bytes=VMEM),
        cost_estimate=SHORT,
        name="contract",
    )(*operands)


def lanes(shape):
    return lax.broadcasted_iota(jnp.int32, shape, 1)


def model_stats(summed, res, table, head, cot):
    patch, rows = cot.shape
    gate, shift, scale = table[0:1, :], table[1:2, :], 1.0 + table[2:3, :]
    stream = res[...].astype(F32) + gate * summed
    scaled = turned_dot(cot.astype(BF16), head[...]) * scale
    mean = jnp.mean(stream, axis=1, keepdims=True)
    centred = stream - mean
    columns = [
        mean,
        jnp.sum(centred * centred, axis=1, keepdims=True),
        jnp.sum(scaled, axis=1, keepdims=True),
        jnp.sum(scaled * centred, axis=1, keepdims=True),
    ]
    lane = lanes((rows, rows))
    spread = jnp.zeros((rows, rows), F32)
    for place, column in enumerate(columns):
        spread = jnp.where(lane == place, column, spread)
    first = spread.T[:8]
    wide = head[...].astype(F32)
    slope = jnp.sum(wide * scale, axis=1, keepdims=True)
    offset = jnp.sum(wide * shift, axis=1, keepdims=True)
    lane, row = lanes((patch, rows)), lax.broadcasted_iota(jnp.int32, (patch, rows), 0)
    both = jnp.where(lane == row, slope, jnp.where(lane == row + patch, offset, 0.0))
    both = jnp.sum(both, axis=0, keepdims=True)
    first = jnp.where(lax.broadcasted_iota(jnp.int32, (8, rows), 0) == len(columns), both, first)
    product = lax.dot_general(
        head[...], (centred * scale).astype(BF16), (((1,), (1,)), ((), ())), preferred_element_type=F32
    )
    return stream, scaled, jnp.concatenate([first, product], axis=0)


def stats_kernel(n, *refs):
    big, guide = refs[n : n + 3], refs[n + 3 : n + 6]
    cot, strength = refs[n + 6][...], refs[n + 7][refs[n + 8][0]]
    stream_big, scaled_big, stream_guide, scaled_guide, told = refs[n + 9 :]
    summed = total([ref[...] for ref in refs[:n]])
    width = big[0].shape[1]
    stream_big[...], scaled_big[...], told_big = model_stats(summed[:, :width], *big, strength * cot)
    stream_guide[...], scaled_guide[...], told_guide = model_stats(
        summed[:, width:], *guide, (1.0 - strength) * cot
    )
    left = jnp.concatenate([told_big[:8], told_guide[:8]], axis=0)
    parts = []
    for _ in range(3):
        parts.append(left.astype(BF16).astype(F32))
        left = left - parts[-1]
    told[...] = jnp.concatenate([*parts, told_big[8:], told_guide[8:]], axis=0).astype(BF16)


def specs(arrays):
    return [pl.BlockSpec(memory_space=pltpu.VMEM) for _ in arrays] + [
        pl.BlockSpec(memory_space=pltpu.SMEM) for _ in range(2)
    ]


def local_stats(received, big, guide, cot, weight):
    patch, rows = cot.shape
    widths = [model[-1].shape[1] for model in (big, guide)]
    shapes = [(rows, w) for w in widths for _ in range(2)]
    arrays = [*received, *big, *guide, cot]
    return pl.pallas_call(
        functools.partial(stats_kernel, len(received)),
        in_specs=specs(arrays),
        out_shape=[jax.ShapeDtypeStruct(shape, F32) for shape in shapes]
        + [jax.ShapeDtypeStruct((48 + 2 * patch, rows), BF16)],
        compiler_params=pltpu.CompilerParams(vmem_limit_bytes=VMEM_NORM),
        cost_estimate=SHORT,
        name="local_stats",
    )(*arrays, *weight)


def model_norm(parts, products, stream, scaled):
    rows, width = stream.shape
    full, count = width * len(parts), len(parts)
    patch = products[0].shape[0]
    centre = sum(p[0:1] for p in parts) / count
    squares = sum(p[1:2] + width * jnp.square(p[0:1] - centre) for p in parts)
    inverse = lax.rsqrt(squares / full + EPSILON)
    first = sum(p[2:3] for p in parts) / full
    second = inverse * sum(p[3:4] + (p[0:1] - centre) * p[2:3] for p in parts) / full
    sums = jnp.concatenate([inverse, first, second], axis=0)
    turned = jnp.concatenate([sums, centre, jnp.zeros((4, rows), F32)], axis=0).T
    normed = (stream[...] - turned[:, 3:4]) * turned[:, 0:1]
    grad = turned[:, 0:1] * (scaled[...] - turned[:, 1:2] - normed * turned[:, 2:3])
    lane, row = lanes((patch, rows)), lax.broadcasted_iota(jnp.int32, (patch, rows), 0)
    out, offset = 0.0, 0.0
    for p, product in zip(parts, products):
        slope = jnp.sum(jnp.where(lane == row, p[4:5], 0.0), axis=1, keepdims=True)
        offset += jnp.sum(jnp.where(lane == row + patch, p[4:5], 0.0), axis=1, keepdims=True)
        out += product + (p[0:1] - centre) * slope
    return normed, grad, sums, inverse * out + offset


def norm_kernel(n, *refs):
    told = [ref[...].astype(F32) for ref in refs[:n]]
    first = [t[:16] + t[16:32] + t[32:48] for t in told]
    stream_big, scaled_big, stream_guide, scaled_guide, cot = refs[n : n + 5]
    strength = refs[n + 5][refs[n + 6][0]]
    sent, grad_big, grad_guide, guided = refs[n + 7 :]
    half = 48 + (told[0].shape[0] - 48) // 2
    normed, grad, sums, out_big = model_norm(
        [f[:8] for f in first], [t[48:half] for t in told], stream_big, scaled_big
    )
    grad_big[...] = grad.astype(BF16)
    rows, width = normed.shape
    high = sums.astype(BF16).astype(F32)
    pieces = [jnp.concatenate([high, sums - high, jnp.zeros((2, rows), F32)], axis=0)]
    weighted = strength * cot[...]
    pieces += [weighted[r : r + 8] for r in range(0, weighted.shape[0], 8)]
    across = width // rows
    lines = [normed]
    for r in range(0, len(pieces), across):
        line = pieces[r : r + across]
        line += [jnp.zeros((8, width - rows * len(line)), F32)] if width > rows * len(line) else []
        lines.append(jnp.concatenate(line, axis=1))
    sent[...] = jnp.concatenate(lines, axis=0).astype(BF16)
    _, grad, _, out_guide = model_norm(
        [f[8:] for f in first], [t[half:] for t in told], stream_guide, scaled_guide
    )
    grad_guide[...] = grad.astype(BF16)
    guided[...] = out_guide + strength * (out_big - out_guide)


def whole_norm(told, streams, cot, weight):
    patch, rows = cot.shape
    width_big, width_guide = streams[0].shape[1], streams[2].shape[1]
    below = 8 * pl.cdiv(1 + patch // 8, width_big // rows)
    arrays = [*told, *streams, cot]
    return pl.pallas_call(
        functools.partial(norm_kernel, len(told)),
        in_specs=specs(arrays),
        out_shape=[
            jax.ShapeDtypeStruct((rows + below, width_big), BF16),
            jax.ShapeDtypeStruct((rows, width_big), BF16),
            jax.ShapeDtypeStruct((rows, width_guide), BF16),
            jax.ShapeDtypeStruct((patch, rows), F32),
        ],
        compiler_params=pltpu.CompilerParams(vmem_limit_bytes=VMEM_NORM),
        cost_estimate=SHORT,
        name="whole_norm",
    )(*arrays, *weight)


def shards(
    sizes,
    fc_big,
    fc_guide,
    res_big,
    res_guide,
    cotangent,
    proj_big,
    proj_guide,
    head_big,
    head_guide,
    modulation_big,
    modulation_guide,
    weight_table,
    time_index,
    weight_index,
):
    n_grp, n_seq, n_tp = sizes
    width_big, width_guide = proj_big.shape[1], proj_guide.shape[1]
    tile = 256 if width_big % 256 == 0 else 128
    width_big, width_guide = proj_big.shape[1], proj_guide.shape[1]
    tile = 256 if width_big % 256 == 0 else 128
    near_big, far_big = near_far(fc_big, n_seq)
    near_guide, far_guide = near_far(fc_guide, n_seq, near_big[1])
    early_big = project_early(near_big, proj_big, tile)
    far_big = forward(far_big, n_seq, early_big)
    big_blocks = near_big + far_big
    early_guide = project_early(after(near_guide, early_big), proj_guide, 128)
    far_guide = forward(far_guide, n_seq, (early_guide, far_big[0]))
    fc_crossed = [swap(fc_big, "grp", n_grp, g) for g in range(1, n_grp)]

    width = width_big + width_guide
    terms = project(far_big, proj_big, tile, width, early_big)
    terms = project(far_guide, proj_guide, 128, width, early_guide, terms)
    received, joined = scatter(terms, n_tp)
    begun = after((fc_crossed, modulation_big, modulation_guide), terms)
    time_late = after(time_index, terms)
    time_others = [swap(time_late, "grp", n_grp, g) for g in range(1, n_grp)]
    fc_far = [
        [block, *(swap(block, "seq", n_seq, k) for k in range(2, n_seq, 2))] for block in begun[0]
    ]
    table_big, table_guide, *tables = lookup(
        [begun[1], begun[2], *(begun[1] for _ in time_others)], [time_index, time_index, *time_others]
    )
    received, fc_far, tables, table_big, table_guide = lax.optimization_barrier(
        (received, fc_far, tables, table_big, table_guide)
    )
    fc_others = [forward(far, n_seq) for far in fc_far]
    weight = (weight_table, weight_index)

    head_big, head_guide, cot = head_big.T, head_guide.T, cotangent.T
    *streams, told = local_stats(
        received, [res_big, table_big, head_big], [res_guide, table_guide, head_guide], cot, weight
    )
    told = gather_direct(told, "seq", n_seq)
    sent, grad_big, grad_guide, guided = whole_norm(told, streams, cot, weight)

    if (n_grp, n_tp) == (2, 4):
        sent_tp, crossed = gather_pairs(sent)
        own = (big_blocks, (0, 2, 3), sent_tp, table_big)
        other = (fc_others[0], (0, 1, 2), crossed, tables[0])
        grads = contract([own, other], head_big)
        own, other = (own[0], (1,), *own[2:]), (other[0], (3,), *other[2:])
        grads = contract([own, other], head_big, grads)
    else:
        sent_tp = gather_direct(sent, "tp", n_tp)
        every = tuple(range(n_tp))
        grads = contract([(big_blocks, every, sent_tp, table_big)], head_big)
        for g in range(1, n_grp):
            crossed = [swap(x, "grp", n_grp, g) for x in sent_tp]
            sample = (fc_others[g - 1], every, crossed, tables[g - 1])
            grads = contract([sample], head_big, grads)
    return (
        guided.T,
        grads[0],
        grads[1].T,
        grad_big,
        grad_guide,
    )


def solution(mesh):
    sizes = tuple(mesh.shape[name] for name in ("grp", "seq", "tp"))
    placed = (
        P(("grp", "seq"), "tp"),
        P(("grp", "seq"), "tp"),
        P(("grp", "tp"), "seq"),
        P(("grp", "tp"), "seq"),
        P(("grp", "tp"), None),
        P("tp", "seq"),
        P("tp", "seq"),
        P("seq", None),
        P("seq", None),
        P(None, None, "seq"),
        P(None, None, "seq"),
        P(),
        P("grp"),
        P("grp"),
    )
    return jax.shard_map(
        functools.partial(shards, sizes),
        mesh=mesh,
        in_specs=placed,
        out_specs=(
            P(("grp", "tp"), None),
            P("tp", "seq"),
            P("seq", None),
            P(("grp", "tp"), "seq"),
            P(("grp", "tp"), "seq"),
        ),
        check_vma=False,
    )
```

time: 358 us -> 115 us (0.32)
  waiting for transfers between devices: 286 us -> 55.6 us
  starting transfers between devices: 0.24 us -> 27 us
  Pallas kernels: 0 us -> 25.4 us
  blocking collectives: 23.3 us -> 0 us
  matrix products: 17.9 us -> 0 us
  between operations: 16.4 us -> 2.14 us
  other arithmetic: 7.52 us -> 0 us
    psum x2 -> x0, waiting for transfers between devices: 180 us -> none  [the longest x1 115 us: shards(): grad_proj = lax.psum(group_grad.astype(jnp.bfloat16), 'grp')]
    all_gather x3 -> x0, waiting for transfers between devices: 71.4 us -> none  [the longest x1 30 us: shards(): lax.all_gather(signal, 'tp', axis=0, tiled=True)]
    ppermute x0 -> x24, waiting for transfers between devices: none -> 55.6 us  [the longest x23 54.3 us: swap(): return lax.ppermute(x, axis, [(i, i ^ bits) for i in range(size)])]
    reduce_scatter x1 -> x0, waiting for transfers between devices: 32.9 us -> none  [shards(): lax.psum_scatter(jnp.concatenate([term_big, term_guide], axis=1).astype(j...]
    ppermute x0 -> x24, starting transfers between devices: none -> 27 us  [the longest x23 21.9 us: swap(): return lax.ppermute(x, axis, [(i, i ^ bits) for i in range(size)])]
    pallas_call x0 -> x10, Pallas kernels: none -> 25.4 us  [the longest x2 12.2 us: contract(): pl.pallas_call(functools.partial(contract_kernel, n, counts, before is no...]
    psum x3 -> x0, blocking collectives: 23.3 us -> none  [the longest x1 11 us: shards(): lax.psum(product_guide.astype(jnp.bfloat16), 'seq').astype(jnp.float32)]
    dot_general x10 -> x0, matrix products: 17.9 us -> none  [the longest x1 6.4 us: shards(): lax.dot_general(full_big, lax.all_gather(signal, 'tp', axis=0, tiled=True...]
  transfers between devices with their start and end apart: 6 -> 24, of which waited for: 6 -> 13; matrix products, arithmetic and copies ran while one was open for 4% -> 0% of each run, Pallas kernels for 0% -> 15%
where the time goes in v1:
time: 115 us; the launch traced here: 114 us
  waiting for transfers between devices  55.6 us (48%)
  starting transfers between devices  27 us (23%)
  Pallas kernels  25.4 us (22%)
  local copies, waits for them, and re-layouts  4.28 us (4%)
  between operations  2.14 us (2%)
    ppermute x23, waiting for transfers between devices, swap(): return lax.ppermute(x, axis, [(i, i ^ bits) for i in range(size)])  54.3 us
    ppermute x23, starting transfers between devices, swap(): return lax.ppermute(x, axis, [(i, i ^ bits) for i in range(size)])  21.9 us
    pallas_call x2, Pallas kernels, contract(): pl.pallas_call(functools.partial(contract_kernel, n, counts, before is no...  12.2 us
    ppermute x1, starting transfers between devices, gather_pairs(): across_one = lax.ppermute(block, ('grp', 'tp'), pairs)  5.19 us
    pallas_call x2, Pallas kernels, project(): pl.pallas_call(functools.partial(project_kernel, True, bool(before), n),...  5.07 us
    unnamed x28, local copies, waits for them, and re-layouts  4.28 us
    pallas_call x2, Pallas kernels, project_early(): pl.pallas_call(functools.partial(project_kernel, False, False, n), grid=(...  4.13 us
  transfers between devices with their start and end apart: 24, of which 13 were waited for; matrix products, arithmetic and copies ran while one was open for 0% of the time, Pallas kernels for 15%

profile of v1, /device:TPU:0, one launch (start us, length us, event | category | flops | bytes accessed | tf_op | source)
XLA Modules:
  0.0 114.5 jit_solution(410213098610487100)
XLA Ops:
  0.6 0.5 collective-permute-start
  1.1 2.6 %collective-permute-start.3 = (bf16[128,1728]{0,1:T(8,128)(2,1)}, bf16[128,1728]{0,1:T(8,128)(2,1)S(1)}, u32[]{:S(2)}, u32[]{:S(2)}) collective-permute-start(bf16[128,1728]{0,1:T(8,128)(2,1)} %param.14), channel_id=1, source_target_pairs={{0,8},{4,12},{8,0},{12,4},{1,9},{5,13},{9,1},{13,5},{2,10},{6,14},... | collective-permute-start | bytes 1327112 | tf_op jit(solution)/shard_map/ppermute | solution.py:20
  3.7 0.2 collective-permute-start.2
  3.9 0.0 collective-permute-done
  3.9 1.8 %collective-permute-start.1 = (bf16[128,1120]{0,1:T(8,128)(2,1)}, bf16[128,1120]{0,1:T(8,128)(2,1)S(1)}, u32[]{:S(2)}, u32[]{:S(2)}) collective-permute-start(bf16[128,1120]{0,1:T(8,128)(2,1)} %param.15), channel_id=1, source_target_pairs={{0,8},{4,12},{8,0},{12,4},{1,9},{5,13},{9,1},{13,5},{2,10},{6,14},... | collective-permute-start | bytes 860168 | tf_op jit(solution)/shard_map/ppermute | solution.py:20
  5.6 2.3 %copy-done = bf16[1728,1280]{1,0:T(8,128)(2,1)S(1)} copy-done((bf16[1728,1280]{1,0:T(8,128)(2,1)S(1)}, bf16[1728,1280]{1,0:T(8,128)(2,1)}, u32[]{:S(2)}) %copy-start) | copy-done | bytes 4423704
  7.9 1.0 copy-done.2
  8.9 2.8 %project_early.2.refs_3_ = bf16[256,1280]{1,0:T(8,128)(2,1)S(1)} custom-call(bf16[1728,128]{1,0:T(8,128)(2,1)S(1)} %bitcast.19, bf16[1728,128]{1,0:T(8,128)(2,1)S(1)} %bitcast.22, bf16[1728,1280]{1,0:T(8,128)(2,1)S(1)} %copy-done), custom_call_target="tpu_custom_call" | custom-call | tf_op jit(solution)/shard_map/project_early/pallas_call | solution.py:143
  11.7 3.3 %collective-permute-done.3 = bf16[128,1728]{0,1:T(8,128)(2,1)S(1)} collective-permute-done((bf16[128,1728]{0,1:T(8,128)(2,1)}, bf16[128,1728]{0,1:T(8,128)(2,1)S(1)}, u32[]{:S(2)}, u32[]{:S(2)}) %collective-permute-start.3) | collective-permute-done | bytes 442400 | tf_op jit(solution)/shard_map/ppermute | solution.py:20
  14.9 0.0 collective-permute-start.5
  14.9 0.0 collective-permute-done.2
  15.0 0.0 copy-start.8
  15.0 0.9 copy-done.8
  15.9 1.4 %project_early.3.refs_3_ = bf16[256,384]{1,0:T(8,128)(2,1)S(1)} custom-call(bf16[1120,128]{1,0:T(8,128)(2,1)S(1)} %bitcast.44, bf16[1120,128]{1,0:T(8,128)(2,1)S(1)} %bitcast.47, bf16[1120,384]{1,0:T(8,128)(2,1)S(1)} %copy-done.4), custom_call_target="tpu_custom_call" | custom-call | tf_op jit(solution)/shard_map/project_early/pallas_call | solution.py:143
  17.3 3.5 %collective-permute-done.1 = bf16[128,1120]{0,1:T(8,128)(2,1)S(1)} collective-permute-done((bf16[128,1120]{0,1:T(8,128)(2,1)}, bf16[128,1120]{0,1:T(8,128)(2,1)S(1)}, u32[]{:S(2)}, u32[]{:S(2)}) %collective-permute-start.1) | collective-permute-done | bytes 286752 | tf_op jit(solution)/shard_map/ppermute | solution.py:20
  20.8 0.0 collective-permute-start.4
  20.8 1.8 %collective-permute-start.9 = (bf16[128,1728]{0,1:T(8,128)(2,1)S(1)}, bf16[128,1728]{0,1:T(8,128)(2,1)S(1)}, u32[]{:S(2)}, u32[]{:S(2)}) collective-permute-start(bf16[128,1728]{0,1:T(8,128)(2,1)S(1)} %copy-done.3), channel_id=1, source_target_pairs={{0,16},{16,0},{1,17},{17,1},{2,18},{18,2},{3,19},{19,3},{4,20},{20... | collective-permute-start | bytes 1327112 | tf_op jit(solution)/shard_map/ppermute | solution.py:20
  22.6 3.5 %project.2 = (bf16[128,1664]{1,0:T(8,128)(2,1)S(1)}, bf16[128,1664]{1,0:T(8,128)(2,1)S(1)}, bf16[128,1664]{1,0:T(8,128)(2,1)S(1)}, bf16[128,1664]{1,0:T(8,128)(2,1)S(1)}) custom-call(bf16[1728,128]{1,0:T(8,128)(2,1)S(1)} %bitcast.25, bf16[1728,128]{1,0:T(8,128)(2,1)S(1)} %bitcast.28, bf16[1728,1280]{1,0:T(8,128)(2,1)S(1)} %copy-done.1, ...), custom_call_target="tpu_custom_call" | custom-call | tf_op jit(solution)/shard_map/project/pallas_call | solution.py:164
  26.2 0.0 copy-start.6
  26.2 0.0 copy-start.7
  26.2 0.0 copy-start.10
  26.2 0.0 copy-start.11
  26.2 0.0 copy-start.12
  26.2 0.0 copy-start.13
  26.3 0.0 collective-permute-done.4
  26.3 1.5 %project.3 = (bf16[128,1664]{1,0:T(8,128)(2,1)S(1)}, bf16[128,1664]{1,0:T(8,128)(2,1)S(1)}, bf16[128,1664]{1,0:T(8,128)(2,1)S(1)}, bf16[128,1664]{1,0:T(8,128)(2,1)S(1)}) custom-call(bf16[1120,128]{1,0:T(8,128)(2,1)S(1)} %bitcast.45, bf16[1120,128]{1,0:T(8,128)(2,1)S(1)} %bitcast.46, ...), custom_call_target="tpu_custom_call", output_to_operand_aliasing={{0}: (4, {}), {1}: (5, {}), {2}: (6, {}), {3}: (7, {})} | custom-call | tf_op jit(solution)/shard_map/project/pallas_call | solution.py:164
  27.8 1.6 %collective-permute-start.7 = (bf16[128,1664]{1,0:T(8,128)(2,1)S(1)}, bf16[128,1664]{1,0:T(8,128)(2,1)S(1)}, u32[]{:S(2)}, u32[]{:S(2)}) collective-permute-start(bf16[128,1664]{1,0:T(8,128)(2,1)S(1)} %get-tuple-element.61), channel_id=1, source_target_pairs={{0,1},{1,0},{2,3},{3,2},{4,5},{5,4},{6,7},{7,6},{8,9},{9,8},{10,11... | collective-permute-start | bytes 1277960 | tf_op jit(solution)/shard_map/ppermute | solution.py:20
  29.4 4.0 %collective-permute-done.9 = bf16[128,1728]{0,1:T(8,128)(2,1)S(1)} collective-permute-done((bf16[128,1728]{0,1:T(8,128)(2,1)S(1)}, bf16[128,1728]{0,1:T(8,128)(2,1)S(1)}, u32[]{:S(2)}, u32[]{:S(2)}) %collective-permute-start.9) | collective-permute-done | bytes 442400 | tf_op jit(solution)/shard_map/ppermute | solution.py:20
  33.5 1.7 %collective-permute-start.10 = (bf16[128,1728]{0,1:T(8,128)(2,1)S(1)}, bf16[128,1728]{0,1:T(8,128)(2,1)S(1)}, u32[]{:S(2)}, u32[]{:S(2)}) collective-permute-start(bf16[128,1728]{0,1:T(8,128)(2,1)S(1)} %collective-permute-done.9), channel_id=1, source_target_pairs={{0,8},{4,12},{8,0},{12,4},{1,9},{5,13},{9,1},{13,5},{2,10},{6,14},... | collective-permute-start | bytes 1327112 | tf_op jit(solution)/shard_map/ppermute | solution.py:20
  35.2 1.6 %collective-permute-start.6 = (bf16[128,1664]{1,0:T(8,128)(2,1)S(1)}, bf16[128,1664]{1,0:T(8,128)(2,1)S(1)}, u32[]{:S(2)}, u32[]{:S(2)}) collective-permute-start(bf16[128,1664]{1,0:T(8,128)(2,1)S(1)} %get-tuple-element.59), channel_id=1, source_target_pairs={{0,1},{1,0},{2,3},{3,2},{4,5},{5,4},{6,7},{7,6},{8,9},{9,8},{10,11... | collective-permute-start | bytes 1277960 | tf_op jit(solution)/shard_map/ppermute | solution.py:20
  36.8 3.8 %collective-permute-done.7.right = bf16[128,1664]{1,0:T(8,128)(2,1)S(1)} collective-permute-done((bf16[128,1664]{1,0:T(8,128)(2,1)S(1)}, bf16[128,1664]{1,0:T(8,128)(2,1)S(1)}, u32[]{:S(2)}, u32[]{:S(2)}) %collective-permute-start.7) | collective-permute-done | bytes 426016 | tf_op jit(solution)/shard_map/ppermute | solution.py:20
  40.5 0.1 add.1
  40.6 2.7 %collective-permute-start.8 = (bf16[128,1664]{1,0:T(8,128)(2,1)S(1)}, bf16[128,1664]{1,0:T(8,128)(2,1)S(1)}, u32[]{:S(2)}, u32[]{:S(2)}) collective-permute-start(bf16[128,1664]{1,0:T(8,128)(2,1)S(1)} %add.1), channel_id=1, source_target_pairs={{0,2},{1,3},{2,0},{3,1},{4,6},{5,7},{6,4},{7,5},{8,10},{9,11},{10,... | collective-permute-start | bytes 1277960 | tf_op jit(solution)/shard_map/ppermute | solution.py:20
  44.6 0.6 collective-permute-start.11
  45.2 3.3 %collective-permute-done.11.refs_2_ = s32[1]{0:T(128)} collective-permute-done((s32[1]{0:T(128)}, s32[1]{0:T(128)}, u32[]{:S(2)}, u32[]{:S(2)}) %collective-permute-start.11) | collective-permute-done | bytes 36 | tf_op jit(solution)/shard_map/ppermute | solution.py:20
  48.4 0.6 lookup.1
  49.1 8.0 %collective-permute-done.6.refs_1_ = bf16[128,1664]{1,0:T(8,128)(2,1)S(1)} collective-permute-done((bf16[128,1664]{1,0:T(8,128)(2,1)S(1)}, bf16[128,1664]{1,0:T(8,128)(2,1)S(1)}, u32[]{:S(2)}, u32[]{:S(2)}) %collective-permute-start.6) | collective-permute-done | bytes 426016 | tf_op jit(solution)/shard_map/ppermute | solution.py:20
  57.1 0.0 collective-permute-done.10
  57.1 4.1 %collective-permute-done.8.refs_2_ = bf16[128,1664]{1,0:T(8,128)(2,1)S(1)} collective-permute-done((bf16[128,1664]{1,0:T(8,128)(2,1)S(1)}, bf16[128,1664]{1,0:T(8,128)(2,1)S(1)}, u32[]{:S(2)}, u32[]{:S(2)}) %collective-permute-start.8) | collective-permute-done | bytes 426016 | tf_op jit(solution)/shard_map/ppermute | solution.py:20
  61.2 1.4 %local_stats.1 = (f32[128,1280]{1,0:T(8,128)S(1)}, f32[128,1280]{1,0:T(8,128)S(1)}, f32[128,384]{1,0:T(8,128)S(1)}, f32[128,384]{1,0:T(8,128)S(1)}, bf16[176,128]{1,0:T(8,128)(2,1)S(1)}) custom-call(bf16[128,1664]{1,0:T(8,128)(2,1)S(1)} %get-tuple-element.69.refs_0_, bf16[128,1664]{1,0:T(8,128)(2,1)S(1)} %collective-permute-done.6.refs_1_, ...), custom_call_target="tpu_custom_call" | custom-call | tf_op jit(solution)/shard_map/local_stats/pallas_call | solution.py:340
  62.7 0.1 collective-permute-start.14
  62.7 1.6 %collective-permute-start.13 = (bf16[176,128]{1,0:T(8,128)(2,1)S(1)}, bf16[176,128]{1,0:T(8,128)(2,1)S(1)}, u32[]{:S(2)}, u32[]{:S(2)}) collective-permute-start(bf16[176,128]{1,0:T(8,128)(2,1)S(1)} %get-tuple-element.74.refs_0_), channel_id=1, source_target_pairs={{0,8},{4,12},{8,0},{12,4},{1,9},{5,13},{9,1},{13,5},{2,10},{6,14},... | collective-permute-start | bytes 135176 | tf_op jit(solution)/shard_map/ppermute | solution.py:20
  64.3 0.3 collective-permute-start.12
  64.6 2.0 %collective-permute-done.14.refs_3_ = bf16[176,128]{1,0:T(8,128)(2,1)S(1)} collective-permute-done((bf16[176,128]{1,0:T(8,128)(2,1)S(1)}, bf16[176,128]{1,0:T(8,128)(2,1)S(1)}, u32[]{:S(2)}, u32[]{:S(2)}) %collective-permute-start.14) | collective-permute-done | bytes 45088 | tf_op jit(solution)/shard_map/ppermute | solution.py:20
  66.6 0.7 collective-permute-done.13.refs_2_
  67.3 0.0 collective-permute-done.12.refs_1_
  67.4 1.9 %whole_norm.1 = (bf16[136,1280]{1,0:T(8,128)(2,1)S(1)}, bf16[128,1280]{1,0:T(8,128)(2,1)}, bf16[128,384]{1,0:T(8,128)(2,1)}, f32[64,128]{1,0:T(8,128)}) custom-call(bf16[176,128]{1,0:T(8,128)(2,1)S(1)} %get-tuple-element.74.refs_0_, bf16[176,128]{1,0:T(8,128)(2,1)S(1)} %collective-permute-done.12.refs_1_, ...), custom_call_target="tpu_custom_call" | custom-call | tf_op jit(solution)/shard_map/whole_norm/pallas_call | solution.py:408
  69.2 0.0 collective-permute-start.17
  69.2 0.4 collective-permute-start.16
  69.6 5.2 %collective-permute-start.15 = (bf16[136,1280]{1,0:T(8,128)(2,1)S(1)}, bf16[136,1280]{1,0:T(8,128)(2,1)S(1)}, u32[]{:S(2)}, u32[]{:S(2)}) collective-permute-start(bf16[136,1280]{1,0:T(8,128)(2,1)S(1)} %get-tuple-element.82.refs_4_), channel_id=1, source_target_pairs={{0,17},{1,16},{2,19},{3,18},{16,1},{17,0},{18,3},{19,2},{4,21},{5,... | collective-permute-start | bytes 1044488 | tf_op jit(solution)/shard_map/ppermute | solution.py:44
  74.8 13.0 %collective-permute-done.17.refs_5_ = bf16[136,1280]{1,0:T(8,128)(2,1)S(1)} collective-permute-done((bf16[136,1280]{1,0:T(8,128)(2,1)S(1)}, bf16[136,1280]{1,0:T(8,128)(2,1)S(1)}, u32[]{:S(2)}, u32[]{:S(2)}) %collective-permute-start.17) | collective-permute-done | bytes 348192 | tf_op jit(solution)/shard_map/ppermute | solution.py:20
  87.8 1.2 %collective-permute-done.15.refs_13_ = bf16[136,1280]{1,0:T(8,128)(2,1)S(1)} collective-permute-done((bf16[136,1280]{1,0:T(8,128)(2,1)S(1)}, bf16[136,1280]{1,0:T(8,128)(2,1)S(1)}, u32[]{:S(2)}, u32[]{:S(2)}) %collective-permute-start.15) | collective-permute-done | bytes 348192 | tf_op jit(solution)/shard_map/ppermute | solution.py:44
  89.1 0.6 collective-permute-start.22
  89.7 1.6 %collective-permute-start.21 = (bf16[136,1280]{1,0:T(8,128)(2,1)S(1)}, bf16[136,1280]{1,0:T(8,128)(2,1)S(1)}, u32[]{:S(2)}, u32[]{:S(2)}) collective-permute-start(bf16[136,1280]{1,0:T(8,128)(2,1)S(1)} %collective-permute-done.17.refs_5_), channel_id=1, source_target_pairs={{0,1},{1,0},{2,3},{3,2},{4,5},{5,4},{6,7},{7,6},{8,9},{9,8},{10,11... | collective-permute-start | bytes 1044488 | tf_op jit(solution)/shard_map/ppermute | solution.py:20
  91.2 0.0 collective-permute-start.20
  91.2 0.5 collective-permute-start.19
  91.8 0.5 collective-permute-start.18
  92.2 5.9 %collective-permute-done.22.refs_14_ = bf16[136,1280]{1,0:T(8,128)(2,1)S(1)} collective-permute-done((bf16[136,1280]{1,0:T(8,128)(2,1)S(1)}, bf16[136,1280]{1,0:T(8,128)(2,1)S(1)}, u32[]{:S(2)}, u32[]{:S(2)}) %collective-permute-start.22) | collective-permute-done | bytes 348192 | tf_op jit(solution)/shard_map/ppermute | solution.py:20
  98.1 2.6 %collective-permute-done.21.refs_6_ = bf16[136,1280]{1,0:T(8,128)(2,1)S(1)} collective-permute-done((bf16[136,1280]{1,0:T(8,128)(2,1)S(1)}, bf16[136,1280]{1,0:T(8,128)(2,1)S(1)}, u32[]{:S(2)}, u32[]{:S(2)}) %collective-permute-start.21) | collective-permute-done | bytes 348192 | tf_op jit(solution)/shard_map/ppermute | solution.py:20
  100.8 1.4 %collective-permute-start.23 = (bf16[136,1280]{1,0:T(8,128)(2,1)S(1)}, bf16[136,1280]{1,0:T(8,128)(2,1)S(1)}, u32[]{:S(2)}, u32[]{:S(2)}) collective-permute-start(bf16[136,1280]{1,0:T(8,128)(2,1)S(1)} %collective-permute-done.21.refs_6_), channel_id=1, source_target_pairs={{0,16},{16,0},{1,17},{17,1},{2,18},{18,2},{3,19},{19,3},{4,20},{20... | collective-permute-start | bytes 1044488 | tf_op jit(solution)/shard_map/ppermute | solution.py:20
  102.2 0.0 collective-permute-done.20
  102.2 0.0 collective-permute-done.19
  102.2 7.6 %contract.2 = (bf16[1728,1280]{1,0:T(8,128)(2,1)S(1)}, f32[64,1280]{1,0:T(8,128)S(1)}) custom-call(bf16[1728,128]{1,0:T(8,128)(2,1)S(1)} %bitcast.20, bf16[1728,128]{1,0:T(8,128)(2,1)S(1)} %bitcast.23, bf16[1728,128]{1,0:T(8,128)(2,1)S(1)} %bitcast.26, bf16[1728,128]{1,0:T(8,128)(2,1)S(1)} %bitcast.29, bf16[136,1280]{1,0:T(8,128)(2,1)S(1)} %get-tuple-element.82.refs_4_, ...), custom_call_target="tpu_custom_call" | custom-call | tf_op jit(solution)/shard_map/contract/pallas_call | solution.py:256
  109.8 4.6 %contract.3 = (bf16[1728,1280]{1,0:T(8,128)(2,1)}, f32[64,1280]{1,0:T(8,128)}) custom-call(bf16[1728,128]{1,0:T(8,128)(2,1)S(1)} %bitcast.21, bf16[1728,128]{1,0:T(8,128)(2,1)S(1)} %bitcast.24, bf16[1728,128]{1,0:T(8,128)(2,1)S(1)} %bitcast.27, bf16[1728,128]{1,0:T(8,128)(2,1)S(1)} %bitcast.30, bf16[136,1280]{1,0:T(8,128)(2,1)S(1)} %collective-permute-done.18.refs_4_, ...), custom_call_target="tpu_custom_call" | custom-call | tf_op jit(solution)/shard_map/contract/pallas_call | solution.py:256
  (22 shorter events, 0.0 us)
Async XLA Ops:
  0.6 3.3 %collective-permute-start = (bf16[128,1728]{0,1:T(8,128)(2,1)}, bf16[128,1728]{0,1:T(8,128)(2,1)S(1)}, u32[]{:S(2)}, u32[]{:S(2)}) collective-permute-start(bf16[128,1728]{0,1:T(8,128)(2,1)} %param.14), channel_id=1, source_target_pairs={{0,4},{4,0},{8,12},{12,8},{1,5},{5,1},{9,13},{13,9},{2,6},{6,2},{1... | collective-permute-start | bytes 1327112 | tf_op jit(solution)/shard_map/ppermute | solution.py:20
  1.1 13.8 %collective-permute-start.3 = (bf16[128,1728]{0,1:T(8,128)(2,1)}, bf16[128,1728]{0,1:T(8,128)(2,1)S(1)}, u32[]{:S(2)}, u32[]{:S(2)}) collective-permute-start(bf16[128,1728]{0,1:T(8,128)(2,1)} %param.14), channel_id=1, source_target_pairs={{0,8},{4,12},{8,0},{12,4},{1,9},{5,13},{9,1},{13,5},{2,10},{6,14},... | collective-permute-start | bytes 1327112 | tf_op jit(solution)/shard_map/ppermute | solution.py:20
  3.7 11.2 %collective-permute-start.2 = (bf16[128,1120]{0,1:T(8,128)(2,1)}, bf16[128,1120]{0,1:T(8,128)(2,1)S(1)}, u32[]{:S(2)}, u32[]{:S(2)}) collective-permute-start(bf16[128,1120]{0,1:T(8,128)(2,1)} %param.15), channel_id=1, source_target_pairs={{0,4},{4,0},{8,12},{12,8},{1,5},{5,1},{9,13},{13,9},{2,6},{6,2},{1... | collective-permute-start | bytes 860168 | tf_op jit(solution)/shard_map/ppermute | solution.py:20
  3.9 16.9 %collective-permute-start.1 = (bf16[128,1120]{0,1:T(8,128)(2,1)}, bf16[128,1120]{0,1:T(8,128)(2,1)S(1)}, u32[]{:S(2)}, u32[]{:S(2)}) collective-permute-start(bf16[128,1120]{0,1:T(8,128)(2,1)} %param.15), channel_id=1, source_target_pairs={{0,8},{4,12},{8,0},{12,4},{1,9},{5,13},{9,1},{13,5},{2,10},{6,14},... | collective-permute-start | bytes 860168 | tf_op jit(solution)/shard_map/ppermute | solution.py:20
  5.6 2.3 %copy-start = (bf16[1728,1280]{1,0:T(8,128)(2,1)S(1)}, bf16[1728,1280]{1,0:T(8,128)(2,1)}, u32[]{:S(2)}) copy-start(bf16[1728,1280]{1,0:T(8,128)(2,1)} %refs_2_.6) | copy-start | bytes 13271044
  7.9 1.0 copy-start.2
  8.9 6.0 %copy-start.4 = (bf16[1120,384]{1,0:T(8,128)(2,1)S(1)}, bf16[1120,384]{1,0:T(8,128)(2,1)}, u32[]{:S(2)}) copy-start(bf16[1120,384]{1,0:T(8,128)(2,1)} %refs_2_.7) | copy-start | bytes 2580484
  8.9 11.9 %copy-start.3 = (bf16[128,1728]{0,1:T(8,128)(2,1)S(1)}, bf16[128,1728]{0,1:T(8,128)(2,1)}, u32[]{:S(2)}) copy-start(bf16[128,1728]{0,1:T(8,128)(2,1)} %param.14) | copy-start | bytes 1327108
  8.9 13.7 %copy-start.1 = (bf16[1728,1280]{1,0:T(8,128)(2,1)S(1)}, bf16[1728,1280]{1,0:T(8,128)(2,1)}, u32[]{:S(2)}) copy-start(bf16[1728,1280]{1,0:T(8,128)(2,1)} %refs_2_.6) | copy-start | bytes 13271044
  14.9 7.7 %collective-permute-start.5 = (bf16[128,1728]{0,1:T(8,128)(2,1)S(1)}, bf16[128,1728]{0,1:T(8,128)(2,1)S(1)}, u32[]{:S(2)}, u32[]{:S(2)}) collective-permute-start(bf16[128,1728]{0,1:T(8,128)(2,1)S(1)} %collective-permute-done.3), channel_id=1, source_target_pairs={{0,4},{4,0},{8,12},{12,8},{1,5},{5,1},{9,13},{13,9},{2,6},{6,2},{1... | collective-permute-start | bytes 1327112 | tf_op jit(solution)/shard_map/ppermute | solution.py:20
  15.0 1.0 copy-start.8
  20.8 5.4 %collective-permute-start.4 = (bf16[128,1120]{0,1:T(8,128)(2,1)S(1)}, bf16[128,1120]{0,1:T(8,128)(2,1)S(1)}, u32[]{:S(2)}, u32[]{:S(2)}) collective-permute-start(bf16[128,1120]{0,1:T(8,128)(2,1)S(1)} %collective-permute-done.1), channel_id=1, source_target_pairs={{0,4},{4,0},{8,12},{12,8},{1,5},{5,1},{9,13},{13,9},{2,6},{6,2},{1... | collective-permute-start | bytes 860168 | tf_op jit(solution)/shard_map/ppermute | solution.py:20
  20.8 12.6 %collective-permute-start.9 = (bf16[128,1728]{0,1:T(8,128)(2,1)S(1)}, bf16[128,1728]{0,1:T(8,128)(2,1)S(1)}, u32[]{:S(2)}, u32[]{:S(2)}) collective-permute-start(bf16[128,1728]{0,1:T(8,128)(2,1)S(1)} %copy-done.3), channel_id=1, source_target_pairs={{0,16},{16,0},{1,17},{17,1},{2,18},{18,2},{3,19},{19,3},{4,20},{20... | collective-permute-start | bytes 1327112 | tf_op jit(solution)/shard_map/ppermute | solution.py:20
  22.6 25.8 %copy-start.5 = (f32[50,3,1280]{2,0,1:T(8,128)S(1)}, f32[50,3,1280]{2,0,1:T(8,128)}, u32[]{:S(2)}) copy-start(f32[50,3,1280]{2,0,1:T(8,128)} %param.23) | copy-start | bytes 2304004
  22.6 25.8 %copy-start.9 = (f32[50,3,384]{2,0,1:T(8,128)S(1)}, f32[50,3,384]{2,0,1:T(8,128)}, u32[]{:S(2)}) copy-start(f32[50,3,384]{2,0,1:T(8,128)} %param.24) | copy-start | bytes 691204
  26.2 35.0 %copy-start.6 = (bf16[1280,64]{0,1:T(8,128)(2,1)S(1)}, bf16[1280,64]{0,1:T(8,128)(2,1)}, u32[]{:S(2)}) copy-start(bf16[1280,64]{0,1:T(8,128)(2,1)} %param.21) | copy-start | bytes 491524
  26.2 35.0 %copy-start.7 = (bf16[128,1280]{1,0:T(8,128)(2,1)S(1)}, bf16[128,1280]{1,0:T(8,128)(2,1)}, u32[]{:S(2)}) copy-start(bf16[128,1280]{1,0:T(8,128)(2,1)} %refs_3_.1) | copy-start | bytes 983044
  26.2 35.0 %copy-start.10 = (f32[128,64]{0,1:T(8,128)S(1)}, f32[128,64]{0,1:T(8,128)}, u32[]{:S(2)}) copy-start(f32[128,64]{0,1:T(8,128)} %param.18) | copy-start | bytes 98308
  26.2 35.0 %copy-start.11 = (bf16[128,384]{1,0:T(8,128)(2,1)S(1)}, bf16[128,384]{1,0:T(8,128)(2,1)}, u32[]{:S(2)}) copy-start(bf16[128,384]{1,0:T(8,128)(2,1)} %refs_6_.1) | copy-start | bytes 294916
  26.2 35.0 %copy-start.12 = (bf16[384,64]{0,1:T(8,128)(2,1)S(1)}, bf16[384,64]{0,1:T(8,128)(2,1)}, u32[]{:S(2)}) copy-start(bf16[384,64]{0,1:T(8,128)(2,1)} %param.22) | copy-start | bytes 147460
  26.2 35.0 %copy-start.13 = (f32[8]{0:T(128)S(1)}, f32[8]{0:T(128)}, u32[]{:S(2)}) copy-start(f32[8]{0:T(128)} %refs_9_.1) | copy-start | bytes 100
  27.8 12.7 %collective-permute-start.7 = (bf16[128,1664]{1,0:T(8,128)(2,1)S(1)}, bf16[128,1664]{1,0:T(8,128)(2,1)S(1)}, u32[]{:S(2)}, u32[]{:S(2)}) collective-permute-start(bf16[128,1664]{1,0:T(8,128)(2,1)S(1)} %get-tuple-element.61), channel_id=1, source_target_pairs={{0,1},{1,0},{2,3},{3,2},{4,5},{5,4},{6,7},{7,6},{8,9},{9,8},{10,11... | collective-permute-start | bytes 1277960 | tf_op jit(solution)/shard_map/ppermute | solution.py:20
  33.5 23.6 %collective-permute-start.10 = (bf16[128,1728]{0,1:T(8,128)(2,1)S(1)}, bf16[128,1728]{0,1:T(8,128)(2,1)S(1)}, u32[]{:S(2)}, u32[]{:S(2)}) collective-permute-start(bf16[128,1728]{0,1:T(8,128)(2,1)S(1)} %collective-permute-done.9), channel_id=1, source_target_pairs={{0,8},{4,12},{8,0},{12,4},{1,9},{5,13},{9,1},{13,5},{2,10},{6,14},... | collective-permute-start | bytes 1327112 | tf_op jit(solution)/shard_map/ppermute | solution.py:20
  35.2 21.9 %collective-permute-start.6 = (bf16[128,1664]{1,0:T(8,128)(2,1)S(1)}, bf16[128,1664]{1,0:T(8,128)(2,1)S(1)}, u32[]{:S(2)}, u32[]{:S(2)}) collective-permute-start(bf16[128,1664]{1,0:T(8,128)(2,1)S(1)} %get-tuple-element.59), channel_id=1, source_target_pairs={{0,1},{1,0},{2,3},{3,2},{4,5},{5,4},{6,7},{7,6},{8,9},{9,8},{10,11... | collective-permute-start | bytes 1277960 | tf_op jit(solution)/shard_map/ppermute | solution.py:20
  40.6 20.6 %collective-permute-start.8 = (bf16[128,1664]{1,0:T(8,128)(2,1)S(1)}, bf16[128,1664]{1,0:T(8,128)(2,1)S(1)}, u32[]{:S(2)}, u32[]{:S(2)}) collective-permute-start(bf16[128,1664]{1,0:T(8,128)(2,1)S(1)} %add.1), channel_id=1, source_target_pairs={{0,2},{1,3},{2,0},{3,1},{4,6},{5,7},{6,4},{7,5},{8,10},{9,11},{10,... | collective-permute-start | bytes 1277960 | tf_op jit(solution)/shard_map/ppermute | solution.py:20
  44.6 3.8 %collective-permute-start.11 = (s32[1]{0:T(128)}, s32[1]{0:T(128)}, u32[]{:S(2)}, u32[]{:S(2)}) collective-permute-start(s32[1]{0:T(128)} %param.26), channel_id=1, source_target_pairs={{0,16},{16,0},{1,17},{17,1},{2,18},{18,2},{3,19},{19,3},{4,20},{20... | collective-permute-start | bytes 20 | tf_op jit(solution)/shard_map/ppermute | solution.py:20
  62.7 4.0 %collective-permute-start.14 = (bf16[176,128]{1,0:T(8,128)(2,1)S(1)}, bf16[176,128]{1,0:T(8,128)(2,1)S(1)}, u32[]{:S(2)}, u32[]{:S(2)}) collective-permute-start(bf16[176,128]{1,0:T(8,128)(2,1)S(1)} %get-tuple-element.74.refs_0_), channel_id=1, source_target_pairs={{0,12},{4,8},{8,4},{12,0},{1,13},{5,9},{9,5},{13,1},{2,14},{6,10},... | collective-permute-start | bytes 135176 | tf_op jit(solution)/shard_map/ppermute | solution.py:20
  62.7 4.6 %collective-permute-start.13 = (bf16[176,128]{1,0:T(8,128)(2,1)S(1)}, bf16[176,128]{1,0:T(8,128)(2,1)S(1)}, u32[]{:S(2)}, u32[]{:S(2)}) collective-permute-start(bf16[176,128]{1,0:T(8,128)(2,1)S(1)} %get-tuple-element.74.refs_0_), channel_id=1, source_target_pairs={{0,8},{4,12},{8,0},{12,4},{1,9},{5,13},{9,1},{13,5},{2,10},{6,14},... | collective-permute-start | bytes 135176 | tf_op jit(solution)/shard_map/ppermute | solution.py:20
  64.3 3.0 %collective-permute-start.12 = (bf16[176,128]{1,0:T(8,128)(2,1)S(1)}, bf16[176,128]{1,0:T(8,128)(2,1)S(1)}, u32[]{:S(2)}, u32[]{:S(2)}) collective-permute-start(bf16[176,128]{1,0:T(8,128)(2,1)S(1)} %get-tuple-element.74.refs_0_), channel_id=1, source_target_pairs={{0,4},{4,0},{8,12},{12,8},{1,5},{5,1},{9,13},{13,9},{2,6},{6,2},{1... | collective-permute-start | bytes 135176 | tf_op jit(solution)/shard_map/ppermute | solution.py:20
  69.2 18.6 %collective-permute-start.17 = (bf16[136,1280]{1,0:T(8,128)(2,1)S(1)}, bf16[136,1280]{1,0:T(8,128)(2,1)S(1)}, u32[]{:S(2)}, u32[]{:S(2)}) collective-permute-start(bf16[136,1280]{1,0:T(8,128)(2,1)S(1)} %get-tuple-element.82.refs_4_), channel_id=1, source_target_pairs={{0,2},{1,3},{2,0},{3,1},{4,6},{5,7},{6,4},{7,5},{8,10},{9,11},{10,... | collective-permute-start | bytes 1044488 | tf_op jit(solution)/shard_map/ppermute | solution.py:20
  69.2 18.6 %collective-permute-start.16 = (bf16[136,1280]{1,0:T(8,128)(2,1)S(1)}, bf16[136,1280]{1,0:T(8,128)(2,1)S(1)}, u32[]{:S(2)}, u32[]{:S(2)}) collective-permute-start(bf16[136,1280]{1,0:T(8,128)(2,1)S(1)} %get-tuple-element.82.refs_4_), channel_id=1, source_target_pairs={{0,16},{16,0},{1,17},{17,1},{2,18},{18,2},{3,19},{19,3},{4,20},{20... | collective-permute-start | bytes 1044488 | tf_op jit(solution)/shard_map/ppermute | solution.py:20
  69.6 19.5 %collective-permute-start.15 = (bf16[136,1280]{1,0:T(8,128)(2,1)S(1)}, bf16[136,1280]{1,0:T(8,128)(2,1)S(1)}, u32[]{:S(2)}, u32[]{:S(2)}) collective-permute-start(bf16[136,1280]{1,0:T(8,128)(2,1)S(1)} %get-tuple-element.82.refs_4_), channel_id=1, source_target_pairs={{0,17},{1,16},{2,19},{3,18},{16,1},{17,0},{18,3},{19,2},{4,21},{5,... | collective-permute-start | bytes 1044488 | tf_op jit(solution)/shard_map/ppermute | solution.py:44
  89.1 9.1 %collective-permute-start.22 = (bf16[136,1280]{1,0:T(8,128)(2,1)S(1)}, bf16[136,1280]{1,0:T(8,128)(2,1)S(1)}, u32[]{:S(2)}, u32[]{:S(2)}) collective-permute-start(bf16[136,1280]{1,0:T(8,128)(2,1)S(1)} %collective-permute-done.17.refs_5_), channel_id=1, source_target_pairs={{0,16},{16,0},{1,17},{17,1},{2,18},{18,2},{3,19},{19,3},{4,20},{20... | collective-permute-start | bytes 1044488 | tf_op jit(solution)/shard_map/ppermute | solution.py:20
  89.7 11.1 %collective-permute-start.21 = (bf16[136,1280]{1,0:T(8,128)(2,1)S(1)}, bf16[136,1280]{1,0:T(8,128)(2,1)S(1)}, u32[]{:S(2)}, u32[]{:S(2)}) collective-permute-start(bf16[136,1280]{1,0:T(8,128)(2,1)S(1)} %collective-permute-done.17.refs_5_), channel_id=1, source_target_pairs={{0,1},{1,0},{2,3},{3,2},{4,5},{5,4},{6,7},{7,6},{8,9},{9,8},{10,11... | collective-permute-start | bytes 1044488 | tf_op jit(solution)/shard_map/ppermute | solution.py:20
  91.2 11.0 %collective-permute-start.20 = (bf16[128,1728]{0,1:T(8,128)(2,1)S(1)}, bf16[128,1728]{0,1:T(8,128)(2,1)S(1)}, u32[]{:S(2)}, u32[]{:S(2)}) collective-permute-start(bf16[128,1728]{0,1:T(8,128)(2,1)S(1)} %collective-permute-done.10), channel_id=1, source_target_pairs={{0,4},{4,0},{8,12},{12,8},{1,5},{5,1},{9,13},{13,9},{2,6},{6,2},{1... | collective-permute-start | bytes 1327112 | tf_op jit(solution)/shard_map/ppermute | solution.py:20
  91.2 11.0 %collective-permute-start.19 = (bf16[128,1728]{0,1:T(8,128)(2,1)S(1)}, bf16[128,1728]{0,1:T(8,128)(2,1)S(1)}, u32[]{:S(2)}, u32[]{:S(2)}) collective-permute-start(bf16[128,1728]{0,1:T(8,128)(2,1)S(1)} %collective-permute-done.9), channel_id=1, source_target_pairs={{0,4},{4,0},{8,12},{12,8},{1,5},{5,1},{9,13},{13,9},{2,6},{6,2},{1... | collective-permute-start | bytes 1327112 | tf_op jit(solution)/shard_map/ppermute | solution.py:20
  91.8 18.1 %collective-permute-start.18 = (bf16[136,1280]{1,0:T(8,128)(2,1)S(1)}, bf16[136,1280]{1,0:T(8,128)(2,1)S(1)}, u32[]{:S(2)}, u32[]{:S(2)}) collective-permute-start(bf16[136,1280]{1,0:T(8,128)(2,1)S(1)} %get-tuple-element.82.refs_4_), channel_id=1, source_target_pairs={{0,1},{1,0},{2,3},{3,2},{4,5},{5,4},{6,7},{7,6},{8,9},{9,8},{10,11... | collective-permute-start | bytes 1044488 | tf_op jit(solution)/shard_map/ppermute | solution.py:20
  100.8 9.1 %collective-permute-start.23 = (bf16[136,1280]{1,0:T(8,128)(2,1)S(1)}, bf16[136,1280]{1,0:T(8,128)(2,1)S(1)}, u32[]{:S(2)}, u32[]{:S(2)}) collective-permute-start(bf16[136,1280]{1,0:T(8,128)(2,1)S(1)} %collective-permute-done.21.refs_6_), channel_id=1, source_target_pairs={{0,16},{16,0},{1,17},{17,1},{2,18},{18,2},{3,19},{19,3},{4,20},{20... | collective-permute-start | bytes 1044488 | tf_op jit(solution)/shard_map/ppermute | solution.py:20

commit v2 on v1

--- a/solution.py
+++ b/solution.py
@@ -37,18 +37,18 @@
     return lax.optimization_barrier((x, others))[0]
 
 
-def gather_pairs(block):
+def gather_pairs(block, meanwhile):
     pairs = [(4 * g + t, 4 * (1 - g) + (t ^ 1)) for g in range(2) for t in range(4)]
     two = swap(block, "tp", 4, 2)
     across = swap(block, "grp", 2, 1)
     across_one = lax.ppermute(block, ("grp", "tp"), pairs)
-    two = lax.optimization_barrier((across_one, across, two))[2]
+    two, meanwhile = lax.optimization_barrier((across_one, across, two, meanwhile))[2:]
     three = swap(two, "tp", 4, 1)
     across_two = swap(two, "grp", 2, 1)
     three = after(three, across_two)
     across_three = swap(three, "grp", 2, 1)
     one = swap(after(block, two), "tp", 4, 1)
-    return [block, one, two, three], [across, across_one, across_two, across_three]
+    return [block, one, two, three], [across, across_one, across_two, across_three], meanwhile
 
 
 def add_kernel(left, right, out):
@@ -187,20 +187,13 @@
     samples = [(take(n), take(len(slots)), *take(1)) for slots in counts]
     (head,) = take(1)
     before = take(2) if more else None
-    out, head_out, signal, shelf, done = refs
-    patch, rows, tile = head.shape[0], shelf.shape[2], out.shape[0]
+    out, head_out, signal, shelf = refs
+    patch = head.shape[0]
+    rows = shelf.shape[2]
     turn = meeting()
-    wanted = [(hidden, k) for slots, (hidden, *_) in zip(counts, samples) for k in slots]
 
     @pl.when(pl.program_id(0) == 0)
     def _():
-        for place, (hidden, k) in enumerate(wanted):
-            for j in range(n):
-
-                @pl.when(jnp.bitwise_xor(turn, k) == j)
-                def _():
-                    pltpu.make_async_copy(hidden[j], shelf.at[place], done.at[place]).start()
-
         gradient = before[1][...] if more else jnp.zeros(head_out.shape, F32)
         place = 0
         for _, sent, table in samples:
@@ -224,14 +217,16 @@
                 gradient = gradient + jnp.dot(cot, shaped, preferred_element_type=F32)
                 place += rows
         head_out[...] = gradient
-        for place, (hidden, _) in enumerate(wanted):
-            pltpu.make_async_copy(hidden[0], shelf.at[place], done.at[place]).wait()
-
-    here = pl.ds(pl.multiple_of(pl.program_id(0) * tile, tile), tile)
-    left = jnp.concatenate([shelf[place, here, :] for place in range(len(wanted))], axis=1)
+
+    left = []
+    for g, (slots, (hidden, *_)) in enumerate(zip(counts, samples)):
+        for j in range(n):
+            shelf[g * n + j] = hidden[j][...]
+        left += [shelf[g * n + jnp.bitwise_xor(turn, k)] for k in slots]
+    left = jnp.concatenate(left, axis=1)
     product = jnp.dot(left, signal[...], preferred_element_type=F32)
     if more:
-        product = product + before[0][here, :].astype(F32)
+        product = product + before[0][...].astype(F32)
     out[...] = product.astype(BF16)
 
 
@@ -244,7 +239,7 @@
     operands, in_specs = [], []
     for hidden, slots, sent, table in samples:
         operands += [block.T for block in hidden]
-        in_specs += [pl.BlockSpec(memory_space=pl.ANY) for _ in range(n)]
+        in_specs += [pl.BlockSpec((tile, tokens), lambda i: (i, 0)) for _ in range(n)]
         rest = [*(sent[k] for k in slots), table]
         operands += rest
         in_specs += [whole_block(x) for x in rest]
@@ -252,7 +247,7 @@
     in_specs.append(whole_block(head))
     if before is not None:
         operands += before
-        in_specs += [pl.BlockSpec(memory_space=pltpu.VMEM), whole_block(before[1])]
+        in_specs += [pl.BlockSpec((tile, width), lambda i: (i, 0)), whole_block(before[1])]
     return pl.pallas_call(
         functools.partial(contract_kernel, n, counts, before is not None),
         grid=(depth // tile,),
@@ -264,8 +259,7 @@
         ],
         scratch_shapes=[
             pltpu.VMEM((sum(map(len, counts)) * tokens, width), BF16),
-            pltpu.VMEM((sum(map(len, counts)), depth, tokens), BF16),
-            pltpu.SemaphoreType.DMA((sum(map(len, counts)),)),
+            pltpu.VMEM((len(samples) * n, tile, tokens), BF16),
         ],
         compiler_params=pltpu.CompilerParams(vmem_limit_bytes=VMEM),
         cost_estimate=SHORT,
@@ -348,43 +342,50 @@
     )(*arrays, *weight)
 
 
-def model_norm(parts, products, stream, scaled):
+def gathered(refs):
+    told = [ref[...].astype(F32) for ref in refs]
+    first = [t[:16] + t[16:32] + t[32:48] for t in told]
+    half = 48 + (told[0].shape[0] - 48) // 2
+    return (
+        ([f[:8] for f in first], [t[48:half] for t in told]),
+        ([f[8:] for f in first], [t[half:] for t in told]),
+    )
+
+
+def model_norm(parts, stream):
     rows, width = stream.shape
-    full, count = width * len(parts), len(parts)
-    patch = products[0].shape[0]
-    centre = sum(p[0:1] for p in parts) / count
+    full = width * len(parts)
+    centre = sum(p[0:1] for p in parts) / len(parts)
     squares = sum(p[1:2] + width * jnp.square(p[0:1] - centre) for p in parts)
     inverse = lax.rsqrt(squares / full + EPSILON)
     first = sum(p[2:3] for p in parts) / full
     second = inverse * sum(p[3:4] + (p[0:1] - centre) * p[2:3] for p in parts) / full
     sums = jnp.concatenate([inverse, first, second], axis=0)
     turned = jnp.concatenate([sums, centre, jnp.zeros((4, rows), F32)], axis=0).T
-    normed = (stream[...] - turned[:, 3:4]) * turned[:, 0:1]
+    return centre, sums, turned, (stream[...] - turned[:, 3:4]) * turned[:, 0:1]
+
+
+def model_rest(parts, products, stream, scaled):
+    centre, sums, turned, normed = model_norm(parts, stream)
     grad = turned[:, 0:1] * (scaled[...] - turned[:, 1:2] - normed * turned[:, 2:3])
+    patch, rows = products[0].shape
     lane, row = lanes((patch, rows)), lax.broadcasted_iota(jnp.int32, (patch, rows), 0)
     out, offset = 0.0, 0.0
     for p, product in zip(parts, products):
         slope = jnp.sum(jnp.where(lane == row, p[4:5], 0.0), axis=1, keepdims=True)
         offset += jnp.sum(jnp.where(lane == row + patch, p[4:5], 0.0), axis=1, keepdims=True)
         out += product + (p[0:1] - centre) * slope
-    return normed, grad, sums, inverse * out + offset
+    return grad.astype(BF16), sums[0:1] * out + offset
 
 
 def norm_kernel(n, *refs):
-    told = [ref[...].astype(F32) for ref in refs[:n]]
-    first = [t[:16] + t[16:32] + t[32:48] for t in told]
-    stream_big, scaled_big, stream_guide, scaled_guide, cot = refs[n : n + 5]
-    strength = refs[n + 5][refs[n + 6][0]]
-    sent, grad_big, grad_guide, guided = refs[n + 7 :]
-    half = 48 + (told[0].shape[0] - 48) // 2
-    normed, grad, sums, out_big = model_norm(
-        [f[:8] for f in first], [t[48:half] for t in told], stream_big, scaled_big
-    )
-    grad_big[...] = grad.astype(BF16)
+    (parts, _), _ = gathered(refs[:n])
+    stream, cot, weights, which, sent = refs[n:]
+    _, sums, _, normed = model_norm(parts, stream)
     rows, width = normed.shape
     high = sums.astype(BF16).astype(F32)
     pieces = [jnp.concatenate([high, sums - high, jnp.zeros((2, rows), F32)], axis=0)]
-    weighted = strength * cot[...]
+    weighted = weights[which[0]] * cot[...]
     pieces += [weighted[r : r + 8] for r in range(0, weighted.shape[0], 8)]
     across = width // rows
     lines = [normed]
@@ -393,30 +394,46 @@
         line += [jnp.zeros((8, width - rows * len(line)), F32)] if width > rows * len(line) else []
         lines.append(jnp.concatenate(line, axis=1))
     sent[...] = jnp.concatenate(lines, axis=0).astype(BF16)
-    _, grad, _, out_guide = model_norm(
-        [f[8:] for f in first], [t[half:] for t in told], stream_guide, scaled_guide
-    )
-    grad_guide[...] = grad.astype(BF16)
-    guided[...] = out_guide + strength * (out_big - out_guide)
-
-
-def whole_norm(told, streams, cot, weight):
+
+
+def whole_norm(told, stream, cot, weight):
     patch, rows = cot.shape
-    width_big, width_guide = streams[0].shape[1], streams[2].shape[1]
-    below = 8 * pl.cdiv(1 + patch // 8, width_big // rows)
-    arrays = [*told, *streams, cot]
+    width = stream.shape[1]
+    below = 8 * pl.cdiv(1 + patch // 8, width // rows)
+    arrays = [*told, stream, cot]
     return pl.pallas_call(
         functools.partial(norm_kernel, len(told)),
         in_specs=specs(arrays),
+        out_shape=jax.ShapeDtypeStruct((rows + below, width), BF16),
+        compiler_params=pltpu.CompilerParams(vmem_limit_bytes=VMEM_NORM),
+        cost_estimate=SHORT,
+        name="whole_norm",
+    )(*arrays, *weight)
+
+
+def rest_kernel(n, *refs):
+    big, guide = gathered(refs[:n])
+    stream_big, scaled_big, stream_guide, scaled_guide, weights, which = refs[n : n + 6]
+    grad_big, grad_guide, guided = refs[n + 6 :]
+    grad_big[...], out_big = model_rest(*big, stream_big, scaled_big)
+    grad_guide[...], out_guide = model_rest(*guide, stream_guide, scaled_guide)
+    guided[...] = out_guide + weights[which[0]] * (out_big - out_guide)
+
+
+def norm_rest(told, streams, patch, weight):
+    rows = told[0].shape[1]
+    arrays = [*told, *streams]
+    return pl.pallas_call(
+        functools.partial(rest_kernel, len(told)),
+        in_specs=specs(arrays),
         out_shape=[
-            jax.ShapeDtypeStruct((rows + below, width_big), BF16),
-            jax.ShapeDtypeStruct((rows, width_big), BF16),
-            jax.ShapeDtypeStruct((rows, width_guide), BF16),
+            jax.ShapeDtypeStruct(streams[0].shape, BF16),
+            jax.ShapeDtypeStruct(streams[2].shape, BF16),
             jax.ShapeDtypeStruct((patch, rows), F32),
         ],
         compiler_params=pltpu.CompilerParams(vmem_limit_bytes=VMEM_NORM),
         cost_estimate=SHORT,
-        name="whole_norm",
+        name="norm_rest",
     )(*arrays, *weight)
 
 
@@ -449,10 +466,11 @@
     big_blocks = near_big + far_big
     early_guide = project_early(after(near_guide, early_big), proj_guide, 128)
     far_guide = forward(far_guide, n_seq, (early_guide, far_big[0]))
-    fc_crossed = [swap(fc_big, "grp", n_grp, g) for g in range(1, n_grp)]
 
     width = width_big + width_guide
     terms = project(far_big, proj_big, tile, width, early_big)
+    fc_late = after(fc_big, terms)
+    fc_crossed = [swap(fc_late, "grp", n_grp, g) for g in range(1, n_grp)]
     terms = project(far_guide, proj_guide, 128, width, early_guide, terms)
     received, joined = scatter(terms, n_tp)
     begun = after((fc_crossed, modulation_big, modulation_guide), terms)
@@ -475,10 +493,11 @@
         received, [res_big, table_big, head_big], [res_guide, table_guide, head_guide], cot, weight
     )
     told = gather_direct(told, "seq", n_seq)
-    sent, grad_big, grad_guide, guided = whole_norm(told, streams, cot, weight)
+    sent = whole_norm(told, streams[0], cot, weight)
+    rest = norm_rest(told, streams, cot.shape[0], weight)
 
     if (n_grp, n_tp) == (2, 4):
-        sent_tp, crossed = gather_pairs(sent)
+        sent_tp, crossed, rest = gather_pairs(sent, rest)
         own = (big_blocks, (0, 2, 3), sent_tp, table_big)
         other = (fc_others[0], (0, 1, 2), crossed, tables[0])
         grads = contract([own, other], head_big)
@@ -493,11 +512,11 @@
             sample = (fc_others[g - 1], every, crossed, tables[g - 1])
             grads = contract([sample], head_big, grads)
     return (
-        guided.T,
+        rest[2].T,
         grads[0],
         grads[1].T,
-        grad_big,
-        grad_guide,
+        rest[0],
+        rest[1],
     )
 
 

time: 115 us -> 113 us (0.983)
  Pallas kernels: 25.4 us -> 24.1 us
    ppermute x23, starting transfers between devices: 21.9 us -> 24.2 us  [swap(): return lax.ppermute(x, axis, [(i, i ^ bits) for i in range(size)])]
    pallas_call x2, Pallas kernels: 12.2 us -> 10.2 us  [contract(): pl.pallas_call(functools.partial(contract_kernel, n, counts, before is no...]
    pallas_call x0 -> x1, Pallas kernels: none -> 1.82 us  [norm_rest(): pl.pallas_call(functools.partial(rest_kernel, len(told)), in_specs=specs(...]
    ppermute x23, waiting for transfers between devices: 54.3 us -> 52.7 us  [swap(): return lax.ppermute(x, axis, [(i, i ^ bits) for i in range(size)])]
    ppermute x1, starting transfers between devices: 5.19 us -> 3.81 us  [gather_pairs(): across_one = lax.ppermute(block, ('grp', 'tp'), pairs)]
  transfers between devices with their start and end apart: 24 -> 24, of which waited for: 13 -> 12; matrix products, arithmetic and copies ran while one was open for 0% -> 0% of each run, Pallas kernels for 15% -> 16%
where the time goes in v2:
time: 113 us; the launch traced here: 112 us
  waiting for transfers between devices  54.7 us (48%)
  starting transfers between devices  28.1 us (25%)
  Pallas kernels  24.1 us (21%)
  local copies, waits for them, and re-layouts  3.33 us (3%)
  between operations  2.17 us (2%)
    ppermute x23, waiting for transfers between devices, swap(): return lax.ppermute(x, axis, [(i, i ^ bits) for i in range(size)])  52.7 us
    ppermute x23, starting transfers between devices, swap(): return lax.ppermute(x, axis, [(i, i ^ bits) for i in range(size)])  24.2 us
    pallas_call x2, Pallas kernels, contract(): pl.pallas_call(functools.partial(contract_kernel, n, counts, before is no...  10.2 us
    pallas_call x2, Pallas kernels, project(): pl.pallas_call(functools.partial(project_kernel, True, bool(before), n),...  5.05 us
    pallas_call x2, Pallas kernels, project_early(): pl.pallas_call(functools.partial(project_kernel, False, False, n), grid=(...  4.14 us
    ppermute x1, starting transfers between devices, gather_pairs(): across_one = lax.ppermute(block, ('grp', 'tp'), pairs)  3.81 us
    unnamed x28, local copies, waits for them, and re-layouts  3.33 us
  transfers between devices with their start and end apart: 24, of which 12 were waited for; matrix products, arithmetic and copies ran while one was open for 0% of the time, Pallas kernels for 16%

profile of v2, /device:TPU:0, one launch (start us, length us, event | category | flops | bytes accessed | tf_op | source)
XLA Modules:
  0.0 112.4 jit_solution(5249287621719068319)
XLA Ops:
  0.6 0.5 collective-permute-start
  1.1 2.6 %collective-permute-start.3 = (bf16[128,1728]{0,1:T(8,128)(2,1)}, bf16[128,1728]{0,1:T(8,128)(2,1)S(1)}, u32[]{:S(2)}, u32[]{:S(2)}) collective-permute-start(bf16[128,1728]{0,1:T(8,128)(2,1)} %param.14), channel_id=1, source_target_pairs={{0,8},{4,12},{8,0},{12,4},{1,9},{5,13},{9,1},{13,5},{2,10},{6,14},... | collective-permute-start | bytes 1327112 | tf_op jit(solution)/shard_map/ppermute | solution.py:20
  3.7 0.2 collective-permute-start.2
  3.9 0.0 collective-permute-done
  3.9 1.8 %collective-permute-start.1 = (bf16[128,1120]{0,1:T(8,128)(2,1)}, bf16[128,1120]{0,1:T(8,128)(2,1)S(1)}, u32[]{:S(2)}, u32[]{:S(2)}) collective-permute-start(bf16[128,1120]{0,1:T(8,128)(2,1)} %param.15), channel_id=1, source_target_pairs={{0,8},{4,12},{8,0},{12,4},{1,9},{5,13},{9,1},{13,5},{2,10},{6,14},... | collective-permute-start | bytes 860168 | tf_op jit(solution)/shard_map/ppermute | solution.py:20
  5.6 2.3 %copy-done = bf16[1728,1280]{1,0:T(8,128)(2,1)S(1)} copy-done((bf16[1728,1280]{1,0:T(8,128)(2,1)S(1)}, bf16[1728,1280]{1,0:T(8,128)(2,1)}, u32[]{:S(2)}) %copy-start) | copy-done | bytes 4423704
  7.9 1.0 copy-done.2
  8.9 2.8 %project_early.2.refs_3_ = bf16[256,1280]{1,0:T(8,128)(2,1)S(1)} custom-call(bf16[1728,128]{1,0:T(8,128)(2,1)S(1)} %bitcast.19, bf16[1728,128]{1,0:T(8,128)(2,1)S(1)} %bitcast.22, bf16[1728,1280]{1,0:T(8,128)(2,1)S(1)} %copy-done), custom_call_target="tpu_custom_call" | custom-call | tf_op jit(solution)/shard_map/project_early/pallas_call | solution.py:143
  11.7 0.0 copy-start.3
  11.7 3.2 %collective-permute-done.3 = bf16[128,1728]{0,1:T(8,128)(2,1)S(1)} collective-permute-done((bf16[128,1728]{0,1:T(8,128)(2,1)}, bf16[128,1728]{0,1:T(8,128)(2,1)S(1)}, u32[]{:S(2)}, u32[]{:S(2)}) %collective-permute-start.3) | collective-permute-done | bytes 442400 | tf_op jit(solution)/shard_map/ppermute | solution.py:20
  15.0 0.0 collective-permute-start.5
  15.0 0.0 collective-permute-done.2
  15.0 1.4 %project_early.3.refs_3_ = bf16[256,384]{1,0:T(8,128)(2,1)S(1)} custom-call(bf16[1120,128]{1,0:T(8,128)(2,1)S(1)} %bitcast.44, bf16[1120,128]{1,0:T(8,128)(2,1)S(1)} %bitcast.47, bf16[1120,384]{1,0:T(8,128)(2,1)S(1)} %copy-done.4), custom_call_target="tpu_custom_call" | custom-call | tf_op jit(solution)/shard_map/project_early/pallas_call | solution.py:143
  16.4 4.5 %collective-permute-done.1 = bf16[128,1120]{0,1:T(8,128)(2,1)S(1)} collective-permute-done((bf16[128,1120]{0,1:T(8,128)(2,1)}, bf16[128,1120]{0,1:T(8,128)(2,1)S(1)}, u32[]{:S(2)}, u32[]{:S(2)}) %collective-permute-start.1) | collective-permute-done | bytes 286752 | tf_op jit(solution)/shard_map/ppermute | solution.py:20
  20.8 0.0 collective-permute-start.4
  20.8 0.0 collective-permute-done.5
  20.8 0.0 copy-start.5
  20.9 0.0 copy-start.9
  20.9 3.5 %project.2 = (bf16[128,1664]{1,0:T(8,128)(2,1)S(1)}, bf16[128,1664]{1,0:T(8,128)(2,1)S(1)}, bf16[128,1664]{1,0:T(8,128)(2,1)S(1)}, bf16[128,1664]{1,0:T(8,128)(2,1)S(1)}) custom-call(bf16[1728,128]{1,0:T(8,128)(2,1)S(1)} %bitcast.25, bf16[1728,128]{1,0:T(8,128)(2,1)S(1)} %bitcast.28, bf16[1728,1280]{1,0:T(8,128)(2,1)S(1)} %copy-done.1, ...), custom_call_target="tpu_custom_call" | custom-call | tf_op jit(solution)/shard_map/project/pallas_call | solution.py:164
  24.4 0.0 copy-start.6
  24.4 0.0 copy-start.7
  24.4 0.0 copy-start.10
  24.5 0.0 copy-start.11
  24.5 0.0 copy-start.12
  24.5 0.0 copy-start.13
  24.5 1.9 %collective-permute-start.9 = (bf16[128,1728]{0,1:T(8,128)(2,1)S(1)}, bf16[128,1728]{0,1:T(8,128)(2,1)S(1)}, u32[]{:S(2)}, u32[]{:S(2)}) collective-permute-start(bf16[128,1728]{0,1:T(8,128)(2,1)S(1)} %copy-done.3), channel_id=1, source_target_pairs={{0,16},{16,0},{1,17},{17,1},{2,18},{18,2},{3,19},{19,3},{4,20},{20... | collective-permute-start | bytes 1327112 | tf_op jit(solution)/shard_map/ppermute | solution.py:20
  26.4 1.5 %project.3 = (bf16[128,1664]{1,0:T(8,128)(2,1)S(1)}, bf16[128,1664]{1,0:T(8,128)(2,1)S(1)}, bf16[128,1664]{1,0:T(8,128)(2,1)S(1)}, bf16[128,1664]{1,0:T(8,128)(2,1)S(1)}) custom-call(bf16[1120,128]{1,0:T(8,128)(2,1)S(1)} %bitcast.45, bf16[1120,128]{1,0:T(8,128)(2,1)S(1)} %bitcast.46, ...), custom_call_target="tpu_custom_call", output_to_operand_aliasing={{0}: (4, {}), {1}: (5, {}), {2}: (6, {}), {3}: (7, {})} | custom-call | tf_op jit(solution)/shard_map/project/pallas_call | solution.py:164
  27.9 1.6 %collective-permute-start.7 = (bf16[128,1664]{1,0:T(8,128)(2,1)S(1)}, bf16[128,1664]{1,0:T(8,128)(2,1)S(1)}, u32[]{:S(2)}, u32[]{:S(2)}) collective-permute-start(bf16[128,1664]{1,0:T(8,128)(2,1)S(1)} %get-tuple-element.64), channel_id=1, source_target_pairs={{0,1},{1,0},{2,3},{3,2},{4,5},{5,4},{6,7},{7,6},{8,9},{9,8},{10,11... | collective-permute-start | bytes 1277960 | tf_op jit(solution)/shard_map/ppermute | solution.py:20
  29.5 7.7 %collective-permute-done.9 = bf16[128,1728]{0,1:T(8,128)(2,1)S(1)} collective-permute-done((bf16[128,1728]{0,1:T(8,128)(2,1)S(1)}, bf16[128,1728]{0,1:T(8,128)(2,1)S(1)}, u32[]{:S(2)}, u32[]{:S(2)}) %collective-permute-start.9) | collective-permute-done | bytes 442400 | tf_op jit(solution)/shard_map/ppermute | solution.py:20
  37.2 1.7 %collective-permute-start.10 = (bf16[128,1728]{0,1:T(8,128)(2,1)S(1)}, bf16[128,1728]{0,1:T(8,128)(2,1)S(1)}, u32[]{:S(2)}, u32[]{:S(2)}) collective-permute-start(bf16[128,1728]{0,1:T(8,128)(2,1)S(1)} %collective-permute-done.9), channel_id=1, source_target_pairs={{0,8},{4,12},{8,0},{12,4},{1,9},{5,13},{9,1},{13,5},{2,10},{6,14},... | collective-permute-start | bytes 1327112 | tf_op jit(solution)/shard_map/ppermute | solution.py:20
  38.9 1.6 %collective-permute-start.6 = (bf16[128,1664]{1,0:T(8,128)(2,1)S(1)}, bf16[128,1664]{1,0:T(8,128)(2,1)S(1)}, u32[]{:S(2)}, u32[]{:S(2)}) collective-permute-start(bf16[128,1664]{1,0:T(8,128)(2,1)S(1)} %get-tuple-element.62), channel_id=1, source_target_pairs={{0,1},{1,0},{2,3},{3,2},{4,5},{5,4},{6,7},{7,6},{8,9},{9,8},{10,11... | collective-permute-start | bytes 1277960 | tf_op jit(solution)/shard_map/ppermute | solution.py:20
  40.5 0.1 add.1
  40.6 2.7 %collective-permute-start.8 = (bf16[128,1664]{1,0:T(8,128)(2,1)S(1)}, bf16[128,1664]{1,0:T(8,128)(2,1)S(1)}, u32[]{:S(2)}, u32[]{:S(2)}) collective-permute-start(bf16[128,1664]{1,0:T(8,128)(2,1)S(1)} %add.1), channel_id=1, source_target_pairs={{0,2},{1,3},{2,0},{3,1},{4,6},{5,7},{6,4},{7,5},{8,10},{9,11},{10,... | collective-permute-start | bytes 1277960 | tf_op jit(solution)/shard_map/ppermute | solution.py:20
  44.5 1.6 %collective-permute-start.11 = (s32[1]{0:T(128)}, s32[1]{0:T(128)}, u32[]{:S(2)}, u32[]{:S(2)}) collective-permute-start(s32[1]{0:T(128)} %param.26), channel_id=1, source_target_pairs={{0,16},{16,0},{1,17},{17,1},{2,18},{18,2},{3,19},{19,3},{4,20},{20... | collective-permute-start | bytes 20 | tf_op jit(solution)/shard_map/ppermute | solution.py:20
  46.1 2.3 %collective-permute-done.11.refs_2_ = s32[1]{0:T(128)} collective-permute-done((s32[1]{0:T(128)}, s32[1]{0:T(128)}, u32[]{:S(2)}, u32[]{:S(2)}) %collective-permute-start.11) | collective-permute-done | bytes 36 | tf_op jit(solution)/shard_map/ppermute | solution.py:20
  48.4 0.6 lookup.1
  49.0 9.9 %collective-permute-done.6.refs_1_ = bf16[128,1664]{1,0:T(8,128)(2,1)S(1)} collective-permute-done((bf16[128,1664]{1,0:T(8,128)(2,1)S(1)}, bf16[128,1664]{1,0:T(8,128)(2,1)S(1)}, u32[]{:S(2)}, u32[]{:S(2)}) %collective-permute-start.6) | collective-permute-done | bytes 426016 | tf_op jit(solution)/shard_map/ppermute | solution.py:20
  58.9 0.0 collective-permute-done.10
  58.9 2.7 %collective-permute-done.8.refs_2_ = bf16[128,1664]{1,0:T(8,128)(2,1)S(1)} collective-permute-done((bf16[128,1664]{1,0:T(8,128)(2,1)S(1)}, bf16[128,1664]{1,0:T(8,128)(2,1)S(1)}, u32[]{:S(2)}, u32[]{:S(2)}) %collective-permute-start.8) | collective-permute-done | bytes 426016 | tf_op jit(solution)/shard_map/ppermute | solution.py:20
  61.6 1.4 %local_stats.1 = (f32[128,1280]{1,0:T(8,128)S(1)}, f32[128,1280]{1,0:T(8,128)S(1)}, f32[128,384]{1,0:T(8,128)S(1)}, f32[128,384]{1,0:T(8,128)S(1)}, bf16[176,128]{1,0:T(8,128)(2,1)S(1)}) custom-call(bf16[128,1664]{1,0:T(8,128)(2,1)S(1)} %get-tuple-element.73.refs_0_, bf16[128,1664]{1,0:T(8,128)(2,1)S(1)} %collective-permute-done.6.refs_1_, ...), custom_call_target="tpu_custom_call" | custom-call | tf_op jit(solution)/shard_map/local_stats/pallas_call | solution.py:334
  63.0 0.1 collective-permute-start.14
  63.1 1.2 %collective-permute-start.13 = (bf16[176,128]{1,0:T(8,128)(2,1)S(1)}, bf16[176,128]{1,0:T(8,128)(2,1)S(1)}, u32[]{:S(2)}, u32[]{:S(2)}) collective-permute-start(bf16[176,128]{1,0:T(8,128)(2,1)S(1)} %get-tuple-element.78.refs_0_), channel_id=1, source_target_pairs={{0,8},{4,12},{8,0},{12,4},{1,9},{5,13},{9,1},{13,5},{2,10},{6,14},... | collective-permute-start | bytes 135176 | tf_op jit(solution)/shard_map/ppermute | solution.py:20
  64.3 0.6 collective-permute-start.12
  64.9 1.9 %collective-permute-done.14.refs_3_ = bf16[176,128]{1,0:T(8,128)(2,1)S(1)} collective-permute-done((bf16[176,128]{1,0:T(8,128)(2,1)S(1)}, bf16[176,128]{1,0:T(8,128)(2,1)S(1)}, u32[]{:S(2)}, u32[]{:S(2)}) %collective-permute-start.14) | collective-permute-done | bytes 45088 | tf_op jit(solution)/shard_map/ppermute | solution.py:20
  66.8 0.7 collective-permute-done.13.refs_2_
  67.5 0.0 collective-permute-done.12.refs_1_
  67.5 0.8 whole_norm.1.refs_4_
  68.3 0.2 collective-permute-start.17
  68.5 1.5 %collective-permute-start.16 = (bf16[136,1280]{1,0:T(8,128)(2,1)S(1)}, bf16[136,1280]{1,0:T(8,128)(2,1)S(1)}, u32[]{:S(2)}, u32[]{:S(2)}) collective-permute-start(bf16[136,1280]{1,0:T(8,128)(2,1)S(1)} %whole_norm.1.refs_4_), channel_id=1, source_target_pairs={{0,16},{16,0},{1,17},{17,1},{2,18},{18,2},{3,19},{19,3},{4,20},{20... | collective-permute-start | bytes 1044488 | tf_op jit(solution)/shard_map/ppermute | solution.py:20
  70.0 3.8 %collective-permute-start.15 = (bf16[136,1280]{1,0:T(8,128)(2,1)S(1)}, bf16[136,1280]{1,0:T(8,128)(2,1)S(1)}, u32[]{:S(2)}, u32[]{:S(2)}) collective-permute-start(bf16[136,1280]{1,0:T(8,128)(2,1)S(1)} %whole_norm.1.refs_4_), channel_id=1, source_target_pairs={{0,17},{1,16},{2,19},{3,18},{16,1},{17,0},{18,3},{19,2},{4,21},{5,... | collective-permute-start | bytes 1044488 | tf_op jit(solution)/shard_map/ppermute | solution.py:44
  73.9 1.8 %norm_rest.1 = (bf16[128,1280]{1,0:T(8,128)(2,1)}, bf16[128,384]{1,0:T(8,128)(2,1)}, f32[64,128]{1,0:T(8,128)}) custom-call(bf16[176,128]{1,0:T(8,128)(2,1)S(1)} %get-tuple-element.78.refs_0_, bf16[176,128]{1,0:T(8,128)(2,1)S(1)} %collective-permute-done.12.refs_1_, bf16[176,128]{1,0:T(8,128)(2,1)S(1)} %collective-permute-done.13.refs_2_, ...), custom_call_target="tpu_custom_call" | custom-call | tf_op jit(solution)/shard_map/norm_rest/pallas_call | solution.py:426
  75.7 11.3 %collective-permute-done.17.refs_5_ = bf16[136,1280]{1,0:T(8,128)(2,1)S(1)} collective-permute-done((bf16[136,1280]{1,0:T(8,128)(2,1)S(1)}, bf16[136,1280]{1,0:T(8,128)(2,1)S(1)}, u32[]{:S(2)}, u32[]{:S(2)}) %collective-permute-start.17) | collective-permute-done | bytes 348192 | tf_op jit(solution)/shard_map/ppermute | solution.py:20
  87.0 0.0 collective-permute-done.16.refs_12_
  87.0 2.1 %collective-permute-done.15.refs_13_ = bf16[136,1280]{1,0:T(8,128)(2,1)S(1)} collective-permute-done((bf16[136,1280]{1,0:T(8,128)(2,1)S(1)}, bf16[136,1280]{1,0:T(8,128)(2,1)S(1)}, u32[]{:S(2)}, u32[]{:S(2)}) %collective-permute-start.15) | collective-permute-done | bytes 348192 | tf_op jit(solution)/shard_map/ppermute | solution.py:44
  89.1 1.3 %collective-permute-start.21 = (bf16[136,1280]{1,0:T(8,128)(2,1)S(1)}, bf16[136,1280]{1,0:T(8,128)(2,1)S(1)}, u32[]{:S(2)}, u32[]{:S(2)}) collective-permute-start(bf16[136,1280]{1,0:T(8,128)(2,1)S(1)} %collective-permute-done.17.refs_5_), channel_id=1, source_target_pairs={{0,1},{1,0},{2,3},{3,2},{4,5},{5,4},{6,7},{7,6},{8,9},{9,8},{10,11... | collective-permute-start | bytes 1044488 | tf_op jit(solution)/shard_map/ppermute | solution.py:20
  90.4 0.0 collective-permute-start.20
  90.4 0.5 collective-permute-start.19
  90.9 0.7 collective-permute-start.18
  91.6 6.5 %collective-permute-done.22.refs_14_ = bf16[136,1280]{1,0:T(8,128)(2,1)S(1)} collective-permute-done((bf16[136,1280]{1,0:T(8,128)(2,1)S(1)}, bf16[136,1280]{1,0:T(8,128)(2,1)S(1)}, u32[]{:S(2)}, u32[]{:S(2)}) %collective-permute-start.22) | collective-permute-done | bytes 348192 | tf_op jit(solution)/shard_map/ppermute | solution.py:20
  98.1 2.0 %collective-permute-done.21.refs_6_ = bf16[136,1280]{1,0:T(8,128)(2,1)S(1)} collective-permute-done((bf16[136,1280]{1,0:T(8,128)(2,1)S(1)}, bf16[136,1280]{1,0:T(8,128)(2,1)S(1)}, u32[]{:S(2)}, u32[]{:S(2)}) %collective-permute-start.21) | collective-permute-done | bytes 348192 | tf_op jit(solution)/shard_map/ppermute | solution.py:20
  100.1 2.0 %collective-permute-start.23 = (bf16[136,1280]{1,0:T(8,128)(2,1)S(1)}, bf16[136,1280]{1,0:T(8,128)(2,1)S(1)}, u32[]{:S(2)}, u32[]{:S(2)}) collective-permute-start(bf16[136,1280]{1,0:T(8,128)(2,1)S(1)} %collective-permute-done.21.refs_6_), channel_id=1, source_target_pairs={{0,16},{16,0},{1,17},{17,1},{2,18},{18,2},{3,19},{19,3},{4,20},{20... | collective-permute-start | bytes 1044488 | tf_op jit(solution)/shard_map/ppermute | solution.py:20
  102.2 0.0 collective-permute-done.20
  102.2 6.0 %contract.2 = (bf16[1728,1280]{1,0:T(8,128)(2,1)S(1)}, f32[64,1280]{1,0:T(8,128)S(1)}) custom-call(bf16[1728,128]{1,0:T(8,128)(2,1)S(1)} %bitcast.20, bf16[1728,128]{1,0:T(8,128)(2,1)S(1)} %bitcast.23, bf16[1728,128]{1,0:T(8,128)(2,1)S(1)} %bitcast.26, bf16[1728,128]{1,0:T(8,128)(2,1)S(1)} %bitcast.29, bf16[136,1280]{1,0:T(8,128)(2,1)S(1)} %whole_norm.1.refs_4_, ...), custom_call_target="tpu_custom_call" | custom-call | tf_op jit(solution)/shard_map/contract/pallas_call | solution.py:251
  108.2 4.2 %contract.3 = (bf16[1728,1280]{1,0:T(8,128)(2,1)}, f32[64,1280]{1,0:T(8,128)}) custom-call(bf16[1728,128]{1,0:T(8,128)(2,1)S(1)} %bitcast.21, bf16[1728,128]{1,0:T(8,128)(2,1)S(1)} %bitcast.24, bf16[1728,128]{1,0:T(8,128)(2,1)S(1)} %bitcast.27, bf16[1728,128]{1,0:T(8,128)(2,1)S(1)} %bitcast.30, bf16[136,1280]{1,0:T(8,128)(2,1)S(1)} %collective-permute-done.18.refs_4_, ...), custom_call_target="tpu_custom_call" | custom-call | tf_op jit(solution)/shard_map/contract/pallas_call | solution.py:251
  (23 shorter events, 0.0 us)
Async XLA Ops:
  0.6 3.3 %collective-permute-start = (bf16[128,1728]{0,1:T(8,128)(2,1)}, bf16[128,1728]{0,1:T(8,128)(2,1)S(1)}, u32[]{:S(2)}, u32[]{:S(2)}) collective-permute-start(bf16[128,1728]{0,1:T(8,128)(2,1)} %param.14), channel_id=1, source_target_pairs={{0,4},{4,0},{8,12},{12,8},{1,5},{5,1},{9,13},{13,9},{2,6},{6,2},{1... | collective-permute-start | bytes 1327112 | tf_op jit(solution)/shard_map/ppermute | solution.py:20
  1.1 13.8 %collective-permute-start.3 = (bf16[128,1728]{0,1:T(8,128)(2,1)}, bf16[128,1728]{0,1:T(8,128)(2,1)S(1)}, u32[]{:S(2)}, u32[]{:S(2)}) collective-permute-start(bf16[128,1728]{0,1:T(8,128)(2,1)} %param.14), channel_id=1, source_target_pairs={{0,8},{4,12},{8,0},{12,4},{1,9},{5,13},{9,1},{13,5},{2,10},{6,14},... | collective-permute-start | bytes 1327112 | tf_op jit(solution)/shard_map/ppermute | solution.py:20
  3.7 11.2 %collective-permute-start.2 = (bf16[128,1120]{0,1:T(8,128)(2,1)}, bf16[128,1120]{0,1:T(8,128)(2,1)S(1)}, u32[]{:S(2)}, u32[]{:S(2)}) collective-permute-start(bf16[128,1120]{0,1:T(8,128)(2,1)} %param.15), channel_id=1, source_target_pairs={{0,4},{4,0},{8,12},{12,8},{1,5},{5,1},{9,13},{13,9},{2,6},{6,2},{1... | collective-permute-start | bytes 860168 | tf_op jit(solution)/shard_map/ppermute | solution.py:20
  3.9 16.9 %collective-permute-start.1 = (bf16[128,1120]{0,1:T(8,128)(2,1)}, bf16[128,1120]{0,1:T(8,128)(2,1)S(1)}, u32[]{:S(2)}, u32[]{:S(2)}) collective-permute-start(bf16[128,1120]{0,1:T(8,128)(2,1)} %param.15), channel_id=1, source_target_pairs={{0,8},{4,12},{8,0},{12,4},{1,9},{5,13},{9,1},{13,5},{2,10},{6,14},... | collective-permute-start | bytes 860168 | tf_op jit(solution)/shard_map/ppermute | solution.py:20
  5.6 2.3 %copy-start = (bf16[1728,1280]{1,0:T(8,128)(2,1)S(1)}, bf16[1728,1280]{1,0:T(8,128)(2,1)}, u32[]{:S(2)}) copy-start(bf16[1728,1280]{1,0:T(8,128)(2,1)} %refs_2_.6) | copy-start | bytes 13271044
  7.9 1.0 copy-start.2
  8.9 6.1 %copy-start.4 = (bf16[1120,384]{1,0:T(8,128)(2,1)S(1)}, bf16[1120,384]{1,0:T(8,128)(2,1)}, u32[]{:S(2)}) copy-start(bf16[1120,384]{1,0:T(8,128)(2,1)} %refs_2_.7) | copy-start | bytes 2580484
  8.9 6.1 %copy-start.8 = (bf16[128,1120]{0,1:T(8,128)(2,1)S(1)}, bf16[128,1120]{0,1:T(8,128)(2,1)}, u32[]{:S(2)}) copy-start(bf16[128,1120]{0,1:T(8,128)(2,1)} %param.15) | copy-start | bytes 860164
  8.9 11.9 %copy-start.1 = (bf16[1728,1280]{1,0:T(8,128)(2,1)S(1)}, bf16[1728,1280]{1,0:T(8,128)(2,1)}, u32[]{:S(2)}) copy-start(bf16[1728,1280]{1,0:T(8,128)(2,1)} %refs_2_.6) | copy-start | bytes 13271044
  11.7 12.8 %copy-start.3 = (bf16[128,1728]{0,1:T(8,128)(2,1)S(1)}, bf16[128,1728]{0,1:T(8,128)(2,1)}, u32[]{:S(2)}) copy-start(bf16[128,1728]{0,1:T(8,128)(2,1)} %param.14) | copy-start | bytes 1327108
  15.0 5.9 %collective-permute-start.5 = (bf16[128,1728]{0,1:T(8,128)(2,1)S(1)}, bf16[128,1728]{0,1:T(8,128)(2,1)S(1)}, u32[]{:S(2)}, u32[]{:S(2)}) collective-permute-start(bf16[128,1728]{0,1:T(8,128)(2,1)S(1)} %collective-permute-done.3), channel_id=1, source_target_pairs={{0,4},{4,0},{8,12},{12,8},{1,5},{5,1},{9,13},{13,9},{2,6},{6,2},{1... | collective-permute-start | bytes 1327112 | tf_op jit(solution)/shard_map/ppermute | solution.py:20
  20.8 5.5 %collective-permute-start.4 = (bf16[128,1120]{0,1:T(8,128)(2,1)S(1)}, bf16[128,1120]{0,1:T(8,128)(2,1)S(1)}, u32[]{:S(2)}, u32[]{:S(2)}) collective-permute-start(bf16[128,1120]{0,1:T(8,128)(2,1)S(1)} %collective-permute-done.1), channel_id=1, source_target_pairs={{0,4},{4,0},{8,12},{12,8},{1,5},{5,1},{9,13},{13,9},{2,6},{6,2},{1... | collective-permute-start | bytes 860168 | tf_op jit(solution)/shard_map/ppermute | solution.py:20
  20.8 27.5 %copy-start.5 = (f32[50,3,1280]{2,0,1:T(8,128)S(1)}, f32[50,3,1280]{2,0,1:T(8,128)}, u32[]{:S(2)}) copy-start(f32[50,3,1280]{2,0,1:T(8,128)} %param.23) | copy-start | bytes 2304004
  20.9 27.5 %copy-start.9 = (f32[50,3,384]{2,0,1:T(8,128)S(1)}, f32[50,3,384]{2,0,1:T(8,128)}, u32[]{:S(2)}) copy-start(f32[50,3,384]{2,0,1:T(8,128)} %param.24) | copy-start | bytes 691204
  24.4 37.1 %copy-start.6 = (bf16[1280,64]{0,1:T(8,128)(2,1)S(1)}, bf16[1280,64]{0,1:T(8,128)(2,1)}, u32[]{:S(2)}) copy-start(bf16[1280,64]{0,1:T(8,128)(2,1)} %param.21) | copy-start | bytes 491524
  24.4 37.1 %copy-start.7 = (bf16[128,1280]{1,0:T(8,128)(2,1)S(1)}, bf16[128,1280]{1,0:T(8,128)(2,1)}, u32[]{:S(2)}) copy-start(bf16[128,1280]{1,0:T(8,128)(2,1)} %refs_3_.1) | copy-start | bytes 983044
  24.4 37.1 %copy-start.10 = (f32[128,64]{0,1:T(8,128)S(1)}, f32[128,64]{0,1:T(8,128)}, u32[]{:S(2)}) copy-start(f32[128,64]{0,1:T(8,128)} %param.18) | copy-start | bytes 98308
  24.5 37.1 %copy-start.11 = (bf16[128,384]{1,0:T(8,128)(2,1)S(1)}, bf16[128,384]{1,0:T(8,128)(2,1)}, u32[]{:S(2)}) copy-start(bf16[128,384]{1,0:T(8,128)(2,1)} %refs_6_.2) | copy-start | bytes 294916
  24.5 37.1 %copy-start.12 = (bf16[384,64]{0,1:T(8,128)(2,1)S(1)}, bf16[384,64]{0,1:T(8,128)(2,1)}, u32[]{:S(2)}) copy-start(bf16[384,64]{0,1:T(8,128)(2,1)} %param.22) | copy-start | bytes 147460
  24.5 37.1 %copy-start.13 = (f32[8]{0:T(128)S(1)}, f32[8]{0:T(128)}, u32[]{:S(2)}) copy-start(f32[8]{0:T(128)} %refs_8_.1) | copy-start | bytes 100
  24.5 12.7 %collective-permute-start.9 = (bf16[128,1728]{0,1:T(8,128)(2,1)S(1)}, bf16[128,1728]{0,1:T(8,128)(2,1)S(1)}, u32[]{:S(2)}, u32[]{:S(2)}) collective-permute-start(bf16[128,1728]{0,1:T(8,128)(2,1)S(1)} %copy-done.3), channel_id=1, source_target_pairs={{0,16},{16,0},{1,17},{17,1},{2,18},{18,2},{3,19},{19,3},{4,20},{20... | collective-permute-start | bytes 1327112 | tf_op jit(solution)/shard_map/ppermute | solution.py:20
  27.9 12.6 %collective-permute-start.7 = (bf16[128,1664]{1,0:T(8,128)(2,1)S(1)}, bf16[128,1664]{1,0:T(8,128)(2,1)S(1)}, u32[]{:S(2)}, u32[]{:S(2)}) collective-permute-start(bf16[128,1664]{1,0:T(8,128)(2,1)S(1)} %get-tuple-element.64), channel_id=1, source_target_pairs={{0,1},{1,0},{2,3},{3,2},{4,5},{5,4},{6,7},{7,6},{8,9},{9,8},{10,11... | collective-permute-start | bytes 1277960 | tf_op jit(solution)/shard_map/ppermute | solution.py:20
  37.2 21.7 %collective-permute-start.10 = (bf16[128,1728]{0,1:T(8,128)(2,1)S(1)}, bf16[128,1728]{0,1:T(8,128)(2,1)S(1)}, u32[]{:S(2)}, u32[]{:S(2)}) collective-permute-start(bf16[128,1728]{0,1:T(8,128)(2,1)S(1)} %collective-permute-done.9), channel_id=1, source_target_pairs={{0,8},{4,12},{8,0},{12,4},{1,9},{5,13},{9,1},{13,5},{2,10},{6,14},... | collective-permute-start | bytes 1327112 | tf_op jit(solution)/shard_map/ppermute | solution.py:20
  38.9 20.0 %collective-permute-start.6 = (bf16[128,1664]{1,0:T(8,128)(2,1)S(1)}, bf16[128,1664]{1,0:T(8,128)(2,1)S(1)}, u32[]{:S(2)}, u32[]{:S(2)}) collective-permute-start(bf16[128,1664]{1,0:T(8,128)(2,1)S(1)} %get-tuple-element.62), channel_id=1, source_target_pairs={{0,1},{1,0},{2,3},{3,2},{4,5},{5,4},{6,7},{7,6},{8,9},{9,8},{10,11... | collective-permute-start | bytes 1277960 | tf_op jit(solution)/shard_map/ppermute | solution.py:20
  40.6 21.0 %collective-permute-start.8 = (bf16[128,1664]{1,0:T(8,128)(2,1)S(1)}, bf16[128,1664]{1,0:T(8,128)(2,1)S(1)}, u32[]{:S(2)}, u32[]{:S(2)}) collective-permute-start(bf16[128,1664]{1,0:T(8,128)(2,1)S(1)} %add.1), channel_id=1, source_target_pairs={{0,2},{1,3},{2,0},{3,1},{4,6},{5,7},{6,4},{7,5},{8,10},{9,11},{10,... | collective-permute-start | bytes 1277960 | tf_op jit(solution)/shard_map/ppermute | solution.py:20
  44.5 3.8 %collective-permute-start.11 = (s32[1]{0:T(128)}, s32[1]{0:T(128)}, u32[]{:S(2)}, u32[]{:S(2)}) collective-permute-start(s32[1]{0:T(128)} %param.26), channel_id=1, source_target_pairs={{0,16},{16,0},{1,17},{17,1},{2,18},{18,2},{3,19},{19,3},{4,20},{20... | collective-permute-start | bytes 20 | tf_op jit(solution)/shard_map/ppermute | solution.py:20
  63.0 3.8 %collective-permute-start.14 = (bf16[176,128]{1,0:T(8,128)(2,1)S(1)}, bf16[176,128]{1,0:T(8,128)(2,1)S(1)}, u32[]{:S(2)}, u32[]{:S(2)}) collective-permute-start(bf16[176,128]{1,0:T(8,128)(2,1)S(1)} %get-tuple-element.78.refs_0_), channel_id=1, source_target_pairs={{0,12},{4,8},{8,4},{12,0},{1,13},{5,9},{9,5},{13,1},{2,14},{6,10},... | collective-permute-start | bytes 135176 | tf_op jit(solution)/shard_map/ppermute | solution.py:20
  63.1 4.4 %collective-permute-start.13 = (bf16[176,128]{1,0:T(8,128)(2,1)S(1)}, bf16[176,128]{1,0:T(8,128)(2,1)S(1)}, u32[]{:S(2)}, u32[]{:S(2)}) collective-permute-start(bf16[176,128]{1,0:T(8,128)(2,1)S(1)} %get-tuple-element.78.refs_0_), channel_id=1, source_target_pairs={{0,8},{4,12},{8,0},{12,4},{1,9},{5,13},{9,1},{13,5},{2,10},{6,14},... | collective-permute-start | bytes 135176 | tf_op jit(solution)/shard_map/ppermute | solution.py:20
  64.3 3.2 %collective-permute-start.12 = (bf16[176,128]{1,0:T(8,128)(2,1)S(1)}, bf16[176,128]{1,0:T(8,128)(2,1)S(1)}, u32[]{:S(2)}, u32[]{:S(2)}) collective-permute-start(bf16[176,128]{1,0:T(8,128)(2,1)S(1)} %get-tuple-element.78.refs_0_), channel_id=1, source_target_pairs={{0,4},{4,0},{8,12},{12,8},{1,5},{5,1},{9,13},{13,9},{2,6},{6,2},{1... | collective-permute-start | bytes 135176 | tf_op jit(solution)/shard_map/ppermute | solution.py:20
  68.3 18.7 %collective-permute-start.17 = (bf16[136,1280]{1,0:T(8,128)(2,1)S(1)}, bf16[136,1280]{1,0:T(8,128)(2,1)S(1)}, u32[]{:S(2)}, u32[]{:S(2)}) collective-permute-start(bf16[136,1280]{1,0:T(8,128)(2,1)S(1)} %whole_norm.1.refs_4_), channel_id=1, source_target_pairs={{0,2},{1,3},{2,0},{3,1},{4,6},{5,7},{6,4},{7,5},{8,10},{9,11},{10,... | collective-permute-start | bytes 1044488 | tf_op jit(solution)/shard_map/ppermute | solution.py:20
  68.5 18.5 %collective-permute-start.16 = (bf16[136,1280]{1,0:T(8,128)(2,1)S(1)}, bf16[136,1280]{1,0:T(8,128)(2,1)S(1)}, u32[]{:S(2)}, u32[]{:S(2)}) collective-permute-start(bf16[136,1280]{1,0:T(8,128)(2,1)S(1)} %whole_norm.1.refs_4_), channel_id=1, source_target_pairs={{0,16},{16,0},{1,17},{17,1},{2,18},{18,2},{3,19},{19,3},{4,20},{20... | collective-permute-start | bytes 1044488 | tf_op jit(solution)/shard_map/ppermute | solution.py:20
  70.0 19.0 %collective-permute-start.15 = (bf16[136,1280]{1,0:T(8,128)(2,1)S(1)}, bf16[136,1280]{1,0:T(8,128)(2,1)S(1)}, u32[]{:S(2)}, u32[]{:S(2)}) collective-permute-start(bf16[136,1280]{1,0:T(8,128)(2,1)S(1)} %whole_norm.1.refs_4_), channel_id=1, source_target_pairs={{0,17},{1,16},{2,19},{3,18},{16,1},{17,0},{18,3},{19,2},{4,21},{5,... | collective-permute-start | bytes 1044488 | tf_op jit(solution)/shard_map/ppermute | solution.py:44
  89.1 9.1 %collective-permute-start.22 = (bf16[136,1280]{1,0:T(8,128)(2,1)S(1)}, bf16[136,1280]{1,0:T(8,128)(2,1)S(1)}, u32[]{:S(2)}, u32[]{:S(2)}) collective-permute-start(bf16[136,1280]{1,0:T(8,128)(2,1)S(1)} %collective-permute-done.17.refs_5_), channel_id=1, source_target_pairs={{0,16},{16,0},{1,17},{17,1},{2,18},{18,2},{3,19},{19,3},{4,20},{20... | collective-permute-start | bytes 1044488 | tf_op jit(solution)/shard_map/ppermute | solution.py:20
  89.1 11.1 %collective-permute-start.21 = (bf16[136,1280]{1,0:T(8,128)(2,1)S(1)}, bf16[136,1280]{1,0:T(8,128)(2,1)S(1)}, u32[]{:S(2)}, u32[]{:S(2)}) collective-permute-start(bf16[136,1280]{1,0:T(8,128)(2,1)S(1)} %collective-permute-done.17.refs_5_), channel_id=1, source_target_pairs={{0,1},{1,0},{2,3},{3,2},{4,5},{5,4},{6,7},{7,6},{8,9},{9,8},{10,11... | collective-permute-start | bytes 1044488 | tf_op jit(solution)/shard_map/ppermute | solution.py:20
  90.4 11.8 %collective-permute-start.20 = (bf16[128,1728]{0,1:T(8,128)(2,1)S(1)}, bf16[128,1728]{0,1:T(8,128)(2,1)S(1)}, u32[]{:S(2)}, u32[]{:S(2)}) collective-permute-start(bf16[128,1728]{0,1:T(8,128)(2,1)S(1)} %collective-permute-done.10), channel_id=1, source_target_pairs={{0,4},{4,0},{8,12},{12,8},{1,5},{5,1},{9,13},{13,9},{2,6},{6,2},{1... | collective-permute-start | bytes 1327112 | tf_op jit(solution)/shard_map/ppermute | solution.py:20
  90.4 11.8 %collective-permute-start.19 = (bf16[128,1728]{0,1:T(8,128)(2,1)S(1)}, bf16[128,1728]{0,1:T(8,128)(2,1)S(1)}, u32[]{:S(2)}, u32[]{:S(2)}) collective-permute-start(bf16[128,1728]{0,1:T(8,128)(2,1)S(1)} %collective-permute-done.9), channel_id=1, source_target_pairs={{0,4},{4,0},{8,12},{12,8},{1,5},{5,1},{9,13},{13,9},{2,6},{6,2},{1... | collective-permute-start | bytes 1327112 | tf_op jit(solution)/shard_map/ppermute | solution.py:20
  90.9 17.3 %collective-permute-start.18 = (bf16[136,1280]{1,0:T(8,128)(2,1)S(1)}, bf16[136,1280]{1,0:T(8,128)(2,1)S(1)}, u32[]{:S(2)}, u32[]{:S(2)}) collective-permute-start(bf16[136,1280]{1,0:T(8,128)(2,1)S(1)} %whole_norm.1.refs_4_), channel_id=1, source_target_pairs={{0,1},{1,0},{2,3},{3,2},{4,5},{5,4},{6,7},{7,6},{8,9},{9,8},{10,11... | collective-permute-start | bytes 1044488 | tf_op jit(solution)/shard_map/ppermute | solution.py:20
  100.1 8.1 %collective-permute-start.23 = (bf16[136,1280]{1,0:T(8,128)(2,1)S(1)}, bf16[136,1280]{1,0:T(8,128)(2,1)S(1)}, u32[]{:S(2)}, u32[]{:S(2)}) collective-permute-start(bf16[136,1280]{1,0:T(8,128)(2,1)S(1)} %collective-permute-done.21.refs_6_), channel_id=1, source_target_pairs={{0,16},{16,0},{1,17},{17,1},{2,18},{18,2},{3,19},{19,3},{4,20},{20... | collective-permute-start | bytes 1044488 | tf_op jit(solution)/shard_map/ppermute | solution.py:20

commit v3 on v2

--- a/solution.py
+++ b/solution.py
@@ -42,7 +42,7 @@
     two = swap(block, "tp", 4, 2)
     across = swap(block, "grp", 2, 1)
     across_one = lax.ppermute(block, ("grp", "tp"), pairs)
-    two, meanwhile = lax.optimization_barrier((across_one, across, two, meanwhile))[2:]
+    two, meanwhile = lax.optimization_barrier((across, across_one, two, meanwhile))[2:]
     three = swap(two, "tp", 4, 1)
     across_two = swap(two, "grp", 2, 1)
     three = after(three, across_two)
@@ -109,6 +109,16 @@
     return pl.BlockSpec(x.shape, lambda i: (0,) * x.ndim)
 
 
+def in_place():
+    return pl.BlockSpec(memory_space=pltpu.VMEM)
+
+
+def weight_spec(weight, tile):
+    if weight.shape[1] % tile:
+        return pl.BlockSpec((weight.shape[0], tile), lambda i: (0, i))
+    return in_place()
+
+
 def project_kernel(last, filled, n, *refs):
     blocks, weight = refs[:n], refs[n]
     rows = blocks[0].shape[1]
@@ -119,7 +129,12 @@
         for j in range(n):
             left[j * rows : (j + 1) * rows, :] = blocks[j][...].T
 
-    product = jnp.dot(left[...], weight[...], preferred_element_type=F32).astype(BF16)
+    tile = refs[n + 1].shape[1]
+    if weight.shape[1] > tile:
+        here = pl.ds(pl.multiple_of(pl.program_id(0) * tile, tile), tile)
+        product = jnp.dot(left[...], weight[:, here], preferred_element_type=F32).astype(BF16)
+    else:
+        product = jnp.dot(left[...], weight[...], preferred_element_type=F32).astype(BF16)
     if not last:
         refs[n + 1][...] = product
         return
@@ -143,7 +158,7 @@
     return pl.pallas_call(
         functools.partial(project_kernel, False, False, n),
         grid=(pl.cdiv(columns, tile),),
-        in_specs=[whole_block(t) for t in turned] + [pl.BlockSpec((depth, tile), lambda i: (0, i))],
+        in_specs=[in_place() for _ in turned] + [weight_spec(weight, tile)],
         out_specs=pl.BlockSpec((n * rows, tile), lambda i: (0, i)),
         out_shape=jax.ShapeDtypeStruct((n * rows, columns), BF16),
         scratch_shapes=[pltpu.VMEM((n * rows, depth), BF16)],
@@ -164,8 +179,8 @@
     return pl.pallas_call(
         functools.partial(project_kernel, True, bool(before), n),
         grid=(pl.cdiv(columns, tile),),
-        in_specs=[whole_block(t) for t in turned]
-        + [pl.BlockSpec((depth, tile), lambda i: (0, i))]
+        in_specs=[in_place() for _ in turned]
+        + [weight_spec(weight, tile)]
         + [pl.BlockSpec((early.shape[0], tile), lambda i: (0, i))]
         + [anywhere] * len(before),
         out_specs=[pl.BlockSpec((rows, tile), lambda i: (0, first + i)) for _ in range(owners)],
@@ -218,15 +233,20 @@
                 place += rows
         head_out[...] = gradient
 
-    left = []
-    for g, (slots, (hidden, *_)) in enumerate(zip(counts, samples)):
+    tile = out.shape[0]
+    here = pl.ds(pl.multiple_of(pl.program_id(0) * tile, tile), tile)
+    wanted = [(hidden, k) for slots, (hidden, *_) in zip(counts, samples) for k in slots]
+    for place, (hidden, k) in enumerate(wanted):
         for j in range(n):
-            shelf[g * n + j] = hidden[j][...]
-        left += [shelf[g * n + jnp.bitwise_xor(turn, k)] for k in slots]
-    left = jnp.concatenate(left, axis=1)
+
+            @pl.when(jnp.bitwise_xor(turn, k) == j)
+            def _():
+                shelf[place] = hidden[j][here, :]
+
+    left = jnp.concatenate([shelf[place] for place in range(len(wanted))], axis=1)
     product = jnp.dot(left, signal[...], preferred_element_type=F32)
     if more:
-        product = product + before[0][...].astype(F32)
+        product = product + before[0][here, :].astype(F32)
     out[...] = product.astype(BF16)
 
 
@@ -239,7 +259,7 @@
     operands, in_specs = [], []
     for hidden, slots, sent, table in samples:
         operands += [block.T for block in hidden]
-        in_specs += [pl.BlockSpec((tile, tokens), lambda i: (i, 0)) for _ in range(n)]
+        in_specs += [in_place() for _ in range(n)]
         rest = [*(sent[k] for k in slots), table]
         operands += rest
         in_specs += [whole_block(x) for x in rest]
@@ -247,7 +267,7 @@
     in_specs.append(whole_block(head))
     if before is not None:
         operands += before
-        in_specs += [pl.BlockSpec((tile, width), lambda i: (i, 0)), whole_block(before[1])]
+        in_specs += [in_place(), whole_block(before[1])]
     return pl.pallas_call(
         functools.partial(contract_kernel, n, counts, before is not None),
         grid=(depth // tile,),
@@ -259,7 +279,7 @@
         ],
         scratch_shapes=[
             pltpu.VMEM((sum(map(len, counts)) * tokens, width), BF16),
-            pltpu.VMEM((len(samples) * n, tile, tokens), BF16),
+            pltpu.VMEM((sum(map(len, counts)), tile, tokens), BF16),
         ],
         compiler_params=pltpu.CompilerParams(vmem_limit_bytes=VMEM),
         cost_estimate=SHORT,
@@ -456,21 +476,20 @@
 ):
     n_grp, n_seq, n_tp = sizes
     width_big, width_guide = proj_big.shape[1], proj_guide.shape[1]
-    tile = 256 if width_big % 256 == 0 else 128
+    tile = next(t for t in (640, 256, 128) if width_big % t == 0)
     width_big, width_guide = proj_big.shape[1], proj_guide.shape[1]
-    tile = 256 if width_big % 256 == 0 else 128
+    tile = next(t for t in (640, 256, 128) if width_big % t == 0)
     near_big, far_big = near_far(fc_big, n_seq)
     near_guide, far_guide = near_far(fc_guide, n_seq, near_big[1])
     early_big = project_early(near_big, proj_big, tile)
     far_big = forward(far_big, n_seq, early_big)
     big_blocks = near_big + far_big
     early_guide = project_early(after(near_guide, early_big), proj_guide, 128)
-    far_guide = forward(far_guide, n_seq, (early_guide, far_big[0]))
+    fc_crossed = [swap(fc_big, "grp", n_grp, g) for g in range(1, n_grp)]
+    far_guide = forward(far_guide, n_seq, (early_guide, far_big[0], fc_crossed))
 
     width = width_big + width_guide
     terms = project(far_big, proj_big, tile, width, early_big)
-    fc_late = after(fc_big, terms)
-    fc_crossed = [swap(fc_late, "grp", n_grp, g) for g in range(1, n_grp)]
     terms = project(far_guide, proj_guide, 128, width, early_guide, terms)
     received, joined = scatter(terms, n_tp)
     begun = after((fc_crossed, modulation_big, modulation_guide), terms)

time: 113 us -> 111 us (0.982)
  starting transfers between devices: 28.1 us -> 25.8 us
  waiting for transfers between devices: 54.7 us -> 56.7 us
  Pallas kernels: 24.1 us -> 22.7 us
    ppermute x23, starting transfers between devices: 24.2 us -> 20.6 us  [swap(): return lax.ppermute(x, axis, [(i, i ^ bits) for i in range(size)])]
    ppermute x23, waiting for transfers between devices: 52.7 us -> 55.5 us  [swap(): return lax.ppermute(x, axis, [(i, i ^ bits) for i in range(size)])]
    ppermute x1, starting transfers between devices: 3.81 us -> 5.16 us  [gather_pairs(): across_one = lax.ppermute(block, ('grp', 'tp'), pairs)]
  transfers between devices with their start and end apart: 24 -> 24, of which waited for: 12 -> 13; matrix products, arithmetic and copies ran while one was open for 0% -> 0% of each run, Pallas kernels for 16% -> 14%
where the time goes in v3:
time: 111 us
  waiting for transfers between devices  56.7 us (51%)
  starting transfers between devices  25.8 us (23%)
  Pallas kernels  22.7 us (20%)
  local copies, waits for them, and re-layouts  3.33 us (3%)
  between operations  2.19 us (2%)
    ppermute x23, waiting for transfers between devices, swap(): return lax.ppermute(x, axis, [(i, i ^ bits) for i in range(size)])  55.5 us
    ppermute x23, starting transfers between devices, swap(): return lax.ppermute(x, axis, [(i, i ^ bits) for i in range(size)])  20.6 us
    pallas_call x2, Pallas kernels, contract(): pl.pallas_call(functools.partial(contract_kernel, n, counts, before is no...  10.6 us
    ppermute x1, starting transfers between devices, gather_pairs(): across_one = lax.ppermute(block, ('grp', 'tp'), pairs)  5.16 us
    pallas_call x2, Pallas kernels, project(): pl.pallas_call(functools.partial(project_kernel, True, bool(before), n),...  4.07 us
    unnamed x28, local copies, waits for them, and re-layouts  3.33 us
    pallas_call x2, Pallas kernels, project_early(): pl.pallas_call(functools.partial(project_kernel, False, False, n), grid=(...  3.32 us
  transfers between devices with their start and end apart: 24, of which 13 were waited for; matrix products, arithmetic and copies ran while one was open for 0% of the time, Pallas kernels for 14%

profile of v3, /device:TPU:0, one launch (start us, length us, event | category | flops | bytes accessed | tf_op | source)
XLA Modules:
  0.0 110.7 jit_solution(14856554284632549152)
XLA Ops:
  0.6 0.5 collective-permute-start
  1.1 2.6 %collective-permute-start.3 = (bf16[128,1728]{0,1:T(8,128)(2,1)}, bf16[128,1728]{0,1:T(8,128)(2,1)S(1)}, u32[]{:S(2)}, u32[]{:S(2)}) collective-permute-start(bf16[128,1728]{0,1:T(8,128)(2,1)} %param.14), channel_id=1, source_target_pairs={{0,8},{4,12},{8,0},{12,4},{1,9},{5,13},{9,1},{13,5},{2,10},{6,14},... | collective-permute-start | bytes 1327112 | tf_op jit(solution)/shard_map/ppermute | solution.py:20
  3.7 1.5 %collective-permute-start.4 = (bf16[128,1728]{0,1:T(8,128)(2,1)}, bf16[128,1728]{0,1:T(8,128)(2,1)S(1)}, u32[]{:S(2)}, u32[]{:S(2)}) collective-permute-start(bf16[128,1728]{0,1:T(8,128)(2,1)} %param.14), channel_id=1, source_target_pairs={{0,16},{16,0},{1,17},{17,1},{2,18},{18,2},{3,19},{19,3},{4,20},{20... | collective-permute-start | bytes 1327112 | tf_op jit(solution)/shard_map/ppermute | solution.py:20
  5.2 0.0 collective-permute-start.2
  5.2 0.0 collective-permute-done
  5.2 0.5 collective-permute-start.1
  5.8 2.3 %copy-done = bf16[1728,1280]{1,0:T(8,128)(2,1)S(1)} copy-done((bf16[1728,1280]{1,0:T(8,128)(2,1)S(1)}, bf16[1728,1280]{1,0:T(8,128)(2,1)}, u32[]{:S(2)}) %copy-start) | copy-done | bytes 4423704
  8.0 1.0 copy-done.2
  9.1 2.1 %project_early.2.refs_3_ = bf16[256,1280]{1,0:T(8,128)(2,1)S(1)} custom-call(bf16[1728,128]{1,0:T(8,128)(2,1)S(1)} %bitcast.19, bf16[1728,128]{1,0:T(8,128)(2,1)S(1)} %bitcast.22, bf16[1728,1280]{1,0:T(8,128)(2,1)S(1)} %copy-done), custom_call_target="tpu_custom_call" | custom-call | tf_op jit(solution)/shard_map/project_early/pallas_call | solution.py:158
  11.2 3.8 %collective-permute-done.3 = bf16[128,1728]{0,1:T(8,128)(2,1)S(1)} collective-permute-done((bf16[128,1728]{0,1:T(8,128)(2,1)}, bf16[128,1728]{0,1:T(8,128)(2,1)S(1)}, u32[]{:S(2)}, u32[]{:S(2)}) %collective-permute-start.3) | collective-permute-done | bytes 442400 | tf_op jit(solution)/shard_map/ppermute | solution.py:20
  15.0 0.0 collective-permute-start.6
  15.0 0.0 collective-permute-done.2
  15.0 1.2 %project_early.3.refs_3_ = bf16[256,384]{1,0:T(8,128)(2,1)S(1)} custom-call(bf16[1120,128]{1,0:T(8,128)(2,1)S(1)} %bitcast.44, bf16[1120,128]{1,0:T(8,128)(2,1)S(1)} %bitcast.47, bf16[1120,384]{1,0:T(8,128)(2,1)S(1)} %copy-done.4), custom_call_target="tpu_custom_call" | custom-call | tf_op jit(solution)/shard_map/project_early/pallas_call | solution.py:158
  16.2 0.0 collective-permute-done.4
  16.2 4.6 %collective-permute-done.1 = bf16[128,1120]{0,1:T(8,128)(2,1)S(1)} collective-permute-done((bf16[128,1120]{0,1:T(8,128)(2,1)}, bf16[128,1120]{0,1:T(8,128)(2,1)S(1)}, u32[]{:S(2)}, u32[]{:S(2)}) %collective-permute-start.1) | collective-permute-done | bytes 286752 | tf_op jit(solution)/shard_map/ppermute | solution.py:20
  20.8 0.0 copy-start.5
  20.9 0.0 copy-start.9
  20.9 2.7 %project.2 = (bf16[128,1664]{1,0:T(8,128)(2,1)S(1)}, bf16[128,1664]{1,0:T(8,128)(2,1)S(1)}, bf16[128,1664]{1,0:T(8,128)(2,1)S(1)}, bf16[128,1664]{1,0:T(8,128)(2,1)S(1)}) custom-call(bf16[1728,128]{1,0:T(8,128)(2,1)S(1)} %bitcast.25, bf16[1728,128]{1,0:T(8,128)(2,1)S(1)} %bitcast.28, bf16[1728,1280]{1,0:T(8,128)(2,1)S(1)} %copy-done.1, ...), custom_call_target="tpu_custom_call" | custom-call | tf_op jit(solution)/shard_map/project/pallas_call | solution.py:179
  23.6 0.0 copy-start.6
  23.6 0.0 copy-start.7
  23.6 0.0 copy-start.10
  23.6 0.0 copy-start.11
  23.6 0.0 copy-start.12
  23.6 0.0 copy-start.13
  23.6 0.0 collective-permute-done.5
  23.7 1.4 %project.3 = (bf16[128,1664]{1,0:T(8,128)(2,1)S(1)}, bf16[128,1664]{1,0:T(8,128)(2,1)S(1)}, bf16[128,1664]{1,0:T(8,128)(2,1)S(1)}, bf16[128,1664]{1,0:T(8,128)(2,1)S(1)}) custom-call(bf16[1120,128]{1,0:T(8,128)(2,1)S(1)} %bitcast.45, bf16[1120,128]{1,0:T(8,128)(2,1)S(1)} %bitcast.46, ...), custom_call_target="tpu_custom_call", output_to_operand_aliasing={{0}: (4, {}), {1}: (5, {}), {2}: (6, {}), {3}: (7, {})} | custom-call | tf_op jit(solution)/shard_map/project/pallas_call | solution.py:179
  25.0 0.0 copy-start.3
  25.0 1.9 %collective-permute-start.8 = (bf16[128,1664]{1,0:T(8,128)(2,1)S(1)}, bf16[128,1664]{1,0:T(8,128)(2,1)S(1)}, u32[]{:S(2)}, u32[]{:S(2)}) collective-permute-start(bf16[128,1664]{1,0:T(8,128)(2,1)S(1)} %get-tuple-element.63), channel_id=1, source_target_pairs={{0,1},{1,0},{2,3},{3,2},{4,5},{5,4},{6,7},{7,6},{8,9},{9,8},{10,11... | collective-permute-start | bytes 1277960 | tf_op jit(solution)/shard_map/ppermute | solution.py:20
  27.0 1.5 %collective-permute-start.10 = (bf16[128,1728]{0,1:T(8,128)(2,1)S(1)}, bf16[128,1728]{0,1:T(8,128)(2,1)S(1)}, u32[]{:S(2)}, u32[]{:S(2)}) collective-permute-start(bf16[128,1728]{0,1:T(8,128)(2,1)S(1)} %collective-permute-done.4), channel_id=1, source_target_pairs={{0,8},{4,12},{8,0},{12,4},{1,9},{5,13},{9,1},{13,5},{2,10},{6,14},... | collective-permute-start | bytes 1327112 | tf_op jit(solution)/shard_map/ppermute | solution.py:20
  28.5 0.4 collective-permute-start.7
  28.9 8.8 %collective-permute-done.8.right = bf16[128,1664]{1,0:T(8,128)(2,1)S(1)} collective-permute-done((bf16[128,1664]{1,0:T(8,128)(2,1)S(1)}, bf16[128,1664]{1,0:T(8,128)(2,1)S(1)}, u32[]{:S(2)}, u32[]{:S(2)}) %collective-permute-start.8) | collective-permute-done | bytes 426016 | tf_op jit(solution)/shard_map/ppermute | solution.py:20
  37.7 0.1 add.1
  37.8 2.9 %collective-permute-start.9 = (bf16[128,1664]{1,0:T(8,128)(2,1)S(1)}, bf16[128,1664]{1,0:T(8,128)(2,1)S(1)}, u32[]{:S(2)}, u32[]{:S(2)}) collective-permute-start(bf16[128,1664]{1,0:T(8,128)(2,1)S(1)} %add.1), channel_id=1, source_target_pairs={{0,2},{1,3},{2,0},{3,1},{4,6},{5,7},{6,4},{7,5},{8,10},{9,11},{10,... | collective-permute-start | bytes 1277960 | tf_op jit(solution)/shard_map/ppermute | solution.py:20
  42.1 1.6 %collective-permute-start.11 = (s32[1]{0:T(128)}, s32[1]{0:T(128)}, u32[]{:S(2)}, u32[]{:S(2)}) collective-permute-start(s32[1]{0:T(128)} %param.26), channel_id=1, source_target_pairs={{0,16},{16,0},{1,17},{17,1},{2,18},{18,2},{3,19},{19,3},{4,20},{20... | collective-permute-start | bytes 20 | tf_op jit(solution)/shard_map/ppermute | solution.py:20
  43.6 2.3 %collective-permute-done.11.refs_2_ = s32[1]{0:T(128)} collective-permute-done((s32[1]{0:T(128)}, s32[1]{0:T(128)}, u32[]{:S(2)}, u32[]{:S(2)}) %collective-permute-start.11) | collective-permute-done | bytes 36 | tf_op jit(solution)/shard_map/ppermute | solution.py:20
  45.9 0.6 lookup.1
  46.5 7.9 %collective-permute-done.7.refs_1_ = bf16[128,1664]{1,0:T(8,128)(2,1)S(1)} collective-permute-done((bf16[128,1664]{1,0:T(8,128)(2,1)S(1)}, bf16[128,1664]{1,0:T(8,128)(2,1)S(1)}, u32[]{:S(2)}, u32[]{:S(2)}) %collective-permute-start.7) | collective-permute-done | bytes 426016 | tf_op jit(solution)/shard_map/ppermute | solution.py:20
  54.4 4.8 %collective-permute-done.9.refs_2_ = bf16[128,1664]{1,0:T(8,128)(2,1)S(1)} collective-permute-done((bf16[128,1664]{1,0:T(8,128)(2,1)S(1)}, bf16[128,1664]{1,0:T(8,128)(2,1)S(1)}, u32[]{:S(2)}, u32[]{:S(2)}) %collective-permute-start.9) | collective-permute-done | bytes 426016 | tf_op jit(solution)/shard_map/ppermute | solution.py:20
  59.3 1.4 %local_stats.1 = (f32[128,1280]{1,0:T(8,128)S(1)}, f32[128,1280]{1,0:T(8,128)S(1)}, f32[128,384]{1,0:T(8,128)S(1)}, f32[128,384]{1,0:T(8,128)S(1)}, bf16[176,128]{1,0:T(8,128)(2,1)S(1)}) custom-call(bf16[128,1664]{1,0:T(8,128)(2,1)S(1)} %get-tuple-element.71.refs_0_, bf16[128,1664]{1,0:T(8,128)(2,1)S(1)} %collective-permute-done.7.refs_1_, ...), custom_call_target="tpu_custom_call" | custom-call | tf_op jit(solution)/shard_map/local_stats/pallas_call | solution.py:354
  60.7 0.1 collective-permute-start.14
  60.8 1.6 %collective-permute-start.13 = (bf16[176,128]{1,0:T(8,128)(2,1)S(1)}, bf16[176,128]{1,0:T(8,128)(2,1)S(1)}, u32[]{:S(2)}, u32[]{:S(2)}) collective-permute-start(bf16[176,128]{1,0:T(8,128)(2,1)S(1)} %get-tuple-element.76.refs_0_), channel_id=1, source_target_pairs={{0,8},{4,12},{8,0},{12,4},{1,9},{5,13},{9,1},{13,5},{2,10},{6,14},... | collective-permute-start | bytes 135176 | tf_op jit(solution)/shard_map/ppermute | solution.py:20
  62.4 0.3 collective-permute-start.12
  62.6 2.0 %collective-permute-done.14.refs_3_ = bf16[176,128]{1,0:T(8,128)(2,1)S(1)} collective-permute-done((bf16[176,128]{1,0:T(8,128)(2,1)S(1)}, bf16[176,128]{1,0:T(8,128)(2,1)S(1)}, u32[]{:S(2)}, u32[]{:S(2)}) %collective-permute-start.14) | collective-permute-done | bytes 45088 | tf_op jit(solution)/shard_map/ppermute | solution.py:20
  64.6 0.7 collective-permute-done.13.refs_2_
  65.4 0.8 whole_norm.1.refs_4_
  66.2 0.1 collective-permute-start.17
  66.2 5.2 %collective-permute-start.16 = (bf16[136,1280]{1,0:T(8,128)(2,1)S(1)}, bf16[136,1280]{1,0:T(8,128)(2,1)S(1)}, u32[]{:S(2)}, u32[]{:S(2)}) collective-permute-start(bf16[136,1280]{1,0:T(8,128)(2,1)S(1)} %whole_norm.1.refs_4_), channel_id=1, source_target_pairs={{0,17},{1,16},{2,19},{3,18},{16,1},{17,0},{18,3},{19,2},{4,21},{5,... | collective-permute-start | bytes 1044488 | tf_op jit(solution)/shard_map/ppermute | solution.py:44
  71.4 0.5 collective-permute-start.15
  71.9 1.8 %norm_rest.1 = (bf16[128,1280]{1,0:T(8,128)(2,1)}, bf16[128,384]{1,0:T(8,128)(2,1)}, f32[64,128]{1,0:T(8,128)}) custom-call(bf16[176,128]{1,0:T(8,128)(2,1)S(1)} %get-tuple-element.76.refs_0_, bf16[176,128]{1,0:T(8,128)(2,1)S(1)} %collective-permute-done.12.refs_1_, bf16[176,128]{1,0:T(8,128)(2,1)S(1)} %collective-permute-done.13.refs_2_, ...), custom_call_target="tpu_custom_call" | custom-call | tf_op jit(solution)/shard_map/norm_rest/pallas_call | solution.py:446
  73.7 11.1 %collective-permute-done.17.refs_5_ = bf16[136,1280]{1,0:T(8,128)(2,1)S(1)} collective-permute-done((bf16[136,1280]{1,0:T(8,128)(2,1)S(1)}, bf16[136,1280]{1,0:T(8,128)(2,1)S(1)}, u32[]{:S(2)}, u32[]{:S(2)}) %collective-permute-start.17) | collective-permute-done | bytes 348192 | tf_op jit(solution)/shard_map/ppermute | solution.py:20
  84.9 1.2 %collective-permute-done.16.refs_13_ = bf16[136,1280]{1,0:T(8,128)(2,1)S(1)} collective-permute-done((bf16[136,1280]{1,0:T(8,128)(2,1)S(1)}, bf16[136,1280]{1,0:T(8,128)(2,1)S(1)}, u32[]{:S(2)}, u32[]{:S(2)}) %collective-permute-start.16) | collective-permute-done | bytes 348192 | tf_op jit(solution)/shard_map/ppermute | solution.py:44
  86.0 1.0 collective-permute-done.15.refs_12_
  87.0 0.5 collective-permute-start.22
  87.5 1.8 %collective-permute-start.21 = (bf16[136,1280]{1,0:T(8,128)(2,1)S(1)}, bf16[136,1280]{1,0:T(8,128)(2,1)S(1)}, u32[]{:S(2)}, u32[]{:S(2)}) collective-permute-start(bf16[136,1280]{1,0:T(8,128)(2,1)S(1)} %collective-permute-done.17.refs_5_), channel_id=1, source_target_pairs={{0,1},{1,0},{2,3},{3,2},{4,5},{5,4},{6,7},{7,6},{8,9},{9,8},{10,11... | collective-permute-start | bytes 1044488 | tf_op jit(solution)/shard_map/ppermute | solution.py:20
  89.3 0.0 collective-permute-start.20
  89.3 0.5 collective-permute-start.19
  89.8 0.2 collective-permute-start.18
  90.1 7.0 %collective-permute-done.22.refs_14_ = bf16[136,1280]{1,0:T(8,128)(2,1)S(1)} collective-permute-done((bf16[136,1280]{1,0:T(8,128)(2,1)S(1)}, bf16[136,1280]{1,0:T(8,128)(2,1)S(1)}, u32[]{:S(2)}, u32[]{:S(2)}) %collective-permute-start.22) | collective-permute-done | bytes 348192 | tf_op jit(solution)/shard_map/ppermute | solution.py:20
  97.1 1.5 %collective-permute-done.21.refs_6_ = bf16[136,1280]{1,0:T(8,128)(2,1)S(1)} collective-permute-done((bf16[136,1280]{1,0:T(8,128)(2,1)S(1)}, bf16[136,1280]{1,0:T(8,128)(2,1)S(1)}, u32[]{:S(2)}, u32[]{:S(2)}) %collective-permute-start.21) | collective-permute-done | bytes 348192 | tf_op jit(solution)/shard_map/ppermute | solution.py:20
  98.6 1.5 %collective-permute-start.23 = (bf16[136,1280]{1,0:T(8,128)(2,1)S(1)}, bf16[136,1280]{1,0:T(8,128)(2,1)S(1)}, u32[]{:S(2)}, u32[]{:S(2)}) collective-permute-start(bf16[136,1280]{1,0:T(8,128)(2,1)S(1)} %collective-permute-done.21.refs_6_), channel_id=1, source_target_pairs={{0,16},{16,0},{1,17},{17,1},{2,18},{18,2},{3,19},{19,3},{4,20},{20... | collective-permute-start | bytes 1044488 | tf_op jit(solution)/shard_map/ppermute | solution.py:20
  100.1 0.0 collective-permute-done.20
  100.1 6.4 %contract.2 = (bf16[1728,1280]{1,0:T(8,128)(2,1)S(1)}, f32[64,1280]{1,0:T(8,128)S(1)}) custom-call(bf16[1728,128]{1,0:T(8,128)(2,1)S(1)} %bitcast.20, bf16[1728,128]{1,0:T(8,128)(2,1)S(1)} %bitcast.23, bf16[1728,128]{1,0:T(8,128)(2,1)S(1)} %bitcast.26, bf16[1728,128]{1,0:T(8,128)(2,1)S(1)} %bitcast.29, bf16[136,1280]{1,0:T(8,128)(2,1)S(1)} %whole_norm.1.refs_4_, ...), custom_call_target="tpu_custom_call" | custom-call | tf_op jit(solution)/shard_map/contract/pallas_call | solution.py:271
  106.5 0.0 collective-permute-done.23.refs_10_
  106.5 4.2 %contract.3 = (bf16[1728,1280]{1,0:T(8,128)(2,1)}, f32[64,1280]{1,0:T(8,128)}) custom-call(bf16[1728,128]{1,0:T(8,128)(2,1)S(1)} %bitcast.21, bf16[1728,128]{1,0:T(8,128)(2,1)S(1)} %bitcast.24, bf16[1728,128]{1,0:T(8,128)(2,1)S(1)} %bitcast.27, bf16[1728,128]{1,0:T(8,128)(2,1)S(1)} %bitcast.30, bf16[136,1280]{1,0:T(8,128)(2,1)S(1)} %collective-permute-done.18.refs_4_, ...), custom_call_target="tpu_custom_call" | custom-call | tf_op jit(solution)/shard_map/contract/pallas_call | solution.py:271
  (23 shorter events, 0.0 us)
Async XLA Ops:
  0.6 4.6 %collective-permute-start = (bf16[128,1728]{0,1:T(8,128)(2,1)}, bf16[128,1728]{0,1:T(8,128)(2,1)S(1)}, u32[]{:S(2)}, u32[]{:S(2)}) collective-permute-start(bf16[128,1728]{0,1:T(8,128)(2,1)} %param.14), channel_id=1, source_target_pairs={{0,4},{4,0},{8,12},{12,8},{1,5},{5,1},{9,13},{13,9},{2,6},{6,2},{1... | collective-permute-start | bytes 1327112 | tf_op jit(solution)/shard_map/ppermute | solution.py:20
  1.1 13.8 %collective-permute-start.3 = (bf16[128,1728]{0,1:T(8,128)(2,1)}, bf16[128,1728]{0,1:T(8,128)(2,1)S(1)}, u32[]{:S(2)}, u32[]{:S(2)}) collective-permute-start(bf16[128,1728]{0,1:T(8,128)(2,1)} %param.14), channel_id=1, source_target_pairs={{0,8},{4,12},{8,0},{12,4},{1,9},{5,13},{9,1},{13,5},{2,10},{6,14},... | collective-permute-start | bytes 1327112 | tf_op jit(solution)/shard_map/ppermute | solution.py:20
  3.7 12.5 %collective-permute-start.4 = (bf16[128,1728]{0,1:T(8,128)(2,1)}, bf16[128,1728]{0,1:T(8,128)(2,1)S(1)}, u32[]{:S(2)}, u32[]{:S(2)}) collective-permute-start(bf16[128,1728]{0,1:T(8,128)(2,1)} %param.14), channel_id=1, source_target_pairs={{0,16},{16,0},{1,17},{17,1},{2,18},{18,2},{3,19},{19,3},{4,20},{20... | collective-permute-start | bytes 1327112 | tf_op jit(solution)/shard_map/ppermute | solution.py:20
  5.2 9.7 %collective-permute-start.2 = (bf16[128,1120]{0,1:T(8,128)(2,1)}, bf16[128,1120]{0,1:T(8,128)(2,1)S(1)}, u32[]{:S(2)}, u32[]{:S(2)}) collective-permute-start(bf16[128,1120]{0,1:T(8,128)(2,1)} %param.15), channel_id=1, source_target_pairs={{0,4},{4,0},{8,12},{12,8},{1,5},{5,1},{9,13},{13,9},{2,6},{6,2},{1... | collective-permute-start | bytes 860168 | tf_op jit(solution)/shard_map/ppermute | solution.py:20
  5.2 15.6 %collective-permute-start.1 = (bf16[128,1120]{0,1:T(8,128)(2,1)}, bf16[128,1120]{0,1:T(8,128)(2,1)S(1)}, u32[]{:S(2)}, u32[]{:S(2)}) collective-permute-start(bf16[128,1120]{0,1:T(8,128)(2,1)} %param.15), channel_id=1, source_target_pairs={{0,8},{4,12},{8,0},{12,4},{1,9},{5,13},{9,1},{13,5},{2,10},{6,14},... | collective-permute-start | bytes 860168 | tf_op jit(solution)/shard_map/ppermute | solution.py:20
  5.8 2.3 %copy-start = (bf16[1728,1280]{1,0:T(8,128)(2,1)S(1)}, bf16[1728,1280]{1,0:T(8,128)(2,1)}, u32[]{:S(2)}) copy-start(bf16[1728,1280]{1,0:T(8,128)(2,1)} %refs_2_.6) | copy-start | bytes 13271044
  8.0 1.0 copy-start.2
  9.0 5.9 %copy-start.4 = (bf16[1120,384]{1,0:T(8,128)(2,1)S(1)}, bf16[1120,384]{1,0:T(8,128)(2,1)}, u32[]{:S(2)}) copy-start(bf16[1120,384]{1,0:T(8,128)(2,1)} %refs_2_.7) | copy-start | bytes 2580484
  9.0 5.9 %copy-start.8 = (bf16[128,1120]{0,1:T(8,128)(2,1)S(1)}, bf16[128,1120]{0,1:T(8,128)(2,1)}, u32[]{:S(2)}) copy-start(bf16[128,1120]{0,1:T(8,128)(2,1)} %param.15) | copy-start | bytes 860164
  9.1 11.8 %copy-start.1 = (bf16[1728,1280]{1,0:T(8,128)(2,1)S(1)}, bf16[1728,1280]{1,0:T(8,128)(2,1)}, u32[]{:S(2)}) copy-start(bf16[1728,1280]{1,0:T(8,128)(2,1)} %refs_2_.6) | copy-start | bytes 13271044
  15.0 5.9 %collective-permute-start.6 = (bf16[128,1728]{0,1:T(8,128)(2,1)S(1)}, bf16[128,1728]{0,1:T(8,128)(2,1)S(1)}, u32[]{:S(2)}, u32[]{:S(2)}) collective-permute-start(bf16[128,1728]{0,1:T(8,128)(2,1)S(1)} %collective-permute-done.3), channel_id=1, source_target_pairs={{0,4},{4,0},{8,12},{12,8},{1,5},{5,1},{9,13},{13,9},{2,6},{6,2},{1... | collective-permute-start | bytes 1327112 | tf_op jit(solution)/shard_map/ppermute | solution.py:20
  20.8 2.8 %collective-permute-start.5 = (bf16[128,1120]{0,1:T(8,128)(2,1)S(1)}, bf16[128,1120]{0,1:T(8,128)(2,1)S(1)}, u32[]{:S(2)}, u32[]{:S(2)}) collective-permute-start(bf16[128,1120]{0,1:T(8,128)(2,1)S(1)} %collective-permute-done.1), channel_id=1, source_target_pairs={{0,4},{4,0},{8,12},{12,8},{1,5},{5,1},{9,13},{13,9},{2,6},{6,2},{1... | collective-permute-start | bytes 860168 | tf_op jit(solution)/shard_map/ppermute | solution.py:20
  20.8 25.1 %copy-start.5 = (f32[50,3,1280]{2,0,1:T(8,128)S(1)}, f32[50,3,1280]{2,0,1:T(8,128)}, u32[]{:S(2)}) copy-start(f32[50,3,1280]{2,0,1:T(8,128)} %param.23) | copy-start | bytes 2304004
  20.9 25.0 %copy-start.9 = (f32[50,3,384]{2,0,1:T(8,128)S(1)}, f32[50,3,384]{2,0,1:T(8,128)}, u32[]{:S(2)}) copy-start(f32[50,3,384]{2,0,1:T(8,128)} %param.24) | copy-start | bytes 691204
  23.6 35.7 %copy-start.6 = (bf16[1280,64]{0,1:T(8,128)(2,1)S(1)}, bf16[1280,64]{0,1:T(8,128)(2,1)}, u32[]{:S(2)}) copy-start(bf16[1280,64]{0,1:T(8,128)(2,1)} %param.21) | copy-start | bytes 491524
  23.6 35.7 %copy-start.7 = (bf16[128,1280]{1,0:T(8,128)(2,1)S(1)}, bf16[128,1280]{1,0:T(8,128)(2,1)}, u32[]{:S(2)}) copy-start(bf16[128,1280]{1,0:T(8,128)(2,1)} %refs_3_.1) | copy-start | bytes 983044
  23.6 35.7 %copy-start.10 = (f32[128,64]{0,1:T(8,128)S(1)}, f32[128,64]{0,1:T(8,128)}, u32[]{:S(2)}) copy-start(f32[128,64]{0,1:T(8,128)} %param.18) | copy-start | bytes 98308
  23.6 35.6 %copy-start.11 = (bf16[128,384]{1,0:T(8,128)(2,1)S(1)}, bf16[128,384]{1,0:T(8,128)(2,1)}, u32[]{:S(2)}) copy-start(bf16[128,384]{1,0:T(8,128)(2,1)} %refs_6_.2) | copy-start | bytes 294916
  23.6 35.6 %copy-start.12 = (bf16[384,64]{0,1:T(8,128)(2,1)S(1)}, bf16[384,64]{0,1:T(8,128)(2,1)}, u32[]{:S(2)}) copy-start(bf16[384,64]{0,1:T(8,128)(2,1)} %param.22) | copy-start | bytes 147460
  23.6 35.6 %copy-start.13 = (f32[8]{0:T(128)S(1)}, f32[8]{0:T(128)}, u32[]{:S(2)}) copy-start(f32[8]{0:T(128)} %refs_8_.1) | copy-start | bytes 100
  25.0 75.1 %copy-start.3 = (bf16[128,1728]{0,1:T(8,128)(2,1)S(1)}, bf16[128,1728]{0,1:T(8,128)(2,1)}, u32[]{:S(2)}) copy-start(bf16[128,1728]{0,1:T(8,128)(2,1)} %param.14) | copy-start | bytes 1327108
  25.0 12.7 %collective-permute-start.8 = (bf16[128,1664]{1,0:T(8,128)(2,1)S(1)}, bf16[128,1664]{1,0:T(8,128)(2,1)S(1)}, u32[]{:S(2)}, u32[]{:S(2)}) collective-permute-start(bf16[128,1664]{1,0:T(8,128)(2,1)S(1)} %get-tuple-element.63), channel_id=1, source_target_pairs={{0,1},{1,0},{2,3},{3,2},{4,5},{5,4},{6,7},{7,6},{8,9},{9,8},{10,11... | collective-permute-start | bytes 1277960 | tf_op jit(solution)/shard_map/ppermute | solution.py:20
  27.0 27.5 %collective-permute-start.10 = (bf16[128,1728]{0,1:T(8,128)(2,1)S(1)}, bf16[128,1728]{0,1:T(8,128)(2,1)S(1)}, u32[]{:S(2)}, u32[]{:S(2)}) collective-permute-start(bf16[128,1728]{0,1:T(8,128)(2,1)S(1)} %collective-permute-done.4), channel_id=1, source_target_pairs={{0,8},{4,12},{8,0},{12,4},{1,9},{5,13},{9,1},{13,5},{2,10},{6,14},... | collective-permute-start | bytes 1327112 | tf_op jit(solution)/shard_map/ppermute | solution.py:20
  28.5 26.0 %collective-permute-start.7 = (bf16[128,1664]{1,0:T(8,128)(2,1)S(1)}, bf16[128,1664]{1,0:T(8,128)(2,1)S(1)}, u32[]{:S(2)}, u32[]{:S(2)}) collective-permute-start(bf16[128,1664]{1,0:T(8,128)(2,1)S(1)} %get-tuple-element.61), channel_id=1, source_target_pairs={{0,1},{1,0},{2,3},{3,2},{4,5},{5,4},{6,7},{7,6},{8,9},{9,8},{10,11... | collective-permute-start | bytes 1277960 | tf_op jit(solution)/shard_map/ppermute | solution.py:20
  37.8 21.4 %collective-permute-start.9 = (bf16[128,1664]{1,0:T(8,128)(2,1)S(1)}, bf16[128,1664]{1,0:T(8,128)(2,1)S(1)}, u32[]{:S(2)}, u32[]{:S(2)}) collective-permute-start(bf16[128,1664]{1,0:T(8,128)(2,1)S(1)} %add.1), channel_id=1, source_target_pairs={{0,2},{1,3},{2,0},{3,1},{4,6},{5,7},{6,4},{7,5},{8,10},{9,11},{10,... | collective-permute-start | bytes 1277960 | tf_op jit(solution)/shard_map/ppermute | solution.py:20
  42.1 3.8 %collective-permute-start.11 = (s32[1]{0:T(128)}, s32[1]{0:T(128)}, u32[]{:S(2)}, u32[]{:S(2)}) collective-permute-start(s32[1]{0:T(128)} %param.26), channel_id=1, source_target_pairs={{0,16},{16,0},{1,17},{17,1},{2,18},{18,2},{3,19},{19,3},{4,20},{20... | collective-permute-start | bytes 20 | tf_op jit(solution)/shard_map/ppermute | solution.py:20
  60.7 3.9 %collective-permute-start.14 = (bf16[176,128]{1,0:T(8,128)(2,1)S(1)}, bf16[176,128]{1,0:T(8,128)(2,1)S(1)}, u32[]{:S(2)}, u32[]{:S(2)}) collective-permute-start(bf16[176,128]{1,0:T(8,128)(2,1)S(1)} %get-tuple-element.76.refs_0_), channel_id=1, source_target_pairs={{0,12},{4,8},{8,4},{12,0},{1,13},{5,9},{9,5},{13,1},{2,14},{6,10},... | collective-permute-start | bytes 135176 | tf_op jit(solution)/shard_map/ppermute | solution.py:20
  60.8 4.6 %collective-permute-start.13 = (bf16[176,128]{1,0:T(8,128)(2,1)S(1)}, bf16[176,128]{1,0:T(8,128)(2,1)S(1)}, u32[]{:S(2)}, u32[]{:S(2)}) collective-permute-start(bf16[176,128]{1,0:T(8,128)(2,1)S(1)} %get-tuple-element.76.refs_0_), channel_id=1, source_target_pairs={{0,8},{4,12},{8,0},{12,4},{1,9},{5,13},{9,1},{13,5},{2,10},{6,14},... | collective-permute-start | bytes 135176 | tf_op jit(solution)/shard_map/ppermute | solution.py:20
  62.4 3.0 %collective-permute-start.12 = (bf16[176,128]{1,0:T(8,128)(2,1)S(1)}, bf16[176,128]{1,0:T(8,128)(2,1)S(1)}, u32[]{:S(2)}, u32[]{:S(2)}) collective-permute-start(bf16[176,128]{1,0:T(8,128)(2,1)S(1)} %get-tuple-element.76.refs_0_), channel_id=1, source_target_pairs={{0,4},{4,0},{8,12},{12,8},{1,5},{5,1},{9,13},{13,9},{2,6},{6,2},{1... | collective-permute-start | bytes 135176 | tf_op jit(solution)/shard_map/ppermute | solution.py:20
  66.2 18.7 %collective-permute-start.17 = (bf16[136,1280]{1,0:T(8,128)(2,1)S(1)}, bf16[136,1280]{1,0:T(8,128)(2,1)S(1)}, u32[]{:S(2)}, u32[]{:S(2)}) collective-permute-start(bf16[136,1280]{1,0:T(8,128)(2,1)S(1)} %whole_norm.1.refs_4_), channel_id=1, source_target_pairs={{0,2},{1,3},{2,0},{3,1},{4,6},{5,7},{6,4},{7,5},{8,10},{9,11},{10,... | collective-permute-start | bytes 1044488 | tf_op jit(solution)/shard_map/ppermute | solution.py:20
  66.2 19.8 %collective-permute-start.16 = (bf16[136,1280]{1,0:T(8,128)(2,1)S(1)}, bf16[136,1280]{1,0:T(8,128)(2,1)S(1)}, u32[]{:S(2)}, u32[]{:S(2)}) collective-permute-start(bf16[136,1280]{1,0:T(8,128)(2,1)S(1)} %whole_norm.1.refs_4_), channel_id=1, source_target_pairs={{0,17},{1,16},{2,19},{3,18},{16,1},{17,0},{18,3},{19,2},{4,21},{5,... | collective-permute-start | bytes 1044488 | tf_op jit(solution)/shard_map/ppermute | solution.py:44
  71.4 15.6 %collective-permute-start.15 = (bf16[136,1280]{1,0:T(8,128)(2,1)S(1)}, bf16[136,1280]{1,0:T(8,128)(2,1)S(1)}, u32[]{:S(2)}, u32[]{:S(2)}) collective-permute-start(bf16[136,1280]{1,0:T(8,128)(2,1)S(1)} %whole_norm.1.refs_4_), channel_id=1, source_target_pairs={{0,16},{16,0},{1,17},{17,1},{2,18},{18,2},{3,19},{19,3},{4,20},{20... | collective-permute-start | bytes 1044488 | tf_op jit(solution)/shard_map/ppermute | solution.py:20
  87.0 10.1 %collective-permute-start.22 = (bf16[136,1280]{1,0:T(8,128)(2,1)S(1)}, bf16[136,1280]{1,0:T(8,128)(2,1)S(1)}, u32[]{:S(2)}, u32[]{:S(2)}) collective-permute-start(bf16[136,1280]{1,0:T(8,128)(2,1)S(1)} %collective-permute-done.17.refs_5_), channel_id=1, source_target_pairs={{0,16},{16,0},{1,17},{17,1},{2,18},{18,2},{3,19},{19,3},{4,20},{20... | collective-permute-start | bytes 1044488 | tf_op jit(solution)/shard_map/ppermute | solution.py:20
  87.5 11.1 %collective-permute-start.21 = (bf16[136,1280]{1,0:T(8,128)(2,1)S(1)}, bf16[136,1280]{1,0:T(8,128)(2,1)S(1)}, u32[]{:S(2)}, u32[]{:S(2)}) collective-permute-start(bf16[136,1280]{1,0:T(8,128)(2,1)S(1)} %collective-permute-done.17.refs_5_), channel_id=1, source_target_pairs={{0,1},{1,0},{2,3},{3,2},{4,5},{5,4},{6,7},{7,6},{8,9},{9,8},{10,11... | collective-permute-start | bytes 1044488 | tf_op jit(solution)/shard_map/ppermute | solution.py:20
  89.3 10.8 %collective-permute-start.20 = (bf16[128,1728]{0,1:T(8,128)(2,1)S(1)}, bf16[128,1728]{0,1:T(8,128)(2,1)S(1)}, u32[]{:S(2)}, u32[]{:S(2)}) collective-permute-start(bf16[128,1728]{0,1:T(8,128)(2,1)S(1)} %collective-permute-done.10), channel_id=1, source_target_pairs={{0,4},{4,0},{8,12},{12,8},{1,5},{5,1},{9,13},{13,9},{2,6},{6,2},{1... | collective-permute-start | bytes 1327112 | tf_op jit(solution)/shard_map/ppermute | solution.py:20
  89.3 10.8 %collective-permute-start.19 = (bf16[128,1728]{0,1:T(8,128)(2,1)S(1)}, bf16[128,1728]{0,1:T(8,128)(2,1)S(1)}, u32[]{:S(2)}, u32[]{:S(2)}) collective-permute-start(bf16[128,1728]{0,1:T(8,128)(2,1)S(1)} %collective-permute-done.4), channel_id=1, source_target_pairs={{0,4},{4,0},{8,12},{12,8},{1,5},{5,1},{9,13},{13,9},{2,6},{6,2},{1... | collective-permute-start | bytes 1327112 | tf_op jit(solution)/shard_map/ppermute | solution.py:20
  89.8 16.7 %collective-permute-start.18 = (bf16[136,1280]{1,0:T(8,128)(2,1)S(1)}, bf16[136,1280]{1,0:T(8,128)(2,1)S(1)}, u32[]{:S(2)}, u32[]{:S(2)}) collective-permute-start(bf16[136,1280]{1,0:T(8,128)(2,1)S(1)} %whole_norm.1.refs_4_), channel_id=1, source_target_pairs={{0,1},{1,0},{2,3},{3,2},{4,5},{5,4},{6,7},{7,6},{8,9},{9,8},{10,11... | collective-permute-start | bytes 1044488 | tf_op jit(solution)/shard_map/ppermute | solution.py:20
  98.6 7.9 %collective-permute-start.23 = (bf16[136,1280]{1,0:T(8,128)(2,1)S(1)}, bf16[136,1280]{1,0:T(8,128)(2,1)S(1)}, u32[]{:S(2)}, u32[]{:S(2)}) collective-permute-start(bf16[136,1280]{1,0:T(8,128)(2,1)S(1)} %collective-permute-done.21.refs_6_), channel_id=1, source_target_pairs={{0,16},{16,0},{1,17},{17,1},{2,18},{18,2},{3,19},{19,3},{4,20},{20... | collective-permute-start | bytes 1044488 | tf_op jit(solution)/shard_map/ppermute | solution.py:20

commit v4 on v3

--- a/solution.py
+++ b/solution.py
@@ -47,7 +47,7 @@
     across_two = swap(two, "grp", 2, 1)
     three = after(three, across_two)
     across_three = swap(three, "grp", 2, 1)
-    one = swap(after(block, two), "tp", 4, 1)
+    one = swap(after(block, three), "tp", 4, 1)
     return [block, one, two, three], [across, across_one, across_two, across_three], meanwhile
 
 

time: 111 us -> 111 us (level)
  transfers between devices with their start and end apart: 24 -> 24, of which waited for: 13 -> 14; matrix products, arithmetic and copies ran while one was open for 0% -> 0% of each run, Pallas kernels for 14% -> 14%
where the time goes in v4:
time: 111 us; the launch traced here: 110 us
  waiting for transfers between devices  56.5 us (51%)
  starting transfers between devices  25.8 us (23%)
  Pallas kernels  22.7 us (20%)
  local copies, waits for them, and re-layouts  3.33 us (3%)
  between operations  2.17 us (2%)
    ppermute x23, waiting for transfers between devices, swap(): return lax.ppermute(x, axis, [(i, i ^ bits) for i in range(size)])  55.3 us
    ppermute x23, starting transfers between devices, swap(): return lax.ppermute(x, axis, [(i, i ^ bits) for i in range(size)])  20.6 us
    pallas_call x2, Pallas kernels, contract(): pl.pallas_call(functools.partial(contract_kernel, n, counts, before is no...  10.5 us
    ppermute x1, starting transfers between devices, gather_pairs(): across_one = lax.ppermute(block, ('grp', 'tp'), pairs)  5.16 us
    pallas_call x2, Pallas kernels, project(): pl.pallas_call(functools.partial(project_kernel, True, bool(before), n),...  4.07 us
    unnamed x28, local copies, waits for them, and re-layouts  3.33 us
    pallas_call x2, Pallas kernels, project_early(): pl.pallas_call(functools.partial(project_kernel, False, False, n), grid=(...  3.32 us
  transfers between devices with their start and end apart: 24, of which 14 were waited for; matrix products, arithmetic and copies ran while one was open for 0% of the time, Pallas kernels for 14%

profile of v4, /device:TPU:0, one launch (start us, length us, event | category | flops | bytes accessed | tf_op | source)
XLA Modules:
  0.0 110.4 jit_solution(13117499624787292557)
XLA Ops:
  0.6 0.5 collective-permute-start
  1.1 2.6 %collective-permute-start.3 = (bf16[128,1728]{0,1:T(8,128)(2,1)}, bf16[128,1728]{0,1:T(8,128)(2,1)S(1)}, u32[]{:S(2)}, u32[]{:S(2)}) collective-permute-start(bf16[128,1728]{0,1:T(8,128)(2,1)} %param.14), channel_id=1, source_target_pairs={{0,8},{4,12},{8,0},{12,4},{1,9},{5,13},{9,1},{13,5},{2,10},{6,14},... | collective-permute-start | bytes 1327112 | tf_op jit(solution)/shard_map/ppermute | solution.py:20
  3.7 1.5 %collective-permute-start.4 = (bf16[128,1728]{0,1:T(8,128)(2,1)}, bf16[128,1728]{0,1:T(8,128)(2,1)S(1)}, u32[]{:S(2)}, u32[]{:S(2)}) collective-permute-start(bf16[128,1728]{0,1:T(8,128)(2,1)} %param.14), channel_id=1, source_target_pairs={{0,16},{16,0},{1,17},{17,1},{2,18},{18,2},{3,19},{19,3},{4,20},{20... | collective-permute-start | bytes 1327112 | tf_op jit(solution)/shard_map/ppermute | solution.py:20
  5.2 0.0 collective-permute-start.2
  5.2 0.0 collective-permute-done
  5.2 0.5 collective-permute-start.1
  5.8 2.3 %copy-done = bf16[1728,1280]{1,0:T(8,128)(2,1)S(1)} copy-done((bf16[1728,1280]{1,0:T(8,128)(2,1)S(1)}, bf16[1728,1280]{1,0:T(8,128)(2,1)}, u32[]{:S(2)}) %copy-start) | copy-done | bytes 4423704
  8.0 1.0 copy-done.2
  9.1 2.1 %project_early.2.refs_3_ = bf16[256,1280]{1,0:T(8,128)(2,1)S(1)} custom-call(bf16[1728,128]{1,0:T(8,128)(2,1)S(1)} %bitcast.19, bf16[1728,128]{1,0:T(8,128)(2,1)S(1)} %bitcast.22, bf16[1728,1280]{1,0:T(8,128)(2,1)S(1)} %copy-done), custom_call_target="tpu_custom_call" | custom-call | tf_op jit(solution)/shard_map/project_early/pallas_call | solution.py:158
  11.2 3.8 %collective-permute-done.3 = bf16[128,1728]{0,1:T(8,128)(2,1)S(1)} collective-permute-done((bf16[128,1728]{0,1:T(8,128)(2,1)}, bf16[128,1728]{0,1:T(8,128)(2,1)S(1)}, u32[]{:S(2)}, u32[]{:S(2)}) %collective-permute-start.3) | collective-permute-done | bytes 442400 | tf_op jit(solution)/shard_map/ppermute | solution.py:20
  15.0 0.0 collective-permute-start.6
  15.0 0.0 collective-permute-done.2
  15.0 1.2 %project_early.3.refs_3_ = bf16[256,384]{1,0:T(8,128)(2,1)S(1)} custom-call(bf16[1120,128]{1,0:T(8,128)(2,1)S(1)} %bitcast.44, bf16[1120,128]{1,0:T(8,128)(2,1)S(1)} %bitcast.47, bf16[1120,384]{1,0:T(8,128)(2,1)S(1)} %copy-done.4), custom_call_target="tpu_custom_call" | custom-call | tf_op jit(solution)/shard_map/project_early/pallas_call | solution.py:158
  16.2 4.6 %collective-permute-done.1 = bf16[128,1120]{0,1:T(8,128)(2,1)S(1)} collective-permute-done((bf16[128,1120]{0,1:T(8,128)(2,1)}, bf16[128,1120]{0,1:T(8,128)(2,1)S(1)}, u32[]{:S(2)}, u32[]{:S(2)}) %collective-permute-start.1) | collective-permute-done | bytes 286752 | tf_op jit(solution)/shard_map/ppermute | solution.py:20
  20.8 0.0 copy-start.5
  20.9 0.0 copy-start.9
  20.9 2.7 %project.2 = (bf16[128,1664]{1,0:T(8,128)(2,1)S(1)}, bf16[128,1664]{1,0:T(8,128)(2,1)S(1)}, bf16[128,1664]{1,0:T(8,128)(2,1)S(1)}, bf16[128,1664]{1,0:T(8,128)(2,1)S(1)}) custom-call(bf16[1728,128]{1,0:T(8,128)(2,1)S(1)} %bitcast.25, bf16[1728,128]{1,0:T(8,128)(2,1)S(1)} %bitcast.28, bf16[1728,1280]{1,0:T(8,128)(2,1)S(1)} %copy-done.1, ...), custom_call_target="tpu_custom_call" | custom-call | tf_op jit(solution)/shard_map/project/pallas_call | solution.py:179
  23.6 0.0 copy-start.6
  23.6 0.0 copy-start.7
  23.6 0.0 copy-start.10
  23.6 0.0 copy-start.11
  23.6 0.0 copy-start.12
  23.6 0.0 copy-start.13
  23.6 0.0 collective-permute-done.5
  23.7 1.4 %project.3 = (bf16[128,1664]{1,0:T(8,128)(2,1)S(1)}, bf16[128,1664]{1,0:T(8,128)(2,1)S(1)}, bf16[128,1664]{1,0:T(8,128)(2,1)S(1)}, bf16[128,1664]{1,0:T(8,128)(2,1)S(1)}) custom-call(bf16[1120,128]{1,0:T(8,128)(2,1)S(1)} %bitcast.45, bf16[1120,128]{1,0:T(8,128)(2,1)S(1)} %bitcast.46, ...), custom_call_target="tpu_custom_call", output_to_operand_aliasing={{0}: (4, {}), {1}: (5, {}), {2}: (6, {}), {3}: (7, {})} | custom-call | tf_op jit(solution)/shard_map/project/pallas_call | solution.py:179
  25.0 0.0 copy-start.3
  25.0 1.9 %collective-permute-start.8 = (bf16[128,1664]{1,0:T(8,128)(2,1)S(1)}, bf16[128,1664]{1,0:T(8,128)(2,1)S(1)}, u32[]{:S(2)}, u32[]{:S(2)}) collective-permute-start(bf16[128,1664]{1,0:T(8,128)(2,1)S(1)} %get-tuple-element.63), channel_id=1, source_target_pairs={{0,1},{1,0},{2,3},{3,2},{4,5},{5,4},{6,7},{7,6},{8,9},{9,8},{10,11... | collective-permute-start | bytes 1277960 | tf_op jit(solution)/shard_map/ppermute | solution.py:20
  27.0 1.5 %collective-permute-start.10 = (bf16[128,1728]{0,1:T(8,128)(2,1)S(1)}, bf16[128,1728]{0,1:T(8,128)(2,1)S(1)}, u32[]{:S(2)}, u32[]{:S(2)}) collective-permute-start(bf16[128,1728]{0,1:T(8,128)(2,1)S(1)} %collective-permute-done.4), channel_id=1, source_target_pairs={{0,8},{4,12},{8,0},{12,4},{1,9},{5,13},{9,1},{13,5},{2,10},{6,14},... | collective-permute-start | bytes 1327112 | tf_op jit(solution)/shard_map/ppermute | solution.py:20
  28.5 0.4 collective-permute-start.7
  28.9 8.8 %collective-permute-done.8.right = bf16[128,1664]{1,0:T(8,128)(2,1)S(1)} collective-permute-done((bf16[128,1664]{1,0:T(8,128)(2,1)S(1)}, bf16[128,1664]{1,0:T(8,128)(2,1)S(1)}, u32[]{:S(2)}, u32[]{:S(2)}) %collective-permute-start.8) | collective-permute-done | bytes 426016 | tf_op jit(solution)/shard_map/ppermute | solution.py:20
  37.7 0.1 add.1
  37.8 2.9 %collective-permute-start.9 = (bf16[128,1664]{1,0:T(8,128)(2,1)S(1)}, bf16[128,1664]{1,0:T(8,128)(2,1)S(1)}, u32[]{:S(2)}, u32[]{:S(2)}) collective-permute-start(bf16[128,1664]{1,0:T(8,128)(2,1)S(1)} %add.1), channel_id=1, source_target_pairs={{0,2},{1,3},{2,0},{3,1},{4,6},{5,7},{6,4},{7,5},{8,10},{9,11},{10,... | collective-permute-start | bytes 1277960 | tf_op jit(solution)/shard_map/ppermute | solution.py:20
  42.1 1.6 %collective-permute-start.11 = (s32[1]{0:T(128)}, s32[1]{0:T(128)}, u32[]{:S(2)}, u32[]{:S(2)}) collective-permute-start(s32[1]{0:T(128)} %param.26), channel_id=1, source_target_pairs={{0,16},{16,0},{1,17},{17,1},{2,18},{18,2},{3,19},{19,3},{4,20},{20... | collective-permute-start | bytes 20 | tf_op jit(solution)/shard_map/ppermute | solution.py:20
  43.6 2.3 %collective-permute-done.11.refs_2_ = s32[1]{0:T(128)} collective-permute-done((s32[1]{0:T(128)}, s32[1]{0:T(128)}, u32[]{:S(2)}, u32[]{:S(2)}) %collective-permute-start.11) | collective-permute-done | bytes 36 | tf_op jit(solution)/shard_map/ppermute | solution.py:20
  45.9 0.6 lookup.1
  46.5 7.9 %collective-permute-done.7.refs_1_ = bf16[128,1664]{1,0:T(8,128)(2,1)S(1)} collective-permute-done((bf16[128,1664]{1,0:T(8,128)(2,1)S(1)}, bf16[128,1664]{1,0:T(8,128)(2,1)S(1)}, u32[]{:S(2)}, u32[]{:S(2)}) %collective-permute-start.7) | collective-permute-done | bytes 426016 | tf_op jit(solution)/shard_map/ppermute | solution.py:20
  54.4 0.0 collective-permute-done.10
  54.4 4.8 %collective-permute-done.9.refs_2_ = bf16[128,1664]{1,0:T(8,128)(2,1)S(1)} collective-permute-done((bf16[128,1664]{1,0:T(8,128)(2,1)S(1)}, bf16[128,1664]{1,0:T(8,128)(2,1)S(1)}, u32[]{:S(2)}, u32[]{:S(2)}) %collective-permute-start.9) | collective-permute-done | bytes 426016 | tf_op jit(solution)/shard_map/ppermute | solution.py:20
  59.3 1.4 %local_stats.1 = (f32[128,1280]{1,0:T(8,128)S(1)}, f32[128,1280]{1,0:T(8,128)S(1)}, f32[128,384]{1,0:T(8,128)S(1)}, f32[128,384]{1,0:T(8,128)S(1)}, bf16[176,128]{1,0:T(8,128)(2,1)S(1)}) custom-call(bf16[128,1664]{1,0:T(8,128)(2,1)S(1)} %get-tuple-element.71.refs_0_, bf16[128,1664]{1,0:T(8,128)(2,1)S(1)} %collective-permute-done.7.refs_1_, ...), custom_call_target="tpu_custom_call" | custom-call | tf_op jit(solution)/shard_map/local_stats/pallas_call | solution.py:354
  60.7 0.1 collective-permute-start.14
  60.8 1.6 %collective-permute-start.13 = (bf16[176,128]{1,0:T(8,128)(2,1)S(1)}, bf16[176,128]{1,0:T(8,128)(2,1)S(1)}, u32[]{:S(2)}, u32[]{:S(2)}) collective-permute-start(bf16[176,128]{1,0:T(8,128)(2,1)S(1)} %get-tuple-element.76.refs_0_), channel_id=1, source_target_pairs={{0,8},{4,12},{8,0},{12,4},{1,9},{5,13},{9,1},{13,5},{2,10},{6,14},... | collective-permute-start | bytes 135176 | tf_op jit(solution)/shard_map/ppermute | solution.py:20
  62.4 0.3 collective-permute-start.12
  62.6 2.0 %collective-permute-done.14.refs_3_ = bf16[176,128]{1,0:T(8,128)(2,1)S(1)} collective-permute-done((bf16[176,128]{1,0:T(8,128)(2,1)S(1)}, bf16[176,128]{1,0:T(8,128)(2,1)S(1)}, u32[]{:S(2)}, u32[]{:S(2)}) %collective-permute-start.14) | collective-permute-done | bytes 45088 | tf_op jit(solution)/shard_map/ppermute | solution.py:20
  64.6 0.7 collective-permute-done.13.refs_2_
  65.4 0.8 whole_norm.1.refs_4_
  66.2 0.1 collective-permute-start.17
  66.2 5.2 %collective-permute-start.16 = (bf16[136,1280]{1,0:T(8,128)(2,1)S(1)}, bf16[136,1280]{1,0:T(8,128)(2,1)S(1)}, u32[]{:S(2)}, u32[]{:S(2)}) collective-permute-start(bf16[136,1280]{1,0:T(8,128)(2,1)S(1)} %whole_norm.1.refs_4_), channel_id=1, source_target_pairs={{0,17},{1,16},{2,19},{3,18},{16,1},{17,0},{18,3},{19,2},{4,21},{5,... | collective-permute-start | bytes 1044488 | tf_op jit(solution)/shard_map/ppermute | solution.py:44
  71.4 0.5 collective-permute-start.15
  71.9 1.8 %norm_rest.1 = (bf16[128,1280]{1,0:T(8,128)(2,1)}, bf16[128,384]{1,0:T(8,128)(2,1)}, f32[64,128]{1,0:T(8,128)}) custom-call(bf16[176,128]{1,0:T(8,128)(2,1)S(1)} %get-tuple-element.76.refs_0_, bf16[176,128]{1,0:T(8,128)(2,1)S(1)} %collective-permute-done.12.refs_1_, bf16[176,128]{1,0:T(8,128)(2,1)S(1)} %collective-permute-done.13.refs_2_, ...), custom_call_target="tpu_custom_call" | custom-call | tf_op jit(solution)/shard_map/norm_rest/pallas_call | solution.py:446
  73.7 11.1 %collective-permute-done.17.refs_5_ = bf16[136,1280]{1,0:T(8,128)(2,1)S(1)} collective-permute-done((bf16[136,1280]{1,0:T(8,128)(2,1)S(1)}, bf16[136,1280]{1,0:T(8,128)(2,1)S(1)}, u32[]{:S(2)}, u32[]{:S(2)}) %collective-permute-start.17) | collective-permute-done | bytes 348192 | tf_op jit(solution)/shard_map/ppermute | solution.py:20
  84.9 1.2 %collective-permute-done.16.refs_13_ = bf16[136,1280]{1,0:T(8,128)(2,1)S(1)} collective-permute-done((bf16[136,1280]{1,0:T(8,128)(2,1)S(1)}, bf16[136,1280]{1,0:T(8,128)(2,1)S(1)}, u32[]{:S(2)}, u32[]{:S(2)}) %collective-permute-start.16) | collective-permute-done | bytes 348192 | tf_op jit(solution)/shard_map/ppermute | solution.py:44
  86.0 1.0 collective-permute-done.15.refs_12_
  87.0 0.5 collective-permute-start.19
  87.5 1.8 %collective-permute-start.18 = (bf16[136,1280]{1,0:T(8,128)(2,1)S(1)}, bf16[136,1280]{1,0:T(8,128)(2,1)S(1)}, u32[]{:S(2)}, u32[]{:S(2)}) collective-permute-start(bf16[136,1280]{1,0:T(8,128)(2,1)S(1)} %collective-permute-done.17.refs_5_), channel_id=1, source_target_pairs={{0,1},{1,0},{2,3},{3,2},{4,5},{5,4},{6,7},{7,6},{8,9},{9,8},{10,11... | collective-permute-start | bytes 1044488 | tf_op jit(solution)/shard_map/ppermute | solution.py:20
  89.3 0.0 collective-permute-start.22
  89.3 0.5 collective-permute-start.21
  89.8 7.2 %collective-permute-done.19.refs_14_ = bf16[136,1280]{1,0:T(8,128)(2,1)S(1)} collective-permute-done((bf16[136,1280]{1,0:T(8,128)(2,1)S(1)}, bf16[136,1280]{1,0:T(8,128)(2,1)S(1)}, u32[]{:S(2)}, u32[]{:S(2)}) %collective-permute-start.19) | collective-permute-done | bytes 348192 | tf_op jit(solution)/shard_map/ppermute | solution.py:20
  97.1 0.2 collective-permute-done.18.refs_6_
  97.3 0.7 collective-permute-start.20
  98.0 1.1 collective-permute-start.23
  99.1 6.4 %contract.2 = (bf16[1728,1280]{1,0:T(8,128)(2,1)S(1)}, f32[64,1280]{1,0:T(8,128)S(1)}) custom-call(bf16[1728,128]{1,0:T(8,128)(2,1)S(1)} %bitcast.20, bf16[1728,128]{1,0:T(8,128)(2,1)S(1)} %bitcast.23, bf16[1728,128]{1,0:T(8,128)(2,1)S(1)} %bitcast.26, bf16[1728,128]{1,0:T(8,128)(2,1)S(1)} %bitcast.29, bf16[136,1280]{1,0:T(8,128)(2,1)S(1)} %whole_norm.1.refs_4_, ...), custom_call_target="tpu_custom_call" | custom-call | tf_op jit(solution)/shard_map/contract/pallas_call | solution.py:271
  105.5 0.8 collective-permute-done.20.refs_4_
  106.3 0.0 collective-permute-done.23.refs_10_
  106.3 4.1 %contract.3 = (bf16[1728,1280]{1,0:T(8,128)(2,1)}, f32[64,1280]{1,0:T(8,128)}) custom-call(bf16[1728,128]{1,0:T(8,128)(2,1)S(1)} %bitcast.21, bf16[1728,128]{1,0:T(8,128)(2,1)S(1)} %bitcast.24, bf16[1728,128]{1,0:T(8,128)(2,1)S(1)} %bitcast.27, bf16[1728,128]{1,0:T(8,128)(2,1)S(1)} %bitcast.30, bf16[136,1280]{1,0:T(8,128)(2,1)S(1)} %collective-permute-done.20.refs_4_, ...), custom_call_target="tpu_custom_call" | custom-call | tf_op jit(solution)/shard_map/contract/pallas_call | solution.py:271
  (23 shorter events, 0.0 us)
Async XLA Ops:
  0.6 4.6 %collective-permute-start = (bf16[128,1728]{0,1:T(8,128)(2,1)}, bf16[128,1728]{0,1:T(8,128)(2,1)S(1)}, u32[]{:S(2)}, u32[]{:S(2)}) collective-permute-start(bf16[128,1728]{0,1:T(8,128)(2,1)} %param.14), channel_id=1, source_target_pairs={{0,4},{4,0},{8,12},{12,8},{1,5},{5,1},{9,13},{13,9},{2,6},{6,2},{1... | collective-permute-start | bytes 1327112 | tf_op jit(solution)/shard_map/ppermute | solution.py:20
  1.1 13.8 %collective-permute-start.3 = (bf16[128,1728]{0,1:T(8,128)(2,1)}, bf16[128,1728]{0,1:T(8,128)(2,1)S(1)}, u32[]{:S(2)}, u32[]{:S(2)}) collective-permute-start(bf16[128,1728]{0,1:T(8,128)(2,1)} %param.14), channel_id=1, source_target_pairs={{0,8},{4,12},{8,0},{12,4},{1,9},{5,13},{9,1},{13,5},{2,10},{6,14},... | collective-permute-start | bytes 1327112 | tf_op jit(solution)/shard_map/ppermute | solution.py:20
  3.7 12.5 %collective-permute-start.4 = (bf16[128,1728]{0,1:T(8,128)(2,1)}, bf16[128,1728]{0,1:T(8,128)(2,1)S(1)}, u32[]{:S(2)}, u32[]{:S(2)}) collective-permute-start(bf16[128,1728]{0,1:T(8,128)(2,1)} %param.14), channel_id=1, source_target_pairs={{0,16},{16,0},{1,17},{17,1},{2,18},{18,2},{3,19},{19,3},{4,20},{20... | collective-permute-start | bytes 1327112 | tf_op jit(solution)/shard_map/ppermute | solution.py:20
  5.2 9.7 %collective-permute-start.2 = (bf16[128,1120]{0,1:T(8,128)(2,1)}, bf16[128,1120]{0,1:T(8,128)(2,1)S(1)}, u32[]{:S(2)}, u32[]{:S(2)}) collective-permute-start(bf16[128,1120]{0,1:T(8,128)(2,1)} %param.15), channel_id=1, source_target_pairs={{0,4},{4,0},{8,12},{12,8},{1,5},{5,1},{9,13},{13,9},{2,6},{6,2},{1... | collective-permute-start | bytes 860168 | tf_op jit(solution)/shard_map/ppermute | solution.py:20
  5.2 15.6 %collective-permute-start.1 = (bf16[128,1120]{0,1:T(8,128)(2,1)}, bf16[128,1120]{0,1:T(8,128)(2,1)S(1)}, u32[]{:S(2)}, u32[]{:S(2)}) collective-permute-start(bf16[128,1120]{0,1:T(8,128)(2,1)} %param.15), channel_id=1, source_target_pairs={{0,8},{4,12},{8,0},{12,4},{1,9},{5,13},{9,1},{13,5},{2,10},{6,14},... | collective-permute-start | bytes 860168 | tf_op jit(solution)/shard_map/ppermute | solution.py:20
  5.8 2.3 %copy-start = (bf16[1728,1280]{1,0:T(8,128)(2,1)S(1)}, bf16[1728,1280]{1,0:T(8,128)(2,1)}, u32[]{:S(2)}) copy-start(bf16[1728,1280]{1,0:T(8,128)(2,1)} %refs_2_.6) | copy-start | bytes 13271044
  8.0 1.0 copy-start.2
  9.0 5.9 %copy-start.4 = (bf16[1120,384]{1,0:T(8,128)(2,1)S(1)}, bf16[1120,384]{1,0:T(8,128)(2,1)}, u32[]{:S(2)}) copy-start(bf16[1120,384]{1,0:T(8,128)(2,1)} %refs_2_.7) | copy-start | bytes 2580484
  9.0 5.9 %copy-start.8 = (bf16[128,1120]{0,1:T(8,128)(2,1)S(1)}, bf16[128,1120]{0,1:T(8,128)(2,1)}, u32[]{:S(2)}) copy-start(bf16[128,1120]{0,1:T(8,128)(2,1)} %param.15) | copy-start | bytes 860164
  9.1 11.8 %copy-start.1 = (bf16[1728,1280]{1,0:T(8,128)(2,1)S(1)}, bf16[1728,1280]{1,0:T(8,128)(2,1)}, u32[]{:S(2)}) copy-start(bf16[1728,1280]{1,0:T(8,128)(2,1)} %refs_2_.6) | copy-start | bytes 13271044
  15.0 5.9 %collective-permute-start.6 = (bf16[128,1728]{0,1:T(8,128)(2,1)S(1)}, bf16[128,1728]{0,1:T(8,128)(2,1)S(1)}, u32[]{:S(2)}, u32[]{:S(2)}) collective-permute-start(bf16[128,1728]{0,1:T(8,128)(2,1)S(1)} %collective-permute-done.3), channel_id=1, source_target_pairs={{0,4},{4,0},{8,12},{12,8},{1,5},{5,1},{9,13},{13,9},{2,6},{6,2},{1... | collective-permute-start | bytes 1327112 | tf_op jit(solution)/shard_map/ppermute | solution.py:20
  20.8 2.8 %collective-permute-start.5 = (bf16[128,1120]{0,1:T(8,128)(2,1)S(1)}, bf16[128,1120]{0,1:T(8,128)(2,1)S(1)}, u32[]{:S(2)}, u32[]{:S(2)}) collective-permute-start(bf16[128,1120]{0,1:T(8,128)(2,1)S(1)} %collective-permute-done.1), channel_id=1, source_target_pairs={{0,4},{4,0},{8,12},{12,8},{1,5},{5,1},{9,13},{13,9},{2,6},{6,2},{1... | collective-permute-start | bytes 860168 | tf_op jit(solution)/shard_map/ppermute | solution.py:20
  20.8 25.1 %copy-start.5 = (f32[50,3,1280]{2,0,1:T(8,128)S(1)}, f32[50,3,1280]{2,0,1:T(8,128)}, u32[]{:S(2)}) copy-start(f32[50,3,1280]{2,0,1:T(8,128)} %param.23) | copy-start | bytes 2304004
  20.9 25.0 %copy-start.9 = (f32[50,3,384]{2,0,1:T(8,128)S(1)}, f32[50,3,384]{2,0,1:T(8,128)}, u32[]{:S(2)}) copy-start(f32[50,3,384]{2,0,1:T(8,128)} %param.24) | copy-start | bytes 691204
  23.6 35.7 %copy-start.6 = (bf16[1280,64]{0,1:T(8,128)(2,1)S(1)}, bf16[1280,64]{0,1:T(8,128)(2,1)}, u32[]{:S(2)}) copy-start(bf16[1280,64]{0,1:T(8,128)(2,1)} %param.21) | copy-start | bytes 491524
  23.6 35.7 %copy-start.7 = (bf16[128,1280]{1,0:T(8,128)(2,1)S(1)}, bf16[128,1280]{1,0:T(8,128)(2,1)}, u32[]{:S(2)}) copy-start(bf16[128,1280]{1,0:T(8,128)(2,1)} %refs_3_.1) | copy-start | bytes 983044
  23.6 35.7 %copy-start.10 = (f32[128,64]{0,1:T(8,128)S(1)}, f32[128,64]{0,1:T(8,128)}, u32[]{:S(2)}) copy-start(f32[128,64]{0,1:T(8,128)} %param.18) | copy-start | bytes 98308
  23.6 35.6 %copy-start.11 = (bf16[128,384]{1,0:T(8,128)(2,1)S(1)}, bf16[128,384]{1,0:T(8,128)(2,1)}, u32[]{:S(2)}) copy-start(bf16[128,384]{1,0:T(8,128)(2,1)} %refs_6_.2) | copy-start | bytes 294916
  23.6 35.6 %copy-start.12 = (bf16[384,64]{0,1:T(8,128)(2,1)S(1)}, bf16[384,64]{0,1:T(8,128)(2,1)}, u32[]{:S(2)}) copy-start(bf16[384,64]{0,1:T(8,128)(2,1)} %param.22) | copy-start | bytes 147460
  23.6 35.6 %copy-start.13 = (f32[8]{0:T(128)S(1)}, f32[8]{0:T(128)}, u32[]{:S(2)}) copy-start(f32[8]{0:T(128)} %refs_8_.1) | copy-start | bytes 100
  25.0 74.1 %copy-start.3 = (bf16[128,1728]{0,1:T(8,128)(2,1)S(1)}, bf16[128,1728]{0,1:T(8,128)(2,1)}, u32[]{:S(2)}) copy-start(bf16[128,1728]{0,1:T(8,128)(2,1)} %param.14) | copy-start | bytes 1327108
  25.0 12.7 %collective-permute-start.8 = (bf16[128,1664]{1,0:T(8,128)(2,1)S(1)}, bf16[128,1664]{1,0:T(8,128)(2,1)S(1)}, u32[]{:S(2)}, u32[]{:S(2)}) collective-permute-start(bf16[128,1664]{1,0:T(8,128)(2,1)S(1)} %get-tuple-element.63), channel_id=1, source_target_pairs={{0,1},{1,0},{2,3},{3,2},{4,5},{5,4},{6,7},{7,6},{8,9},{9,8},{10,11... | collective-permute-start | bytes 1277960 | tf_op jit(solution)/shard_map/ppermute | solution.py:20
  27.0 27.5 %collective-permute-start.10 = (bf16[128,1728]{0,1:T(8,128)(2,1)S(1)}, bf16[128,1728]{0,1:T(8,128)(2,1)S(1)}, u32[]{:S(2)}, u32[]{:S(2)}) collective-permute-start(bf16[128,1728]{0,1:T(8,128)(2,1)S(1)} %collective-permute-done.4), channel_id=1, source_target_pairs={{0,8},{4,12},{8,0},{12,4},{1,9},{5,13},{9,1},{13,5},{2,10},{6,14},... | collective-permute-start | bytes 1327112 | tf_op jit(solution)/shard_map/ppermute | solution.py:20
  28.5 26.0 %collective-permute-start.7 = (bf16[128,1664]{1,0:T(8,128)(2,1)S(1)}, bf16[128,1664]{1,0:T(8,128)(2,1)S(1)}, u32[]{:S(2)}, u32[]{:S(2)}) collective-permute-start(bf16[128,1664]{1,0:T(8,128)(2,1)S(1)} %get-tuple-element.61), channel_id=1, source_target_pairs={{0,1},{1,0},{2,3},{3,2},{4,5},{5,4},{6,7},{7,6},{8,9},{9,8},{10,11... | collective-permute-start | bytes 1277960 | tf_op jit(solution)/shard_map/ppermute | solution.py:20
  37.8 21.4 %collective-permute-start.9 = (bf16[128,1664]{1,0:T(8,128)(2,1)S(1)}, bf16[128,1664]{1,0:T(8,128)(2,1)S(1)}, u32[]{:S(2)}, u32[]{:S(2)}) collective-permute-start(bf16[128,1664]{1,0:T(8,128)(2,1)S(1)} %add.1), channel_id=1, source_target_pairs={{0,2},{1,3},{2,0},{3,1},{4,6},{5,7},{6,4},{7,5},{8,10},{9,11},{10,... | collective-permute-start | bytes 1277960 | tf_op jit(solution)/shard_map/ppermute | solution.py:20
  42.1 3.8 %collective-permute-start.11 = (s32[1]{0:T(128)}, s32[1]{0:T(128)}, u32[]{:S(2)}, u32[]{:S(2)}) collective-permute-start(s32[1]{0:T(128)} %param.26), channel_id=1, source_target_pairs={{0,16},{16,0},{1,17},{17,1},{2,18},{18,2},{3,19},{19,3},{4,20},{20... | collective-permute-start | bytes 20 | tf_op jit(solution)/shard_map/ppermute | solution.py:20
  60.7 3.9 %collective-permute-start.14 = (bf16[176,128]{1,0:T(8,128)(2,1)S(1)}, bf16[176,128]{1,0:T(8,128)(2,1)S(1)}, u32[]{:S(2)}, u32[]{:S(2)}) collective-permute-start(bf16[176,128]{1,0:T(8,128)(2,1)S(1)} %get-tuple-element.76.refs_0_), channel_id=1, source_target_pairs={{0,12},{4,8},{8,4},{12,0},{1,13},{5,9},{9,5},{13,1},{2,14},{6,10},... | collective-permute-start | bytes 135176 | tf_op jit(solution)/shard_map/ppermute | solution.py:20
  60.8 4.6 %collective-permute-start.13 = (bf16[176,128]{1,0:T(8,128)(2,1)S(1)}, bf16[176,128]{1,0:T(8,128)(2,1)S(1)}, u32[]{:S(2)}, u32[]{:S(2)}) collective-permute-start(bf16[176,128]{1,0:T(8,128)(2,1)S(1)} %get-tuple-element.76.refs_0_), channel_id=1, source_target_pairs={{0,8},{4,12},{8,0},{12,4},{1,9},{5,13},{9,1},{13,5},{2,10},{6,14},... | collective-permute-start | bytes 135176 | tf_op jit(solution)/shard_map/ppermute | solution.py:20
  62.4 3.0 %collective-permute-start.12 = (bf16[176,128]{1,0:T(8,128)(2,1)S(1)}, bf16[176,128]{1,0:T(8,128)(2,1)S(1)}, u32[]{:S(2)}, u32[]{:S(2)}) collective-permute-start(bf16[176,128]{1,0:T(8,128)(2,1)S(1)} %get-tuple-element.76.refs_0_), channel_id=1, source_target_pairs={{0,4},{4,0},{8,12},{12,8},{1,5},{5,1},{9,13},{13,9},{2,6},{6,2},{1... | collective-permute-start | bytes 135176 | tf_op jit(solution)/shard_map/ppermute | solution.py:20
  66.2 18.7 %collective-permute-start.17 = (bf16[136,1280]{1,0:T(8,128)(2,1)S(1)}, bf16[136,1280]{1,0:T(8,128)(2,1)S(1)}, u32[]{:S(2)}, u32[]{:S(2)}) collective-permute-start(bf16[136,1280]{1,0:T(8,128)(2,1)S(1)} %whole_norm.1.refs_4_), channel_id=1, source_target_pairs={{0,2},{1,3},{2,0},{3,1},{4,6},{5,7},{6,4},{7,5},{8,10},{9,11},{10,... | collective-permute-start | bytes 1044488 | tf_op jit(solution)/shard_map/ppermute | solution.py:20
  66.2 19.8 %collective-permute-start.16 = (bf16[136,1280]{1,0:T(8,128)(2,1)S(1)}, bf16[136,1280]{1,0:T(8,128)(2,1)S(1)}, u32[]{:S(2)}, u32[]{:S(2)}) collective-permute-start(bf16[136,1280]{1,0:T(8,128)(2,1)S(1)} %whole_norm.1.refs_4_), channel_id=1, source_target_pairs={{0,17},{1,16},{2,19},{3,18},{16,1},{17,0},{18,3},{19,2},{4,21},{5,... | collective-permute-start | bytes 1044488 | tf_op jit(solution)/shard_map/ppermute | solution.py:44
  71.4 15.6 %collective-permute-start.15 = (bf16[136,1280]{1,0:T(8,128)(2,1)S(1)}, bf16[136,1280]{1,0:T(8,128)(2,1)S(1)}, u32[]{:S(2)}, u32[]{:S(2)}) collective-permute-start(bf16[136,1280]{1,0:T(8,128)(2,1)S(1)} %whole_norm.1.refs_4_), channel_id=1, source_target_pairs={{0,16},{16,0},{1,17},{17,1},{2,18},{18,2},{3,19},{19,3},{4,20},{20... | collective-permute-start | bytes 1044488 | tf_op jit(solution)/shard_map/ppermute | solution.py:20
  87.0 10.1 %collective-permute-start.19 = (bf16[136,1280]{1,0:T(8,128)(2,1)S(1)}, bf16[136,1280]{1,0:T(8,128)(2,1)S(1)}, u32[]{:S(2)}, u32[]{:S(2)}) collective-permute-start(bf16[136,1280]{1,0:T(8,128)(2,1)S(1)} %collective-permute-done.17.refs_5_), channel_id=1, source_target_pairs={{0,16},{16,0},{1,17},{17,1},{2,18},{18,2},{3,19},{19,3},{4,20},{20... | collective-permute-start | bytes 1044488 | tf_op jit(solution)/shard_map/ppermute | solution.py:20
  87.5 9.8 %collective-permute-start.18 = (bf16[136,1280]{1,0:T(8,128)(2,1)S(1)}, bf16[136,1280]{1,0:T(8,128)(2,1)S(1)}, u32[]{:S(2)}, u32[]{:S(2)}) collective-permute-start(bf16[136,1280]{1,0:T(8,128)(2,1)S(1)} %collective-permute-done.17.refs_5_), channel_id=1, source_target_pairs={{0,1},{1,0},{2,3},{3,2},{4,5},{5,4},{6,7},{7,6},{8,9},{9,8},{10,11... | collective-permute-start | bytes 1044488 | tf_op jit(solution)/shard_map/ppermute | solution.py:20
  89.3 9.8 %collective-permute-start.22 = (bf16[128,1728]{0,1:T(8,128)(2,1)S(1)}, bf16[128,1728]{0,1:T(8,128)(2,1)S(1)}, u32[]{:S(2)}, u32[]{:S(2)}) collective-permute-start(bf16[128,1728]{0,1:T(8,128)(2,1)S(1)} %collective-permute-done.10), channel_id=1, source_target_pairs={{0,4},{4,0},{8,12},{12,8},{1,5},{5,1},{9,13},{13,9},{2,6},{6,2},{1... | collective-permute-start | bytes 1327112 | tf_op jit(solution)/shard_map/ppermute | solution.py:20
  89.3 9.8 %collective-permute-start.21 = (bf16[128,1728]{0,1:T(8,128)(2,1)S(1)}, bf16[128,1728]{0,1:T(8,128)(2,1)S(1)}, u32[]{:S(2)}, u32[]{:S(2)}) collective-permute-start(bf16[128,1728]{0,1:T(8,128)(2,1)S(1)} %collective-permute-done.4), channel_id=1, source_target_pairs={{0,4},{4,0},{8,12},{12,8},{1,5},{5,1},{9,13},{13,9},{2,6},{6,2},{1... | collective-permute-start | bytes 1327112 | tf_op jit(solution)/shard_map/ppermute | solution.py:20
  97.3 9.0 %collective-permute-start.20 = (bf16[136,1280]{1,0:T(8,128)(2,1)S(1)}, bf16[136,1280]{1,0:T(8,128)(2,1)S(1)}, u32[]{:S(2)}, u32[]{:S(2)}) collective-permute-start(bf16[136,1280]{1,0:T(8,128)(2,1)S(1)} %whole_norm.1.refs_4_), channel_id=1, source_target_pairs={{0,1},{1,0},{2,3},{3,2},{4,5},{5,4},{6,7},{7,6},{8,9},{9,8},{10,11... | collective-permute-start | bytes 1044488 | tf_op jit(solution)/shard_map/ppermute | solution.py:20
  98.0 8.3 %collective-permute-start.23 = (bf16[136,1280]{1,0:T(8,128)(2,1)S(1)}, bf16[136,1280]{1,0:T(8,128)(2,1)S(1)}, u32[]{:S(2)}, u32[]{:S(2)}) collective-permute-start(bf16[136,1280]{1,0:T(8,128)(2,1)S(1)} %collective-permute-done.18.refs_6_), channel_id=1, source_target_pairs={{0,16},{16,0},{1,17},{17,1},{2,18},{18,2},{3,19},{19,3},{4,20},{20... | collective-permute-start | bytes 1044488 | tf_op jit(solution)/shard_map/ppermute | solution.py:20
